TPU v7x, 32 devices: a whole 2x2x4 slice. The times are simulated.
32 devices in a mesh: page: 4 (over x, core), strip: 8 (over z, y).
Axes of the slice: x: 2, y: 2, z: 4, core: 2. Of those that a mesh axis runs over, the one named last changes fastest.
Arguments:
- visual_in: bfloat16 [8, 48, 96, 768], P('page', 'strip'), may hold values from -6 to 6
- query_in: bfloat16 [8, 1024, 768], P('page', 'strip'), may hold values from -6 to 6
- row_valid: int32 [8, 48], P('page', 'strip'), may hold values from 0 to 1, as said below
- segment_ids: int32 [8, 1024], P('page'), may hold values from 0 to 63, never falling along the last dimension, each value on 1 to 32 neighbouring positions
- slot_valid: int32 [8, 1024], P('page', 'strip'), may hold values from 0 to 1, as said below
- col_shift: int32 [8], P('page'), may hold values from 0 to 11
- row_shifted: int32 [8], P('page'), may hold values from 0 to 1, as said below
- norm_gains: float32 [768, 4], replicated, may hold values from 0.1 to 1.9
- w_vqkv: bfloat16 [768, 2304], replicated, may hold values from -0.21875 to 0.21875
- w_vout: bfloat16 [768, 768], replicated, may hold values from -1.5 to 1.5
- w_up: bfloat16 [768, 3072], replicated, may hold values from -0.21875 to 0.21875
- w_down: bfloat16 [3072, 768], replicated, may hold values from -0.109375 to 0.109375
- w_qqkv: bfloat16 [768, 2304], replicated, may hold values from -0.3125 to 0.3125
- w_xkv: bfloat16 [768, 1536], replicated, may hold values from -0.3125 to 0.3125
- w_qout: bfloat16 [768, 768], replicated, may hold values from -3 to 3
- w_qup: bfloat16 [768, 3072], replicated, may hold values from -0.21875 to 0.21875
- w_qdown: bfloat16 [3072, 768], replicated, may hold values from -0.109375 to 0.109375
- visual_cot: bfloat16 [8, 48, 96, 768], P('page', 'strip'), may hold values from -6 to 6
- query_cot: bfloat16 [8, 1024, 768], P('page', 'strip'), may hold values from -6 to 6
Outputs:
- visual_out: bfloat16 [8, 48, 96, 768], P('page', 'strip')
- query_out: bfloat16 [8, 1024, 768], P('page', 'strip')
- visual_in_grad: float32 [8, 48, 96, 768], P('page', 'strip')
- query_in_grad: float32 [8, 1024, 768], P('page', 'strip')
- gain_grads: float32 [768, 4], P('strip', 'page')
- w_vqkv_grad: float32 [768, 2304], P('strip', 'page')
- w_vout_grad: float32 [768, 768], P('strip', 'page')
- w_up_grad: float32 [768, 3072], P('strip', 'page')
- w_down_grad: float32 [3072, 768], P('strip', 'page')
- w_qqkv_grad: float32 [768, 2304], P('strip', 'page')
- w_xkv_grad: float32 [768, 1536], P('strip', 'page')
- w_qout_grad: float32 [768, 768], P('strip', 'page')
- w_qup_grad: float32 [768, 3072], P('strip', 'page')
- w_qdown_grad: float32 [3072, 768], P('strip', 'page')
Inputs may be any that keep to these rules, and one draw needn't show every extreme that they name: `row_valid`: for each page, 1 on a leading run of patch rows and 0 after it; the run holds 24 rows or more. `slot_valid`: for each page, 1 on a leading run of slots and 0 after it; the run holds 512 slots or more. `segment_ids`: along a page's slots the ids never fall; a segment holds 1 to 32 slots. `row_shifted`: of pages 2k and 2k + 1, exactly one has 1.
All inputs are finite; a program needn't handle non-finite values.
Results may differ from a plain program's by a relative error of at most 0.0144.
Values may be sent and summed in bfloat16 or wider, within the bound.
A program may use at most 448 MiB of HBM per device.

v0:
```python
import jax
import jax.numpy as jnp
from jax import lax
from jax.sharding import PartitionSpec as P

HEADS = 12
WIN = 12


norm_eps = 1e-05
masked_score = -1000000000.0


def extended(block, sides, width):
    for axis, dim in sides:
        count = lax.axis_size(axis)
        forward = [(i, i + 1) for i in range(count - 1)]
        forward.append((count - 1, 0))
        backward = [(target, source) for source, target in forward]
        low = lax.ppermute(
            lax.slice_in_dim(block, block.shape[dim] - width, None, axis=dim), axis, forward
        )
        high = lax.ppermute(lax.slice_in_dim(block, 0, width, axis=dim), axis, backward)
        block = jnp.concatenate([low, block, high], axis=dim)
    return block


def combined_all(array, axis, combine):
    everything = jax.tree.map(lambda part: lax.all_gather(part, axis), array)
    initial = jax.tree.map(lambda part: part[0], everything)

    def lap(k, so_far):
        return combine(so_far, jax.tree.map(lambda part: part[k], everything))

    return lax.fori_loop(1, lax.axis_size(axis), lap, initial)


def norm_rows(inputs, gain_row):
    centre = jnp.mean(inputs, axis=-1, keepdims=True)
    offset = inputs - centre
    spread = jnp.mean(offset * offset, axis=-1, keepdims=True)
    return offset * lax.rsqrt(spread + norm_eps) * gain_row


def gelu_tanh(inputs):
    return jax.nn.gelu(inputs, approximate=True)


def project(inputs, weight):
    return jnp.matmul(inputs, weight, preferred_element_type=jnp.float32)


def project_back(gradient, weight):
    return lax.dot_general(
        gradient,
        weight,
        (((gradient.ndim - 1,), (1,)), ((), ())),
        preferred_element_type=jnp.float32,
    )


def outer_sum(left_rows, right_rows):
    flat_left = left_rows.reshape(-1, left_rows.shape[-1])
    flat_right = right_rows.reshape(-1, right_rows.shape[-1])
    return lax.dot_general(
        flat_left, flat_right, (((0,), (0,)), ((), ())), preferred_element_type=jnp.float32
    )


def roll_columns(inputs, amounts, direction):
    return jax.vmap(lambda single, amount: jnp.roll(single, direction * amount, axis=1))(
        inputs, amounts
    )


def to_windows(inputs):
    page_count, row_count, column_count, features = inputs.shape
    blocks = inputs.reshape(page_count, row_count, column_count // WIN, WIN, features)
    return blocks.transpose(0, 2, 1, 3, 4).reshape(
        page_count, column_count // WIN, row_count * WIN, features
    )


def from_windows(inputs, row_count):
    page_count, window_count, tokens, features = inputs.shape
    blocks = inputs.reshape(page_count, window_count, row_count, WIN, features)
    return blocks.transpose(0, 2, 1, 3, 4).reshape(
        page_count, row_count, window_count * WIN, features
    )


def split_heads(inputs):
    return inputs.reshape(inputs.shape[:-1] + (HEADS, inputs.shape[-1] // HEADS))


def merge_heads(inputs):
    return inputs.reshape(inputs.shape[:-2] + (inputs.shape[-2] * inputs.shape[-1],))


def pick_window(widened, strip_rows, upper_side):
    return jnp.where(upper_side, widened[:, strip_rows:], widened[:, : 2 * strip_rows])


def window_parts(own_query, pair_rows, amounts, model_width):
    query_win = split_heads(to_windows(roll_columns(own_query, amounts, -1)))
    pair_win = to_windows(roll_columns(pair_rows, amounts, -1))
    return (
        query_win,
        split_heads(pair_win[..., :model_width]),
        split_heads(pair_win[..., model_width:]),
    )


def window_softmax(query_win, key_win, score_scale):
    scores = (
        jnp.einsum("bnihd,bnjhd->bnhij", query_win, key_win, preferred_element_type=jnp.float32)
        * score_scale
    )
    peak = jnp.max(scores, axis=-1, keepdims=True)
    raised = jnp.exp(scores - peak)
    return raised / jnp.sum(raised, axis=-1, keepdims=True)


def query_scores(all_queries, local_keys, allowed, score_scale):
    scores = (
        jnp.einsum(
            "bihd,bjhd->bhij",
            split_heads(all_queries),
            split_heads(local_keys),
            preferred_element_type=jnp.float32,
        )
        * score_scale
    )
    return jnp.where(allowed[:, None], scores, masked_score)


def combine_stats(first, second):
    peak = jnp.maximum(first[0], second[0])
    return (peak, first[1] * jnp.exp(first[0] - peak) + second[1] * jnp.exp(second[0] - peak))


def pack_grads(gain_grads, weight_grads, strip_count, page_count):
    gain_rows = gain_grads.shape[0] // strip_count
    gain_cols = gain_grads.shape[1] // page_count
    gain_block = gain_grads.reshape(strip_count, gain_rows, page_count, gain_cols).transpose(
        0, 2, 1, 3
    )
    gain_block = gain_block.reshape(strip_count, page_count, gain_rows * gain_cols)
    gain_block = jnp.pad(gain_block, ((0, 0), (0, 0), (0, 128 - gain_rows * gain_cols)))
    pieces = [gain_block]
    for weight_grad in weight_grads:
        row_total, col_total = weight_grad.shape
        block = weight_grad.reshape(
            strip_count, row_total // strip_count, page_count, col_total // page_count
        )
        pieces.append(block.transpose(0, 2, 1, 3).reshape(strip_count, page_count, -1))
    packed = jnp.concatenate(pieces, axis=2)
    return packed.reshape(-1, 128)


def unpack_grads(summed, gain_grads, weight_grads, strip_count, page_count):
    flat = summed.reshape(-1)
    gain_rows = gain_grads.shape[0] // strip_count
    gain_cols = gain_grads.shape[1] // page_count
    results = [flat[: gain_rows * gain_cols].reshape(gain_rows, gain_cols)]
    offset = 128
    for weight_grad in weight_grads:
        row_part = weight_grad.shape[0] // strip_count
        col_part = weight_grad.shape[1] // page_count
        results.append(flat[offset : offset + row_part * col_part].reshape(row_part, col_part))
        offset = offset + row_part * col_part
    return results


def local(
    visual_in,
    query_in,
    row_valid,
    segment_ids,
    slot_valid,
    col_shift,
    row_shifted,
    norm_gains,
    w_vqkv,
    w_vout,
    w_up,
    w_down,
    w_qqkv,
    w_xkv,
    w_qout,
    w_qup,
    w_qdown,
    visual_cot,
    query_cot,
):
    page_count, strip_rows, column_count, model_width = visual_in.shape
    slot_count = query_in.shape[1]
    total_slots = segment_ids.shape[1]
    patch_count = strip_rows * column_count
    score_scale = (model_width // HEADS) ** (-0.5)
    strip_index = lax.axis_index("strip")
    is_odd = strip_index % 2 == 1
    upper_side = (is_odd == (row_shifted == 1))[:, None, None, None]
    visual = visual_in.astype(jnp.float32)
    queries = query_in.astype(jnp.float32)
    normed_one, norm_one_back = jax.vjp(norm_rows, visual, norm_gains[:, 0])
    normed_one = normed_one.astype(jnp.bfloat16)
    projected = project(normed_one, w_vqkv).astype(jnp.bfloat16)
    own_query = projected[..., :model_width]
    own_pair = projected[..., model_width:]
    widened = extended(own_pair, (("strip", 1),), strip_rows)
    window_pair = pick_window(widened, strip_rows, upper_side)
    query_win, key_win, value_win = window_parts(own_query, window_pair, col_shift, model_width)
    window_probs = window_softmax(query_win, key_win, score_scale)
    mixed_win = jnp.einsum(
        "bnhij,bnjhd->bnihd",
        window_probs.astype(jnp.bfloat16),
        value_win,
        preferred_element_type=jnp.float32,
    )
    attended = roll_columns(from_windows(merge_heads(mixed_win), strip_rows), col_shift, 1).astype(
        jnp.bfloat16
    )
    after_attention = visual + project(attended, w_vout)
    normed_two, norm_two_back = jax.vjp(norm_rows, after_attention, norm_gains[:, 1])
    normed_two = normed_two.astype(jnp.bfloat16)
    hidden_act, gelu_back = jax.vjp(gelu_tanh, project(normed_two, w_up))
    hidden = hidden_act.astype(jnp.bfloat16)
    visual_out = (after_attention + project(hidden, w_down)).astype(jnp.bfloat16)
    cross_pairs = project(normed_one, w_xkv).astype(jnp.bfloat16)
    normed_three, norm_three_back = jax.vjp(norm_rows, queries, norm_gains[:, 2])
    normed_three = normed_three.astype(jnp.bfloat16)
    query_proj = project(normed_three, w_qqkv).astype(jnp.bfloat16)
    all_queries = lax.all_gather(query_proj[..., :model_width], "strip", axis=1, tiled=True)
    local_keys = jnp.concatenate(
        [
            query_proj[..., model_width : 2 * model_width],
            cross_pairs[..., :model_width].reshape(page_count, patch_count, model_width),
        ],
        axis=1,
    )
    local_values = jnp.concatenate(
        [
            query_proj[..., 2 * model_width :],
            cross_pairs[..., model_width:].reshape(page_count, patch_count, model_width),
        ],
        axis=1,
    )
    own_segments = lax.dynamic_slice_in_dim(segment_ids, strip_index * slot_count, slot_count, 1)
    slot_allowed = (segment_ids[:, :, None] == own_segments[:, None, :]) & (
        slot_valid[:, None, :] == 1
    )
    patch_rows = jnp.repeat(row_valid == 1, column_count, axis=1)
    patch_allowed = jnp.broadcast_to(patch_rows[:, None, :], (page_count, total_slots, patch_count))
    allowed = jnp.concatenate([slot_allowed, patch_allowed], axis=2)
    scores = query_scores(all_queries, local_keys, allowed, score_scale)
    local_peak = jnp.max(scores, axis=-1)
    local_total = jnp.sum(jnp.exp(scores - local_peak[..., None]), axis=-1)
    peak_all, total_all = combined_all((local_peak, local_total), "strip", combine_stats)
    log_total = peak_all + jnp.log(total_all)
    query_probs = jnp.exp(scores - log_total[..., None])
    partial_out = jnp.einsum(
        "bhij,bjhd->bihd",
        query_probs.astype(jnp.bfloat16),
        split_heads(local_values),
        preferred_element_type=jnp.float32,
    )
    partial_out = partial_out.reshape(page_count, total_slots, model_width)
    attended_q = lax.psum_scatter(partial_out, "strip", scatter_dimension=1, tiled=True).astype(
        jnp.bfloat16
    )
    after_query = queries + project(attended_q, w_qout)
    normed_four, norm_four_back = jax.vjp(norm_rows, after_query, norm_gains[:, 3])
    normed_four = normed_four.astype(jnp.bfloat16)
    hidden_q_act, gelu_q_back = jax.vjp(gelu_tanh, project(normed_four, w_qup))
    hidden_q = hidden_q_act.astype(jnp.bfloat16)
    query_out = (after_query + project(hidden_q, w_qdown)).astype(jnp.bfloat16)
    grad_qdown = outer_sum(hidden_q, query_cot)
    grad_hidden_q = gelu_q_back(project_back(query_cot, w_qdown))[0].astype(jnp.bfloat16)
    grad_qup = outer_sum(normed_four, grad_hidden_q)
    grad_after_q_part, grad_gain_four = norm_four_back(project_back(grad_hidden_q, w_qup))
    grad_after_q = query_cot.astype(jnp.float32) + grad_after_q_part
    grad_branch_q = grad_after_q.astype(jnp.bfloat16)
    grad_qout = outer_sum(attended_q, grad_branch_q)
    grad_attended_q = project_back(grad_branch_q, w_qout).astype(jnp.bfloat16)
    grad_all_out = lax.all_gather(grad_attended_q, "strip", axis=1, tiled=True)
    scores = query_scores(all_queries, local_keys, allowed, score_scale)
    query_probs = jnp.exp(scores - log_total[..., None])
    grad_probs = jnp.einsum(
        "bihd,bjhd->bhij",
        split_heads(grad_all_out),
        split_heads(local_values),
        preferred_element_type=jnp.float32,
    )
    partial_dot = jnp.sum(query_probs * grad_probs, axis=-1)
    full_dot = lax.psum(partial_dot, "strip")
    grad_scores = (query_probs * (grad_probs - full_dot[..., None])).astype(jnp.bfloat16)
    partial_grad_q = jnp.einsum(
        "bhij,bjhd->bihd", grad_scores, split_heads(local_keys), preferred_element_type=jnp.float32
    )
    partial_grad_q = partial_grad_q.reshape(page_count, total_slots, model_width) * score_scale
    grad_keys = jnp.einsum(
        "bhij,bihd->bjhd", grad_scores, split_heads(all_queries), preferred_element_type=jnp.float32
    )
    grad_keys = merge_heads(grad_keys) * score_scale
    grad_values = merge_heads(
        jnp.einsum(
            "bhij,bihd->bjhd",
            query_probs.astype(jnp.bfloat16),
            split_heads(grad_all_out),
            preferred_element_type=jnp.float32,
        )
    )
    grad_own_q = lax.psum_scatter(partial_grad_q, "strip", scatter_dimension=1, tiled=True)
    grad_query_proj = jnp.concatenate(
        [grad_own_q, grad_keys[:, :slot_count], grad_values[:, :slot_count]], axis=-1
    ).astype(jnp.bfloat16)
    grad_qqkv = outer_sum(normed_three, grad_query_proj)
    grad_queries_part, grad_gain_three = norm_three_back(project_back(grad_query_proj, w_qqkv))
    query_in_grad = grad_after_q + grad_queries_part
    grad_cross = jnp.concatenate([grad_keys[:, slot_count:], grad_values[:, slot_count:]], axis=-1)
    grad_cross = grad_cross.reshape(page_count, strip_rows, column_count, 2 * model_width).astype(
        jnp.bfloat16
    )
    grad_xkv = outer_sum(normed_one, grad_cross)
    grad_normed_cross = project_back(grad_cross, w_xkv)
    grad_down = outer_sum(hidden, visual_cot)
    grad_hidden = gelu_back(project_back(visual_cot, w_down))[0].astype(jnp.bfloat16)
    grad_up = outer_sum(normed_two, grad_hidden)
    grad_after_part, grad_gain_two = norm_two_back(project_back(grad_hidden, w_up))
    grad_after = visual_cot.astype(jnp.float32) + grad_after_part
    grad_branch = grad_after.astype(jnp.bfloat16)
    grad_vout = outer_sum(attended, grad_branch)
    grad_attended = project_back(grad_branch, w_vout).astype(jnp.bfloat16)
    query_win, key_win, value_win = window_parts(own_query, window_pair, col_shift, model_width)
    window_probs = window_softmax(query_win, key_win, score_scale)
    grad_mixed = split_heads(to_windows(roll_columns(grad_attended, col_shift, -1)))
    grad_weights = jnp.einsum(
        "bnihd,bnjhd->bnhij", grad_mixed, value_win, preferred_element_type=jnp.float32
    )
    dot_rows = jnp.sum(window_probs * grad_weights, axis=-1, keepdims=True)
    grad_win_scores = (window_probs * (grad_weights - dot_rows)).astype(jnp.bfloat16)
    grad_query_win = (
        jnp.einsum(
            "bnhij,bnjhd->bnihd", grad_win_scores, key_win, preferred_element_type=jnp.float32
        )
        * score_scale
    )
    grad_key_win = (
        jnp.einsum(
            "bnhij,bnihd->bnjhd", grad_win_scores, query_win, preferred_element_type=jnp.float32
        )
        * score_scale
    )
    grad_value_win = jnp.einsum(
        "bnhij,bnihd->bnjhd",
        window_probs.astype(jnp.bfloat16),
        grad_mixed,
        preferred_element_type=jnp.float32,
    )
    grad_query_rows = roll_columns(
        from_windows(merge_heads(grad_query_win), strip_rows), col_shift, 1
    )
    grad_pair_win = jnp.concatenate(
        [merge_heads(grad_key_win), merge_heads(grad_value_win)], axis=-1
    )
    grad_pair = roll_columns(from_windows(grad_pair_win, 2 * strip_rows), col_shift, 1)
    own_part = jnp.where(upper_side, grad_pair[:, :strip_rows], grad_pair[:, strip_rows:])
    partner_part = jnp.where(upper_side, grad_pair[:, strip_rows:], grad_pair[:, :strip_rows])
    returned = extended(partner_part.astype(jnp.bfloat16), (("strip", 1),), strip_rows).astype(
        partner_part.dtype
    )
    received = jnp.where(upper_side, returned[:, 2 * strip_rows :], returned[:, :strip_rows])
    grad_projected = jnp.concatenate([grad_query_rows, own_part + received], axis=-1).astype(
        jnp.bfloat16
    )
    grad_vqkv = outer_sum(normed_one, grad_projected)
    grad_normed_one = project_back(grad_projected, w_vqkv) + grad_normed_cross
    grad_visual_part, grad_gain_one = norm_one_back(grad_normed_one)
    visual_in_grad = grad_after + grad_visual_part
    gain_grads = jnp.stack([grad_gain_one, grad_gain_two, grad_gain_three, grad_gain_four], axis=1)
    weight_grads = [
        grad_vqkv,
        grad_vout,
        grad_up,
        grad_down,
        grad_qqkv,
        grad_xkv,
        grad_qout,
        grad_qup,
        grad_qdown,
    ]
    strip_count = lax.axis_size("strip")
    page_size = lax.axis_size("page")
    packed = pack_grads(gain_grads, weight_grads, strip_count, page_size)
    sectioned = lax.psum_scatter(packed, "strip", scatter_dimension=0, tiled=True)
    summed = lax.psum_scatter(
        sectioned.astype(jnp.bfloat16), "page", scatter_dimension=0, tiled=True
    ).astype(jnp.float32)
    parts = unpack_grads(summed, gain_grads, weight_grads, strip_count, page_size)
    return (
        visual_out,
        query_out,
        visual_in_grad,
        query_in_grad,
        parts[0],
        parts[1],
        parts[2],
        parts[3],
        parts[4],
        parts[5],
        parts[6],
        parts[7],
        parts[8],
        parts[9],
    )


def solution(mesh):
    placed = (
        P("page", "strip", None, None),
        P("page", "strip", None),
        P("page", "strip"),
        P("page", None),
        P("page", "strip"),
        P("page"),
        P("page"),
        P(),
        P(),
        P(),
        P(),
        P(),
        P(),
        P(),
        P(),
        P(),
        P(),
        P("page", "strip", None, None),
        P("page", "strip", None),
    )
    return jax.shard_map(
        local,
        mesh=mesh,
        in_specs=placed,
        out_specs=(
            P("page", "strip", None, None),
            P("page", "strip", None),
            P("page", "strip", None, None),
            P("page", "strip", None),
            P("strip", "page"),
            P("strip", "page"),
            P("strip", "page"),
            P("strip", "page"),
            P("strip", "page"),
            P("strip", "page"),
            P("strip", "page"),
            P("strip", "page"),
            P("strip", "page"),
            P("strip", "page"),
        ),
        check_vma=False,
    )
```

profile of v0, /device:TPU:0, one launch (start us, length us, event | category | flops | bytes accessed | tf_op | source)
XLA Modules:
  0.0 2883.3 jit_solution(14969002438448723712)
XLA Ops:
  115.5 81.2 %collective-permute-done = bf16[2,6,96,1536]{3,2,1,0:T(8,128)(2,1)} collective-permute-done((bf16[2,6,96,1536]{3,2,1,0:T(8,128)(2,1)}, bf16[2,6,96,1536]{3,2,1,0:T(8,128)(2,1)}, u32[]{:S(2)}, u32[]{:S(2)}) %collective-permute-start) | collective-permute-done | bytes 3538976 | tf_op jit(solution)/shard_map/ppermute | solution.py:23
  208.4 13.3 while.22
  221.7 14.5 copy.271
  245.3 9.1 copy.276
  254.4 9.0 copy.273
  263.4 13.8 fusion.145
  277.2 9.7 fusion.64
  316.2 15.8 multiply_convert_fusion.2
  332.0 16.2 fusion.13
  348.2 11.9 multiply_reduce_fusion.3
  392.9 13.8 multiply_reduce_fusion.1
  411.4 27.1 fusion.5
  439.2 35.3 %all-gather = f32[16,12,1024]{2,1,0:T(8,128)} all-gather(f32[2,12,1024]{2,1,0:T(8,128)S(1)} %get-tuple-element.344), channel_id=2, replica_groups=mesh['page'=4,'strip'=8] {'strip'}, dimensions={0}, use_global_device_ids=true | all-gather | bytes 884736 | tf_op jit(solution)/shard_map/all_gather | solution.py:29
  474.5 23.4 exponential_reduce_fusion
  497.9 33.0 %all-gather.1 = f32[16,12,1024]{2,1,0:T(8,128)S(1)} all-gather(f32[2,12,1024]{2,1,0:T(8,128)} %exponential_reduce_fusion), channel_id=3, replica_groups=mesh['page'=4,'strip'=8] {'strip'}, dimensions={0}, use_global_device_ids=true | all-gather | bytes 884736 | tf_op jit(solution)/shard_map/all_gather | solution.py:29
  533.1 12.8 while.20
  547.6 28.5 fusion.82
  582.7 11.8 multiply_convert_fusion.1
  603.8 19.1 copy.294
  622.9 14.6 concatenate.105
  637.5 10.9 convolution_bitcast_fusion
  648.4 19.0 copy.296
  667.4 14.8 concatenate.106
  688.3 12.2 copy.297
  700.5 36.7 %pad_maximum_fusion = f32[2,12,192,1536]{3,0,2,1:T(2,128)} fusion(f32[2,12,96,1536]{3,0,2,1:T(2,128)} %bitcast.423), kind=kLoop, calls=%fused_computation.22 | loop fusion | flops 7077888 | bytes 42467328 | tf_op jit(solution)/shard_map/vmap(jit(_roll_dynamic))/concatenate | solution.py:71
  737.2 27.4 while.21
  737.8 9.2 constant_dynamic-slice_fusion.8
  751.5 9.2 constant_dynamic-slice_fusion.8
  764.6 7.5 select_convert_fusion
  776.9 8.4 multiply_bitcast_fusion.1
  785.3 7.6 copy.290
  851.4 10.1 copy.311
  865.4 11.2 convolution_bitcast_fusion.4
  876.5 11.6 reshape.431
  888.2 9.9 copy.312
  898.1 11.2 convolution_bitcast_fusion.3
  909.3 11.5 copy.314
  920.8 10.8 reshape.434
  931.5 10.7 add_convert_fusion
  942.2 10.9 fusion.18
  958.2 50.6 %multiply_reduce_fusion = (f32[2,12,1024]{2,1,0:T(8,128)}, f32[2,12,1024,704]{2,3,1,0:T(8,128)}) fusion(f32[2,12,1024,704]{2,3,1,0:T(8,128)} %get-tuple-element.345, f32[2,12,1024]{2,1,0:T(8,128)} %log_add_fusion, pred[2,1024,704]{1,2,0:T(8,128)(4,1)} %pad_add_fusion, bf16[2,1024,12,64]{1,3,2,0:T(8,128)(2,1)} %bitcast.436, ...), kind=kOutput, calls=%fused_computation.16 | convolution fusion | flops 2305400832 | bytes 145358848 | tf_op jit(solution)/shard_map/bihd,bjhd->bhij/dot_general | solution.py:289
  1014.1 8.5 copy.307
  1022.7 54.3 %all-reduce.7.cloned.1.call-done = f32[2,12,1024]{2,1,0:T(8,128)} async-done(((f32[2,12,1024]{2,1,0:T(8,128)}), f32[2,12,1024]{2,1,0:T(8,128)}) %all-reduce.7.cloned.1.call-update) | async-done | bytes 98320 | tf_op jit(solution)/shard_map/psum | solution.py:296
  1077.0 56.0 %multiply_convert_fusion = bf16[2,12,1024,704]{2,3,1,0:T(8,128)(2,1)} fusion(f32[2,12,1024,704]{2,3,1,0:T(8,128)} %get-tuple-element.353, f32[2,12,1024,704]{2,3,1,0:T(8,128)} %get-tuple-element.345, f32[2,12,1024]{2,1,0:T(8,128)} %all-reduce.7.cloned.1.call-done, f32[2,12,1024]{2,1,0:T(8,128)} %log_add_fusion, pred[2,1024,704]{1,2,0:T(8,128)(4,1)} %pad_add_fusion), kind=kLoop, calls=%fused_computation.15 | loop fusion | flops 103809024 | bytes 174653440 | tf_op jit(solution)/shard_map/convert_element_type | solution.py:297
  1133.0 17.6 broadcast_multiply_fusion
  1157.2 9.7 convolution_bitcast_fusion.6
  1166.9 10.4 reshape.425
  1200.9 11.7 reshape.443
  1221.7 11.7 copy.324
  1233.5 10.8 reshape.446
  1249.9 28.4 fusion.114
  1289.0 18.4 broadcast_multiply_fusion.1
  1340.0 8.1 convolution_bitcast_fusion.7
  1376.5 10.7 reshape.436
  1392.7 10.2 copy_dynamic-update-slice_fusion.4
  1405.8 13.0 copy_dynamic-update-slice_fusion.2
  1423.1 10.3 copy_dynamic-update-slice_fusion.3
  1441.1 9.3 copy_dynamic-update-slice_fusion.1
  1450.4 7.9 constant_dynamic-update-slice_fusion
  1458.3 43.4 %copy.332 = f32[8,4,479360]{2,1,0:T(4,128)} copy(f32[8,4,479360]{2,0,1:T(8,128)} %constant_dynamic-update-slice_fusion) | data formatting | bytes 122716160 | tf_op jit(solution)/shard_map/concatenate | solution.py:157
  1501.7 74.4 %reshape.447 = f32[119840,128]{1,0:T(8,128)} reshape(f32[8,4,479360]{2,1,0:T(4,128)} %copy.332) | data formatting | bytes 122716160 | tf_op jit(solution)/shard_map/reshape | solution.py:158
  1576.1 1197.3 %fusion = f32[15008,128]{1,0:T(8,128)} fusion(f32[119840,128]{1,0:T(8,128)} %reshape.447), kind=kCustom, calls=%all-reduce-scatter | all-reduce-scatter fusion | flops 15368193 | bytes 69042688
  2777.4 19.0 concatenate.154
  2800.3 37.8 %fusion.1 = bf16[3760,128]{1,0:T(8,128)(2,1)} fusion(bf16[14980,128]{1,0:T(8,128)(2,1)} %dynamic-slice_convert_fusion), kind=kCustom, calls=%all-reduce-scatter.1 | all-reduce-scatter fusion | flops 1925121 | bytes 4797952
  (405 shorter events, 516.1 us)
Async XLA Ops:
  7.2 6.2 copy-start
  7.2 4.3 copy-start.56
  7.2 399.6 %all-gather.5.cloned.1.call-start = ((), (), s32[]{:S(2)}) async-start(), calls=%async_computation.2 | async-start | bytes 3538944 | tf_op jit(solution)/shard_map/all_gather | solution.py:234
  7.2 5.5 copy-start.2
  12.1 14.3 copy-start.43
  13.3 4.5 copy-start.20
  17.9 8.3 copy-start.23
  17.9 8.1 copy-start.11
  17.9 9.3 copy-start.71
  20.0 176.7 %collective-permute-start = (bf16[2,6,96,1536]{3,2,1,0:T(8,128)(2,1)}, bf16[2,6,96,1536]{3,2,1,0:T(8,128)(2,1)}, u32[]{:S(2)}, u32[]{:S(2)}) collective-permute-start(bf16[2,6,96,1536]{3,2,1,0:T(8,128)(2,1)} %slice.203), channel_id=1, source_target_pairs={{1,0},{2,1},{3,2},{4,3},{5,4},{6,5},{7,6},{0,7},{9,8},{10,9},{11,1... | collective-permute-start | bytes 10616840 | tf_op jit(solution)/shard_map/ppermute | solution.py:23
  26.0 170.9 %collective-permute-start.1 = (bf16[2,6,96,1536]{3,2,1,0:T(8,128)(2,1)}, bf16[2,6,96,1536]{3,2,1,0:T(8,128)(2,1)}, u32[]{:S(2)}, u32[]{:S(2)}) collective-permute-start(bf16[2,6,96,1536]{3,2,1,0:T(8,128)(2,1)} %slice.203), channel_id=1, source_target_pairs={{0,1},{1,2},{2,3},{3,4},{4,5},{5,6},{6,7},{7,0},{8,9},{9,10},{10,1... | collective-permute-start | bytes 10616840 | tf_op jit(solution)/shard_map/ppermute | solution.py:20
  29.4 792.0 %reduce-scatter.7.cloned.1.call-start = ((), (), s32[]{:S(2)}) async-start(), calls=%async_computation.3 | async-start | bytes 7077888 | tf_op jit(solution)/shard_map/reduce_scatter | solution.py:269
  44.5 7.6 copy-start.75
  57.6 9.5 copy-start.70
  67.1 8.4 copy-start.54
  67.1 239.4 %copy-start.52 = (s32[2]{0:T(128)}, s32[2]{0:T(128)S(1)}, u32[]{:S(2)}) copy-start(s32[2]{0:T(128)S(1)} %get-tuple-element.309) | copy-start | bytes 28
  97.8 13.4 copy-start.57
  111.9 90.9 %copy-start.63 = (pred[2]{0:T(512)(128)(4,1)}, pred[2]{0:T(512)(128)(4,1)S(1)}, u32[]{:S(2)}) copy-start(pred[2]{0:T(512)(128)(4,1)S(1)} %compare_compare_fusion) | copy-start | bytes 10
  202.9 5.6 copy-start.69
  315.1 45.1 %copy-start.7 = (f32[2,6,96,768]{3,2,1,0:T(8,128)}, f32[2,6,96,768]{3,2,1,0:T(8,128)S(1)}, u32[]{:S(2)}) copy-start(f32[2,6,96,768]{3,2,1,0:T(8,128)S(1)} %get-tuple-element.341) | copy-start | bytes 10616836
  316.2 15.8 copy-start.17
  316.2 15.8 copy-start.8
  348.2 11.9 copy-start.16
  366.6 4.3 copy-start.55
  582.7 370.5 %all-gather.7.cloned.1.call-start = ((), (), s32[]{:S(2)}) async-start(), calls=%async_computation.4 | async-start | bytes 3538944 | tf_op jit(solution)/shard_map/all_gather | solution.py:286
  582.7 14.8 copy-start.5
  700.5 36.7 %copy-start.68 = (s32[2,4]{1,0:T(2,128)S(1)}, s32[2,4]{1,0:T(2,128)}, u32[]{:S(2)}) copy-start(s32[2,4]{1,0:T(2,128)} %copy.299) | copy-start | bytes 100
  737.2 27.4 copy-start.64
  772.1 170.1 %collective-permute-start.2 = (bf16[2,6,96,1536]{3,2,1,0:T(8,128)(2,1)}, bf16[2,6,96,1536]{3,2,1,0:T(8,128)(2,1)}, u32[]{:S(2)}, u32[]{:S(2)}) collective-permute-start(bf16[2,6,96,1536]{3,2,1,0:T(8,128)(2,1)} %select_convert_fusion), channel_id=1, source_target_pairs={{0,1},{1,2},{2,3},{3,4},{4,5},{5,6},{6,7},{7,0},{8,9},{9,10},{10,1... | collective-permute-start | bytes 10616840 | tf_op jit(solution)/shard_map/ppermute | solution.py:20
  774.2 168.0 %collective-permute-start.3 = (bf16[2,6,96,1536]{3,2,1,0:T(8,128)(2,1)}, bf16[2,6,96,1536]{3,2,1,0:T(8,128)(2,1)}, u32[]{:S(2)}, u32[]{:S(2)}) collective-permute-start(bf16[2,6,96,1536]{3,2,1,0:T(8,128)(2,1)} %select_convert_fusion), channel_id=1, source_target_pairs={{1,0},{2,1},{3,2},{4,3},{5,4},{6,5},{7,6},{0,7},{9,8},{10,9},{11,1... | collective-permute-start | bytes 10616840 | tf_op jit(solution)/shard_map/ppermute | solution.py:23
  805.1 7.8 copy-start.66
  817.5 8.1 copy-start.47
  821.4 10.3 slice-start.10
  825.4 11.6 copy-start.13
  825.9 5.8 copy-start.33
  825.9 5.8 copy-start.26
  825.9 5.8 slice-start.11
  825.9 8.8 slice-start.8
  840.4 236.6 %all-reduce.7.cloned.1.call-start = ((), (), s32[]{:S(2)}) async-start(), calls=%async_computation.5 | async-start | bytes 262144 | tf_op jit(solution)/shard_map/psum | solution.py:296
  1008.8 352.1 %reduce-scatter.9.cloned.1.call-start = ((), (), s32[]{:S(2)}) async-start(), calls=%async_computation.6 | async-start | bytes 7077888 | tf_op jit(solution)/shard_map/reduce_scatter | solution.py:314
  1166.9 10.4 copy-start.67
  1318.1 4.2 copy-start.72
  1325.4 4.9 copy-start.42
  1325.4 5.0 copy-start.38
  1362.1 5.0 copy-start.31
  1362.1 5.0 copy-start.32
  1376.4 10.8 copy-start.61
  1376.4 12.0 copy-start.44
  1376.5 12.0 copy-start.49
  1376.5 12.0 copy-start.51
  1392.7 10.2 copy-start.14
  1392.7 26.1 slice-start.3
  1392.7 26.1 slice-start.4
  1405.8 13.0 slice-start.5
  1405.8 27.6 slice-start.6
  1418.8 14.6 slice-start.7
  1423.1 17.9 slice-start
  1423.1 17.9 slice-start.1
  1433.4 4.9 copy-start.15
  1433.4 7.7 slice-start.2
  1576.1 1200.1 %copy-start.65 = (f32[2,128]{1,0:T(2,128)S(1)}, f32[2,128]{1,0:T(2,128)}, u32[]{:S(2)}) copy-start(f32[2,128]{1,0:T(2,128)} %get-tuple-element.272) | copy-start | bytes 3076
  2774.3 3.1 collective-permute-start.4
  2800.3 40.4 %copy-start.59 = (f32[2,128]{1,0:T(2,128)S(1)}, f32[2,128]{1,0:T(2,128)}, u32[]{:S(2)}) copy-start(f32[2,128]{1,0:T(2,128)} %copy-done.58) | copy-start | bytes 3076
  2838.8 4.8 collective-permute-start.5
  (35 other events, 70.1 us)
Sparse Core Ops, SparseCore 0:
  29.5 146.4 all-gather.4
  582.8 119.2 reduce-scatter.6
  840.6 79.2 all-gather.6
  1008.9 68.0 all-reduce.6
  1157.3 117.2 reduce-scatter.8
where the time goes:
time: 2910 us; the launch traced here: 2880 us
  blocking collectives  1300 us (45%)
  local copies, waits for them, and re-layouts  778 us (27%)
  matrix products  403 us (14%)
  other arithmetic  231 us (8%)
  waiting for transfers between devices  136 us (5%)
    unnamed x2, blocking collectives  1240 us
    unnamed x198, local copies, waits for them, and re-layouts  117 us
    reshape x9, local copies, waits for them, and re-layouts, pack_grads(): block.transpose(0, 2, 1, 3).reshape(strip_count, page_count, -1)  81.7 us
    ppermute x2, waiting for transfers between devices, extended(): lax.ppermute(lax.slice_in_dim(block, 0, width, axis=dim), axis, backward)  81.2 us
    reshape x1, local copies, waits for them, and re-layouts, pack_grads(): return packed.reshape(-1, 128)  74.4 us
    dot_general x16, local copies, waits for them, and re-layouts, outer_sum(): lax.dot_general(flat_left, flat_right, (((0,), (0,)), ((), ())), preferre...  69 us
    all_gather x2, blocking collectives, combined_all(): everything = jax.tree.map(lambda part: lax.all_gather(part, axis), array)  68.3 us
    dot_general x9, matrix products, outer_sum(): lax.dot_general(flat_left, flat_right, (((0,), (0,)), ((), ())), preferre...  68.3 us
  transfers between devices with their start and end apart: 11, of which 4 were waited for; matrix products, arithmetic and copies ran while one was open for 30% of the time, Pallas kernels for 0%

commit v1 on v0

v1 whole, which is shorter than its diff:
```python
import functools

import jax
import jax.numpy as jnp
from jax import lax
from jax.experimental import pallas as pl
from jax.experimental.pallas import tpu as pltpu
from jax.sharding import PartitionSpec as P

HEADS = 12
WIN = 12
EPS = 1e-05
MASKED = -1e9
SCALE = 0.125
BF = jnp.bfloat16
F32 = jnp.float32
LANES = 128
VMEM_BYTES = 60 * 1024 * 1024


def dot(left, right, left_dim=1, right_dim=0):
    return lax.dot_general(
        left, right, (((left_dim,), (right_dim,)), ((), ())), preferred_element_type=F32
    )


def iota(shape, dim):
    return lax.broadcasted_iota(jnp.int32, shape, dim)


def norm_stats(rows):
    offset = rows - jnp.mean(rows, axis=-1, keepdims=True)
    spread = lax.rsqrt(jnp.mean(offset * offset, axis=-1, keepdims=True) + EPS)
    return offset * spread, spread


def norm_back(unit, spread, gain, grad):
    product = grad * unit
    scaled = grad * gain
    centre = jnp.mean(scaled, axis=-1, keepdims=True)
    slope = jnp.mean(scaled * unit, axis=-1, keepdims=True)
    return spread * (scaled - centre - unit * slope), jnp.sum(product, axis=0, keepdims=True)


def gelu_pair(t):
    square = t * t
    th = jnp.tanh(0.7978845608 * (t + 0.044715 * t * square))
    plus = 0.5 * (1.0 + th)
    slope = plus + 0.5 * t * (1.0 - th * th) * (0.7978845608 * (1.0 + 0.134145 * square))
    return t * plus, slope


def three_parts(value):
    high = value.astype(BF).astype(F32)
    rest = value - high
    middle = rest.astype(BF).astype(F32)
    low = (rest - middle).astype(BF).astype(F32)
    return high, middle, low


def place_lanes(column, lane, first):
    high, middle, low = three_parts(column)
    return (
        jnp.where(lane == first, high, 0.0)
        + jnp.where(lane == first + 16, middle, 0.0)
        + jnp.where(lane == first + 32, low, 0.0)
    )


def join_lanes(stats, first):
    total = stats
    rolled = []
    for part in range(3):
        amount = (first + 16 * part) % LANES
        rolled.append(total if amount == 0 else pltpu.roll(total, LANES - amount, 1))
    return rolled[0] + rolled[1] + rolled[2]


def spread_heads(values, width):
    head_dim = width // HEADS
    pick = (iota((LANES, width), 0) == iota((LANES, width), 1) // head_dim).astype(BF)
    high, middle, low = three_parts(values)
    return dot(high.astype(BF), pick) + dot(middle.astype(BF), pick) + dot(low.astype(BF), pick)


def params(limit=VMEM_BYTES):
    return pltpu.CompilerParams(vmem_limit_bytes=limit)


def whole(shape):
    return pl.BlockSpec(shape, lambda *_: (0,) * len(shape))


def cost(flops, moved, exps=0):
    return pl.CostEstimate(flops=int(flops), bytes_accessed=int(moved), transcendentals=int(exps))


def sds(shape, kind):
    return jax.ShapeDtypeStruct(shape, kind)


def patch_in_kernel(src_ref, own_ref, other_ref, gain_ref, wq_ref, wx_ref, x_ref, n_ref, qkv_ref, cross_ref):
    half = own_ref.shape[0]
    part = src_ref.shape[0] // 2
    pieces = []
    for k in range(2):
        onehot = (iota((part, half), 1) == src_ref[k * part : (k + 1) * part, :]).astype(F32).astype(BF)
        pieces.append(dot(onehot, own_ref[...]))
        pieces.append(dot(onehot, other_ref[...]))
    x = jnp.concatenate(pieces, axis=0)
    x_ref[...] = x.astype(BF)
    unit, _ = norm_stats(x)
    normed = (unit * gain_ref[0:1, :]).astype(BF)
    n_ref[...] = normed
    qkv_ref[...] = dot(normed, wq_ref[...]).astype(BF)
    cross_ref[...] = dot(normed, wx_ref[...]).astype(BF)


def patch_in(src, own, other, gains, wq, wx):
    half, width = own.shape
    tokens = 2 * half
    step = 4 * half // (half // 72)
    rows = lambda w: pl.BlockSpec((step, w), lambda i: (i, 0))
    return pl.pallas_call(
        patch_in_kernel,
        grid=(tokens // step,),
        in_specs=[
            pl.BlockSpec((step // 2, 1), lambda i: (i, 0)),
            whole(own.shape),
            whole(own.shape),
            whole(gains.shape),
            whole(wq.shape),
            whole(wx.shape),
        ],
        out_specs=[rows(width), rows(width), rows(wq.shape[1]), rows(wx.shape[1])],
        out_shape=[
            sds((tokens, width), BF),
            sds((tokens, width), BF),
            sds((tokens, wq.shape[1]), BF),
            sds((tokens, wx.shape[1]), BF),
        ],
        compiler_params=params(),
        cost_estimate=cost(2 * tokens * width * (wq.shape[1] + wx.shape[1]), 2e7),
        name="patch_in",
    )(src, own, other, gains, wq, wx)


def window_kernel(qkv_ref, out_ref, stat_ref):
    tokens, width = out_ref.shape
    lane = iota((1, LANES), 1)
    left = lane < 64
    stats = jnp.zeros((tokens, LANES), F32)
    for pair in range(HEADS // 2):
        at = pair * LANES
        q = qkv_ref[:, at : at + LANES] * SCALE
        k = qkv_ref[:, width + at : width + at + LANES]
        v = qkv_ref[:, 2 * width + at : 2 * width + at + LANES]
        mixed = []
        for side in range(2):
            mine = left if side == 0 else ~left
            scores = dot(jnp.where(mine, q, 0).astype(BF), k, 1, 1)
            peak = jnp.max(scores, axis=-1, keepdims=True)
            raised = jnp.exp(scores - peak)
            total = jnp.sum(raised, axis=-1, keepdims=True)
            probs = (raised * (1.0 / total)).astype(BF)
            mixed.append(dot(probs, v))
            stats = stats + place_lanes(peak + jnp.log(total), lane, 2 * pair + side)
        out_ref[:, at : at + LANES] = jnp.where(left, mixed[0], mixed[1]).astype(BF)
    stat_ref[...] = stats.astype(BF)


def window_forward(qkv, tokens):
    total, width3 = qkv.shape
    width = width3 // 3
    return pl.pallas_call(
        window_kernel,
        grid=(total // tokens,),
        in_specs=[pl.BlockSpec((tokens, width3), lambda i: (i, 0))],
        out_specs=[
            pl.BlockSpec((tokens, width), lambda i: (i, 0)),
            pl.BlockSpec((tokens, LANES), lambda i: (i, 0)),
        ],
        out_shape=[sds((total, width), BF), sds((total, LANES), BF)],
        compiler_params=params(),
        cost_estimate=cost(16 * total * tokens * width, 8e6, total * tokens * HEADS),
        name="window_forward",
    )(qkv)


def stat_lanes(stats, head, first, base):
    row, col = iota((LANES, LANES), 0), iota((LANES, LANES), 1)
    hit = (row == first + head + 16 * (col - base)) & (col >= base) & (col < base + 3)
    return dot(stats, jnp.where(hit, -1.0, 0.0).astype(BF))


def window_back_kernel(qkv_ref, go_ref, stat_ref, out_ref):
    tokens, width = go_ref.shape
    lane = iota((1, LANES), 1)
    left = lane < 64
    stats = stat_ref[...]
    for pair in range(HEADS // 2):
        at = pair * LANES
        q = qkv_ref[:, at : at + LANES]
        k = qkv_ref[:, width + at : width + at + LANES]
        v = qkv_ref[:, 2 * width + at : 2 * width + at + LANES]
        g = go_ref[:, at : at + LANES]
        parts = []
        for side in range(2):
            mine = left if side == 0 else ~left
            base = 64 * (1 - side)
            ones = (lane >= base) & (lane < base + 3)
            shifted = jnp.where(mine, q.astype(F32) * SCALE, stat_lanes(stats, 2 * pair + side, 0, base))
            keys = jnp.where(mine, k.astype(F32), jnp.where(ones, 1.0, 0.0)).astype(BF)
            probs = jnp.exp(dot(keys, shifted.astype(BF), 1, 1))
            grads = dot(jnp.where(mine, v.astype(F32), 0.0).astype(BF), g, 1, 1)
            inner = jnp.sum(probs * grads, axis=0, keepdims=True)
            dscore = (probs * (grads - inner)).astype(BF)
            parts.append((dot(dscore, k, 0, 0), dot(dscore, q), dot(probs.astype(BF), g)))
        for index, factor in ((0, SCALE), (1, SCALE), (2, 1.0)):
            joined = jnp.where(left, parts[0][index], parts[1][index]) * factor
            out_ref[:, index * width + at : index * width + at + LANES] = joined.astype(BF)


def window_backward(qkv, go, stats, tokens):
    total, width3 = qkv.shape
    width = width3 // 3
    rows = lambda w: pl.BlockSpec((tokens, w), lambda i: (i, 0))
    return pl.pallas_call(
        window_back_kernel,
        grid=(total // tokens,),
        in_specs=[rows(width3), rows(width), rows(LANES)],
        out_specs=rows(width3),
        out_shape=sds((total, width3), BF),
        compiler_params=params(),
        cost_estimate=cost(40 * total * tokens * width, 1.3e7, total * tokens * HEADS),
        name="window_backward",
    )(qkv, go, stats)


def split_halves(rows, part):
    count = rows.shape[0] // (2 * part)
    return [
        jnp.concatenate([rows[(2 * w + s) * part : (2 * w + s + 1) * part] for w in range(count)], axis=0)
        for s in range(2)
    ]


def patch_ffn_kernel(
    src_ref, inv_ref, att_ref, x_ref, own_ref, other_ref, gain_ref, wo_ref, up_ref, down_ref,
    out_own_ref, out_other_ref, after_grad_ref, att_grad_ref, wo_grad_ref, up_grad_ref, down_grad_ref, gain_grad_ref,
    after, normed, cot, total, back, acts, dacts,
):
    step = pl.program_id(0)
    tokens, width = att_ref.shape
    half = own_ref.shape[0]
    part = 72
    block = 4 * part

    @pl.when(step == 0)
    def _():
        for b in range(tokens // block):
            rows = slice(b * block, (b + 1) * block)
            value = x_ref[rows, :].astype(F32) + dot(att_ref[rows, :], wo_ref[...])
            after[rows, :] = value
            unit, _ = norm_stats(value)
            normed[rows, :] = (unit * gain_ref[1:2, :]).astype(BF)
            pieces = []
            for k in range(2):
                table = src_ref[(2 * b + k) * part : (2 * b + k + 1) * part, :]
                onehot = (iota((part, half), 1) == table).astype(F32).astype(BF)
                pieces.append(dot(onehot, own_ref[...]))
                pieces.append(dot(onehot, other_ref[...]))
            cot[rows, :] = jnp.concatenate(pieces, axis=0).astype(BF)
        total[...] = jnp.zeros_like(total)
        back[...] = jnp.zeros_like(back)

    for b in range(tokens // block):
        rows = slice(b * block, (b + 1) * block)
        value, slope = gelu_pair(dot(normed[rows, :], up_ref[...]))
        act = value.astype(BF)
        acts[rows, :] = act
        total[rows, :] += dot(act, down_ref[...])
        dact = (slope * dot(cot[rows, :], down_ref[...], 1, 1)).astype(BF)
        dacts[rows, :] = dact
        back[rows, :] += dot(dact, up_ref[...], 1, 1)
    up_grad_ref[...] = dot(normed[...], dacts[...], 0, 0).astype(BF)
    down_grad_ref[...] = dot(acts[...], cot[...], 0, 0).astype(BF)

    @pl.when(step == pl.num_programs(0) - 1)
    def _():
        gain_sum = jnp.zeros((1, width), F32)
        for b in range(tokens // block):
            rows = slice(b * block, (b + 1) * block)
            unit, spread = norm_stats(after[rows, :])
            grad, gain_part = norm_back(unit, spread, gain_ref[1:2, :], back[rows, :])
            gain_sum = gain_sum + gain_part
            grad = cot[rows, :].astype(F32) + grad
            after_grad_ref[rows, :] = grad
            branch = grad.astype(BF)
            normed[rows, :] = branch
            att_grad_ref[rows, :] = dot(branch, wo_ref[...], 1, 1).astype(BF)
        gain_grad_ref[...] = jnp.broadcast_to(gain_sum, gain_grad_ref.shape)
        wo_grad_ref[...] = dot(att_ref[...], normed[...], 0, 0).astype(BF)
        halves = split_halves(after[...] + total[...], part)
        onehot = (iota((half, half), 1) == inv_ref[...]).astype(F32).astype(BF)
        out_own_ref[...] = dot(onehot, halves[0].astype(BF)).astype(BF)
        out_other_ref[...] = dot(onehot, halves[1].astype(BF)).astype(BF)


def patch_ffn(src, inv, att, x, own, other, gains, wo, up, down, chunk=384):
    tokens, width = att.shape
    half = tokens // 2
    hidden = up.shape[1]
    return pl.pallas_call(
        patch_ffn_kernel,
        grid=(hidden // chunk,),
        in_specs=[whole(a.shape) for a in (src, inv, att, x, own, other, gains, wo)]
        + [pl.BlockSpec((width, chunk), lambda j: (0, j)), pl.BlockSpec((chunk, width), lambda j: (j, 0))],
        out_specs=[
            whole((half, width)),
            whole((half, width)),
            whole((tokens, width)),
            whole((tokens, width)),
            whole((width, width)),
            pl.BlockSpec((width, chunk), lambda j: (0, j)),
            pl.BlockSpec((chunk, width), lambda j: (j, 0)),
            whole((8, width)),
        ],
        out_shape=[
            sds((half, width), BF),
            sds((half, width), BF),
            sds((tokens, width), F32),
            sds((tokens, width), BF),
            sds((width, width), BF),
            sds((width, hidden), BF),
            sds((hidden, width), BF),
            sds((8, width), F32),
        ],
        scratch_shapes=[
            pltpu.VMEM((tokens, width), F32),
            pltpu.VMEM((tokens, width), BF),
            pltpu.VMEM((tokens, width), BF),
            pltpu.VMEM((tokens, width), F32),
            pltpu.VMEM((tokens, width), F32),
            pltpu.VMEM((tokens, chunk), BF),
            pltpu.VMEM((tokens, chunk), BF),
        ],
        compiler_params=params(),
        cost_estimate=cost(12 * tokens * width * hidden, 4e7, tokens * hidden),
        name="patch_ffn",
    )(src, inv, att, x, own, other, gains, wo, up, down)


def patch_back_kernel(
    inv_ref, gp_ref, gk_ref, gv_ref, n_ref, x_ref, after_ref, gain_ref, wq_ref, wx_ref,
    own_ref, other_ref, wq_grad_ref, wx_grad_ref, gain_grad_ref, back,
    *, q_steps, k_steps,
):
    step = pl.program_id(0)
    half, width = own_ref.shape
    tokens = 2 * half
    part = 72
    block = 4 * part

    @pl.when(step == 0)
    def _():
        back[...] = jnp.zeros_like(back)

    def one(grad_ref, weight_ref, out_ref):
        back[...] += dot(grad_ref[...], weight_ref[...], 1, 1)
        out_ref[...] = dot(n_ref[...], grad_ref[...], 0, 0).astype(BF)

    @pl.when(step < q_steps)
    def _():
        one(gp_ref, wq_ref, wq_grad_ref)

    @pl.when((step >= q_steps) & (step < q_steps + k_steps))
    def _():
        one(gk_ref, wx_ref, wx_grad_ref)

    @pl.when(step >= q_steps + k_steps)
    def _():
        one(gv_ref, wx_ref, wx_grad_ref)

    @pl.when(step == pl.num_programs(0) - 1)
    def _():
        gain_sum = jnp.zeros((1, width), F32)
        for b in range(tokens // block):
            rows = slice(b * block, (b + 1) * block)
            unit, spread = norm_stats(x_ref[rows, :].astype(F32))
            grad, gain_part = norm_back(unit, spread, gain_ref[0:1, :], back[rows, :])
            gain_sum = gain_sum + gain_part
            back[rows, :] = after_ref[rows, :] + grad
        gain_grad_ref[...] = jnp.broadcast_to(gain_sum, gain_grad_ref.shape)
        halves = split_halves(back[...], part)
        onehot = (iota((half, half), 1) == inv_ref[...]).astype(F32).astype(BF)
        high = halves[0].astype(BF)
        low = (halves[0] - high.astype(F32)).astype(BF)
        own_ref[...] = dot(onehot, high) + dot(onehot, low)
        other_ref[...] = dot(onehot, halves[1].astype(BF)).astype(BF)


def patch_back(inv, gp, gk, gv, normed, x, after, gains, wq, wx, chunk=384):
    tokens, width = x.shape
    half = tokens // 2
    q_steps, k_steps = wq.shape[1] // chunk, width // chunk
    steps = q_steps + 2 * k_steps
    at_q = lambda j: jnp.minimum(j, q_steps - 1)
    at_x = lambda j: jnp.maximum(j - q_steps, 0)
    at_k = lambda j: jnp.clip(j - q_steps, 0, k_steps - 1)
    at_v = lambda j: jnp.clip(j - q_steps - k_steps, 0, k_steps - 1)
    return pl.pallas_call(
        functools.partial(patch_back_kernel, q_steps=q_steps, k_steps=k_steps),
        grid=(steps,),
        in_specs=[
            whole(inv.shape),
            pl.BlockSpec((tokens, chunk), lambda j: (0, at_q(j))),
            pl.BlockSpec((tokens, chunk), lambda j: (0, at_k(j))),
            pl.BlockSpec((tokens, chunk), lambda j: (0, at_v(j))),
            whole(normed.shape),
            whole(x.shape),
            whole(after.shape),
            whole(gains.shape),
            pl.BlockSpec((width, chunk), lambda j: (0, at_q(j))),
            pl.BlockSpec((width, chunk), lambda j: (0, at_x(j))),
        ],
        out_specs=[
            whole((half, width)),
            whole((half, width)),
            pl.BlockSpec((width, chunk), lambda j: (0, at_q(j))),
            pl.BlockSpec((width, chunk), lambda j: (0, at_x(j))),
            whole((8, width)),
        ],
        out_shape=[
            sds((half, width), F32),
            sds((half, width), BF),
            sds(wq.shape, BF),
            sds(wx.shape, BF),
            sds((8, width), F32),
        ],
        scratch_shapes=[pltpu.VMEM((tokens, width), F32)],
        compiler_params=params(),
        cost_estimate=cost(4 * tokens * width * (wq.shape[1] + wx.shape[1]), 4e7),
        name="patch_back",
    )(inv, gp, gk, gv, normed, x, after, gains, wq, wx)


def query_in_kernel(x_ref, gain_ref, w_ref, n_ref, q_ref, kv_ref):
    unit, _ = norm_stats(x_ref[...].astype(F32))
    normed = (unit * gain_ref[2:3, :]).astype(BF)
    n_ref[...] = normed
    width = x_ref.shape[1]
    q_ref[...] = dot(normed, w_ref[:, :width]).astype(BF)
    kv_ref[...] = dot(normed, w_ref[:, width:]).astype(BF)


def query_in_call(x, gains, w):
    slots, width = x.shape
    return pl.pallas_call(
        query_in_kernel,
        out_shape=[sds((slots, width), BF), sds((slots, width), BF), sds((slots, 2 * width), BF)],
        compiler_params=params(),
        cost_estimate=cost(2 * slots * width * w.shape[1], 5e6),
        name="query_in",
    )(x, gains, w)


def row_blocks(total, first, length, most=256):
    blocks = []
    for low, high in ((0, first), (first + length, total)):
        at = low
        while at < high:
            count = -(-(high - at) // most)
            size = min(high - at, -(-((high - at) // count) // 16) * 16)
            blocks.append((at, size, False))
            at += size
    blocks.append((first, length, True))
    return blocks


def query_forward_kernel(q_ref, k_ref, v_ref, sk_ref, sv_ref, kb_ref, qs_ref, ks_ref, out_ref, stat_ref, held, *, blocks):
    pair = pl.program_id(0)
    lane = iota((1, LANES), 1)
    left = lane < 64

    @pl.when(pair == 0)
    def _():
        held[...] = jnp.zeros_like(held)

    keys = []
    for side in range(2):
        keys.append(jnp.where(lane == 64 * (1 - side), kb_ref[...], k_ref[...]))
    for at, size, near in blocks:
        q = q_ref[at : at + size, :].astype(F32) * SCALE
        mixed, columns = [], jnp.zeros((size, LANES), F32)
        for side in range(2):
            mine = left if side == 0 else ~left
            own = jnp.where(mine, q, jnp.where(lane == 64 * (1 - side), 1.0, 0.0)).astype(BF)
            scores = dot(own, keys[side], 1, 1)
            peak = jnp.max(scores, axis=-1, keepdims=True)
            if near:
                extra = dot(jnp.where(mine, q, 0.0).astype(BF), sk_ref[...], 1, 1)
                extra = jnp.where(qs_ref[...] == ks_ref[...], extra, MASKED)
                peak = jnp.maximum(peak, jnp.max(extra, axis=-1, keepdims=True))
            raised = jnp.exp(scores - peak)
            total = jnp.sum(raised, axis=-1, keepdims=True)
            value = dot(raised.astype(BF), v_ref[...])
            if near:
                raised = jnp.exp(extra - peak)
                total = total + jnp.sum(raised, axis=-1, keepdims=True)
                value = value + dot(raised.astype(BF), sv_ref[...])
            mixed.append(value * (1.0 / total))
            columns = columns + place_lanes(peak + jnp.log(total), lane, 2 * pair + side)
        out_ref[at : at + size, :] = jnp.where(left, mixed[0], mixed[1]).astype(BF)
        held[at : at + size, :] += columns

    @pl.when(pair == pl.num_programs(0) - 1)
    def _():
        stat_ref[...] = held[...].astype(BF)


def query_forward(q, cross, slot_kv, key_bias, q_seg, k_seg, blocks):
    total, width = q.shape
    patches, slots = cross.shape[0], slot_kv.shape[0]
    pairs = HEADS // 2
    col = lambda rows, first: pl.BlockSpec((rows, LANES), lambda p: (0, first + p))
    return pl.pallas_call(
        functools.partial(query_forward_kernel, blocks=blocks),
        grid=(pairs,),
        in_specs=[
            col(total, 0), col(patches, 0), col(patches, pairs), col(slots, 0), col(slots, pairs),
            whole(key_bias.shape), whole(q_seg.shape), whole(k_seg.shape),
        ],
        out_specs=[col(total, 0), whole((total, LANES))],
        out_shape=[sds((total, width), BF), sds((total, LANES), BF)],
        scratch_shapes=[pltpu.VMEM((total, LANES), F32)],
        compiler_params=params(),
        cost_estimate=cost(16 * total * patches * width, 1e7, total * patches * HEADS),
        name="query_forward",
    )(q, cross, cross, slot_kv, slot_kv, key_bias, q_seg, k_seg)


def query_back_kernel(
    q_ref, go_ref, stat_ref, k_ref, v_ref, sk_ref, sv_ref, kb_ref, qs_ref, ks_ref,
    dq_ref, dk_ref, dv_ref, dsk_ref, dsv_ref, sum_k, sum_v,
    *, blocks,
):
    pair = pl.program_id(0)
    lane = iota((1, LANES), 1)
    left = lane < 64
    sides = []
    for side in range(2):
        mine = left if side == 0 else ~left
        base = 64 * (1 - side)
        ones = jnp.where((lane >= base) & (lane < base + 3), 1.0, 0.0)
        bias = lane == base + 3
        sides.append(
            (
                jnp.where(mine, k_ref[...].astype(F32), jnp.where(bias, kb_ref[...].astype(F32), ones)).astype(BF),
                jnp.where(mine, v_ref[...].astype(F32), ones).astype(BF),
                jnp.where(mine, sk_ref[...].astype(F32), ones).astype(BF),
                jnp.where(mine, sv_ref[...].astype(F32), ones).astype(BF),
            )
        )
    for number, (at, size, near) in enumerate(blocks):
        q = q_ref[at : at + size, :]
        g = go_ref[at : at + size, :]
        stats = stat_ref[at : at + size, :]
        dq, dk, dv, dsk, dsv = [], [], [], [], []
        for side in range(2):
            mine = left if side == 0 else ~left
            base = 64 * (1 - side)
            head = 2 * pair + side
            plain = jnp.where(lane == base + 3, 1.0, 0.0)
            shifted = jnp.where(mine, q.astype(F32) * SCALE, stat_lanes(stats, head, 0, base) + plain).astype(BF)
            lowered = jnp.where(mine, g.astype(F32), stat_lanes(stats, head, 48, base)).astype(BF)
            keys, values, slot_keys, slot_values = sides[side]
            probs = jnp.exp(dot(keys, shifted, 1, 1))
            dscore = (probs * dot(values, lowered, 1, 1)).astype(BF)
            dk.append(dot(dscore, q))
            dv.append(dot(probs.astype(BF), g))
            moved = dot(dscore, k_ref[...], 0, 0)
            if near:
                scores = jnp.where(ks_ref[...] == qs_ref[...], dot(slot_keys, shifted, 1, 1), MASKED)
                probs = jnp.exp(scores)
                dscore = (probs * dot(slot_values, lowered, 1, 1)).astype(BF)
                dsk.append(dot(dscore, q))
                dsv.append(dot(probs.astype(BF), g))
                moved = moved + dot(dscore, sk_ref[...], 0, 0)
            dq.append(moved)
        dq_ref[at : at + size, :] = (jnp.where(left, dq[0], dq[1]) * SCALE).astype(BF)
        if number == 0:
            sum_k[...] = jnp.where(left, dk[0], dk[1])
            sum_v[...] = jnp.where(left, dv[0], dv[1])
        else:
            sum_k[...] += jnp.where(left, dk[0], dk[1])
            sum_v[...] += jnp.where(left, dv[0], dv[1])
        if near:
            dsk_ref[...] = (jnp.where(left, dsk[0], dsk[1]) * SCALE).astype(BF)
            dsv_ref[...] = jnp.where(left, dsv[0], dsv[1]).astype(BF)
    dk_ref[...] = (sum_k[...] * SCALE).astype(BF)
    dv_ref[...] = sum_v[...].astype(BF)


def query_backward(q, go, stats, cross, slot_kv, key_bias, q_seg, k_seg, blocks):
    total, width = q.shape
    patches, slots = cross.shape[0], slot_kv.shape[0]
    pairs = HEADS // 2
    col = lambda rows, first: pl.BlockSpec((rows, LANES), lambda p: (0, first + p))
    return pl.pallas_call(
        functools.partial(query_back_kernel, blocks=blocks),
        grid=(pairs,),
        in_specs=[
            col(total, 0), col(total, 0), whole(stats.shape), col(patches, 0), col(patches, pairs),
            col(slots, 0), col(slots, pairs), whole(key_bias.shape), whole(q_seg.shape), whole(k_seg.shape),
        ],
        out_specs=[col(total, 0), col(patches, 0), col(patches, 0), col(slots, 0), col(slots, 0)],
        out_shape=[
            sds((total, width), BF),
            sds((patches, width), BF),
            sds((patches, width), BF),
            sds((slots, width), BF),
            sds((slots, width), BF),
        ],
        scratch_shapes=[pltpu.VMEM((patches, LANES), F32), pltpu.VMEM((patches, LANES), F32)],
        compiler_params=params(),
        cost_estimate=cost(40 * total * patches * width, 1.5e7, total * patches * HEADS),
        name="query_backward",
    )(q, go, stats, cross, cross, slot_kv, slot_kv, key_bias, q_seg, k_seg)


def query_ffn_kernel(*refs, parts):
    outs, stats = refs[:parts], refs[parts : 2 * parts]
    x_ref, cot_ref, gain_ref, wo_ref, up_ref, down_ref = refs[2 * parts : 2 * parts + 6]
    (
        out_ref, grad_ref, send_ref, stat_ref, att_ref, normed_ref, act_ref, dact_ref, branch_ref, gain_grad_ref,
        mixed, after, total, back, joint,
    ) = refs[2 * parts + 6 :]
    step = pl.program_id(0)
    width = x_ref.shape[1]

    @pl.when(step == 0)
    def _():
        each = [join_lanes(s[...].astype(F32), 0) for s in stats]
        peak = functools.reduce(jnp.maximum, each)
        weights = [jnp.exp(e - peak) for e in each]
        weight_sum = functools.reduce(jnp.add, weights)
        joint[...] = peak + jnp.log(weight_sum)
        value = None
        for o, w in zip(outs, weights):
            term = o[...].astype(F32) * spread_heads(w / weight_sum, width)
            value = term if value is None else value + term
        mixed[...] = value
        att_ref[...] = value.astype(BF)
        rows = x_ref[...].astype(F32) + dot(att_ref[...], wo_ref[...])
        after[...] = rows
        unit, _ = norm_stats(rows)
        normed_ref[...] = (unit * gain_ref[3:4, :]).astype(BF)
        total[...] = jnp.zeros_like(total)
        back[...] = jnp.zeros_like(back)

    value, slope = gelu_pair(dot(normed_ref[...], up_ref[...]))
    act = value.astype(BF)
    act_ref[...] = act
    total[...] += dot(act, down_ref[...])
    dact = (slope * dot(cot_ref[...], down_ref[...], 1, 1)).astype(BF)
    dact_ref[...] = dact
    back[...] += dot(dact, up_ref[...], 1, 1)

    @pl.when(step == pl.num_programs(0) - 1)
    def _():
        out_ref[...] = (after[...] + total[...]).astype(BF)
        unit, spread = norm_stats(after[...])
        grad, gain_part = norm_back(unit, spread, gain_ref[3:4, :], back[...])
        gain_grad_ref[...] = jnp.broadcast_to(gain_part, gain_grad_ref.shape)
        grad = cot_ref[...].astype(F32) + grad
        grad_ref[...] = grad
        branch = grad.astype(BF)
        branch_ref[...] = branch
        sent = dot(branch, wo_ref[...], 1, 1).astype(BF)
        send_ref[...] = sent
        pick = (iota((width, LANES), 0) // (width // HEADS) == iota((width, LANES), 1)).astype(F32).astype(BF)
        high, middle, low = three_parts(sent.astype(F32) * mixed[...])
        inner = dot(high.astype(BF), pick) + dot(middle.astype(BF), pick) + dot(low.astype(BF), pick)
        lane = iota((1, LANES), 1)
        packed = jnp.zeros(inner.shape, F32)
        for source, first in ((joint[...], 0), (inner, 48)):
            kept = jnp.where(lane < HEADS, source, 0.0)
            for number, piece in enumerate(three_parts(kept)):
                amount = first + 16 * number
                packed = packed + (piece if amount == 0 else pltpu.roll(piece, amount, 1))
        stat_ref[...] = packed.astype(BF)


def query_ffn(outs, stats, x, cot, gains, wo, up, down, chunk=768):
    slots, width = x.shape
    hidden = up.shape[1]
    parts = len(outs)
    rows = lambda kind: sds((slots, width), kind)
    return pl.pallas_call(
        functools.partial(query_ffn_kernel, parts=parts),
        grid=(hidden // chunk,),
        in_specs=[whole(a.shape) for a in (*outs, *stats, x, cot, gains, wo)]
        + [pl.BlockSpec((width, chunk), lambda j: (0, j)), pl.BlockSpec((chunk, width), lambda j: (j, 0))],
        out_specs=[
            whole((slots, width)),
            whole((slots, width)),
            whole((slots, width)),
            whole((slots, LANES)),
            whole((slots, width)),
            whole((slots, width)),
            pl.BlockSpec((slots, chunk), lambda j: (0, j)),
            pl.BlockSpec((slots, chunk), lambda j: (0, j)),
            whole((slots, width)),
            whole((8, width)),
        ],
        out_shape=[
            rows(BF), rows(F32), rows(BF), sds((slots, LANES), BF), rows(BF), rows(BF),
            sds((slots, hidden), BF), sds((slots, hidden), BF), rows(BF), sds((8, width), F32),
        ],
        scratch_shapes=[pltpu.VMEM((slots, width), F32)] * 4 + [pltpu.VMEM((slots, LANES), F32)],
        compiler_params=params(),
        cost_estimate=cost(8 * slots * width * hidden, 2e7, slots * hidden),
        name="query_ffn",
    )(*outs, *stats, x, cot, gains, wo, up, down)


def query_weights_kernel(normed_ref, cot_ref, att_ref, branch_ref, act_ref, dact_ref, up_ref, down_ref, wo_ref):
    up_ref[...] = dot(normed_ref[...], dact_ref[...], 0, 0).astype(BF)
    down_ref[...] = dot(act_ref[...], cot_ref[...], 0, 0).astype(BF)

    @pl.when(pl.program_id(0) == 0)
    def _():
        wo_ref[...] = dot(att_ref[...], branch_ref[...], 0, 0).astype(BF)


def query_weights(normed, cot, att, branch, act, dact, chunk=768):
    slots, width = normed.shape
    hidden = act.shape[1]
    return pl.pallas_call(
        query_weights_kernel,
        grid=(hidden // chunk,),
        in_specs=[whole((slots, width))] * 4 + [pl.BlockSpec((slots, chunk), lambda j: (0, j))] * 2,
        out_specs=[
            pl.BlockSpec((width, chunk), lambda j: (0, j)),
            pl.BlockSpec((chunk, width), lambda j: (j, 0)),
            whole((width, width)),
        ],
        out_shape=[sds((width, hidden), BF), sds((hidden, width), BF), sds((width, width), BF)],
        compiler_params=params(),
        cost_estimate=cost(4 * slots * width * hidden, 1.6e7),
        name="query_weights",
    )(normed, cot, att, branch, act, dact)


def query_out_kernel(*refs, parts):
    dqs = refs[:parts]
    dk_ref, dv_ref, n_ref, x_ref, grad_ref, gain_ref, w_ref = refs[parts : parts + 7]
    out_ref, w_grad_ref, gain_grad_ref = refs[parts + 7 :]
    width = x_ref.shape[1]
    value = dqs[0][...].astype(F32)
    for d in dqs[1:]:
        value = value + d[...].astype(F32)
    back = None
    for number, piece in enumerate((value.astype(BF), dk_ref[...], dv_ref[...])):
        cols = slice(number * width, (number + 1) * width)
        term = dot(piece, w_ref[:, cols], 1, 1)
        back = term if back is None else back + term
        w_grad_ref[:, cols] = dot(n_ref[...], piece, 0, 0).astype(BF)
    unit, spread = norm_stats(x_ref[...].astype(F32))
    grad, gain_part = norm_back(unit, spread, gain_ref[2:3, :], back)
    gain_grad_ref[...] = jnp.broadcast_to(gain_part, gain_grad_ref.shape)
    out_ref[...] = grad_ref[...] + grad


def query_out(dqs, dk, dv, normed, x, grad, gains, w):
    slots, width = x.shape
    return pl.pallas_call(
        functools.partial(query_out_kernel, parts=len(dqs)),
        out_shape=[sds((slots, width), F32), sds(w.shape, BF), sds((8, width), F32)],
        compiler_params=params(),
        cost_estimate=cost(4 * slots * width * w.shape[1], 1e7),
        name="query_out",
    )(*dqs, dk, dv, normed, x, grad, gains, w)


def from_ahead(array, count, distance):
    return lax.ppermute(array, "strip", [(i, (i - distance) % count) for i in range(count)])


def from_partner(array, count):
    return lax.ppermute(array, "strip", [(i, i ^ 1) for i in range(count)])


def scattered(grad):
    strips, pages = lax.axis_size("strip"), lax.axis_size("page")
    rows, cols = grad.shape
    part = lax.psum_scatter(grad, "strip", scatter_dimension=0, tiled=True)
    part = part.reshape(rows // strips, pages, cols // pages).transpose(1, 0, 2)
    return lax.psum_scatter(part, "page", scatter_dimension=0, tiled=False).astype(F32)


def local(
    visual_in, query_in, row_valid, segment_ids, slot_valid, col_shift, row_shifted, norm_gains,
    w_vqkv, w_vout, w_up, w_down, w_qqkv, w_xkv, w_qout, w_qup, w_qdown, visual_cot, query_cot,
):
    pages, strip_rows, columns, width = visual_in.shape
    own_slots, all_slots = query_in.shape[1], segment_ids.shape[1]
    count = lax.axis_size("strip")
    group = count // 2
    half = strip_rows * columns
    slots = 2 * own_slots
    window = WIN * WIN
    part = strip_rows * WIN
    place = lax.axis_index("strip")
    odd = place % 2 == 1
    up = jnp.where(odd, 1 - row_shifted[0], row_shifted[0])
    down = 1 - up
    pick = lambda array, which: lax.dynamic_index_in_dim(array, which, 0, keepdims=False)

    def put(own, other):
        first = jnp.where(up == 0, own, other)
        second = jnp.where(up == 0, other, own)
        return jnp.stack([first, second], axis=0)

    def pair_slots(array):
        mine, theirs = pick(array, up), from_partner(pick(array, down), count)
        return jnp.where(odd, jnp.concatenate([theirs, mine]), jnp.concatenate([mine, theirs]))

    gains = jnp.pad(norm_gains.T, ((0, 4), (0, 0)))
    shift = pick(col_shift, up)
    query_rows = pair_slots(query_in)
    patch_own = pick(visual_in, up).reshape(half, width)
    patch_other = from_ahead(pick(visual_in, down).reshape(half, width), count, 1)
    query_cots = pair_slots(query_cot)
    cot_own = pick(visual_cot, up).reshape(half, width)
    cot_other = from_ahead(pick(visual_cot, down).reshape(half, width), count, 1)
    rows_ok = jnp.concatenate([pick(row_valid, up), from_ahead(pick(row_valid, down), count, 1)])
    slots_ok = pair_slots(slot_valid)

    token = jnp.arange(half, dtype=jnp.int32)
    in_window = token % part
    src = (in_window // WIN) * columns + (token // part * WIN + in_window % WIN + shift) % columns
    turned = (token % columns - shift) % columns
    inv = (turned // WIN) * part + (token // columns) * WIN + turned % WIN
    src, inv = src[:, None], inv[:, None]
    key_bias = jnp.where(jnp.tile(jnp.repeat(rows_ok, WIN), 2 * half // window) == 1, 0.0, MASKED)
    key_bias = jnp.broadcast_to(key_bias.astype(BF)[:, None], (2 * half, LANES))

    order = [-1] + list(range(group - 1))
    near_first, near_length = slots - 32, slots + 64
    segments = pick(segment_ids, up)
    twice = jnp.concatenate([segments, segments, segments])
    base = (place // 2) * slots
    near_ids = lax.dynamic_slice_in_dim(twice, all_slots + base - 32, near_length)
    own_ids = lax.dynamic_slice_in_dim(segments, base, slots)
    own_ids = jnp.where(slots_ok == 1, own_ids, -1)
    blocks = row_blocks(all_slots, near_first, near_length)

    def gather(array):
        return jnp.concatenate(
            [array if k == 0 else from_ahead(array, count, 2 * k) for k in order], axis=0
        )

    def give_back(array):
        pieces = []
        for number, k in enumerate(order):
            piece = array[number * slots : (number + 1) * slots]
            pieces.append(piece if k == 0 else from_ahead(piece, count, -2 * k))
        return pieces

    normed_three, q_own, slot_kv = query_in_call(query_rows, gains, w_qqkv)
    q_all = gather(q_own)
    x, normed_one, qkv, cross = patch_in(src, patch_own, patch_other, gains, w_vqkv, w_xkv)
    att, win_stats = window_forward(qkv, window)
    q_out, q_stats = query_forward(q_all, cross, slot_kv, key_bias, near_ids[:, None], own_ids[None, :], blocks)
    out_parts, stat_parts = give_back(q_out), give_back(q_stats)
    (vis_own, vis_other, grad_after, grad_att, g_vout, g_up, g_down, gain_two) = patch_ffn(
        src, inv, att, x, cot_own, cot_other, gains, w_vout, w_up, w_down
    )
    (q_res, grad_q, send_q, send_stats, att_q, normed_four, act_q, dact_q, branch_q, gain_four) = query_ffn(
        out_parts, stat_parts, query_rows, query_cots, gains, w_qout, w_qup, w_qdown
    )
    go_all, stats_all = gather(send_q), gather(send_stats)
    g_qup, g_qdown, g_qout = query_weights(normed_four, query_cots, att_q, branch_q, act_q, dact_q)
    g_proj = window_backward(qkv, grad_att, win_stats, window)
    dq, dk, dv, dsk, dsv = query_backward(
        q_all, go_all, stats_all, cross, slot_kv, key_bias, near_ids[None, :], own_ids[:, None], blocks
    )
    dq_parts = give_back(dq)
    vin_own, vin_other, g_vqkv, g_xkv, gain_one = patch_back(
        inv, g_proj, dk, dv, normed_one, x, grad_after, gains, w_vqkv, w_xkv
    )
    qin_grad, g_qqkv, gain_three = query_out(dq_parts, dsk, dsv, normed_three, query_rows, grad_q, gains, w_qqkv)

    shape = (pages, strip_rows, columns, width)
    visual_out = put(vis_own, from_ahead(vis_other, count, -1)).reshape(shape)
    visual_in_grad = put(vin_own, from_ahead(vin_other, count, -1).astype(F32)).reshape(shape)

    def return_slots(pair, kind):
        low, high = pair[:own_slots], pair[own_slots:]
        mine = jnp.where(odd, high, low)
        theirs = from_partner(jnp.where(odd, low, high).astype(BF), count)
        return put(mine.astype(kind), theirs.astype(kind))

    query_out_rows = return_slots(q_res, BF)
    query_in_grad = return_slots(qin_grad, F32)

    gain_rows = jnp.stack([gain_one[0], gain_two[0], gain_three[0], gain_four[0]])
    gain_rows = lax.psum_scatter(gain_rows, "page", scatter_dimension=0, tiled=True)
    gain_part = lax.psum_scatter(gain_rows, "strip", scatter_dimension=1, tiled=True).reshape(-1, 1)
    return (
        visual_out, query_out_rows, visual_in_grad, query_in_grad, gain_part,
        scattered(g_vqkv), scattered(g_vout), scattered(g_up), scattered(g_down), scattered(g_qqkv),
        scattered(g_xkv), scattered(g_qout), scattered(g_qup), scattered(g_qdown),
    )


def solution(mesh):
    tokens, slots, table = P("page", "strip", None, None), P("page", "strip", None), P("page", "strip")
    tile = P("strip", "page")
    return jax.shard_map(
        local,
        mesh=mesh,
        in_specs=(tokens, slots, table, P("page", None), table, P("page"), P("page")) + (P(),) * 10 + (tokens, slots),
        out_specs=(tokens, slots, tokens, slots) + (tile,) * 10,
        check_vma=False,
    )
```

time: 2910 us -> 1400 us (0.48)
  blocking collectives: 1300 us -> 10.1 us
  waiting for transfers between devices: 136 us -> 923 us
  local copies, waits for them, and re-layouts: 778 us -> 46.3 us
  matrix products: 403 us -> 0 us
  Pallas kernels: 0 us -> 302 us
  other arithmetic: 231 us -> 32.4 us
  starting transfers between devices: 14.8 us -> 60.9 us
    unnamed x2 -> x1, blocking collectives: 1240 us -> 10.1 us
    reduce_scatter x2 -> x18, waiting for transfers between devices: 0.01 us -> 761 us  [the longest x9 566 us: scattered(): part = lax.psum_scatter(grad, 'strip', scatter_dimension=0, tiled=True)]
    dot_general x38 -> x0, matrix products: 389 us -> none  [the longest x9 68.3 us: outer_sum(): lax.dot_general(flat_left, flat_right, (((0,), (0,)), ((), ())), preferre...]
    pallas_call x0 -> x11, Pallas kernels: none -> 302 us  [the longest x1 69.2 us: patch_ffn(): pl.pallas_call(patch_ffn_kernel, grid=(hidden // chunk,), in_specs=[whole...]
    reshape x24 -> x11, local copies, waits for them, and re-layouts: 189 us -> 14.2 us  [scattered(): part = part.reshape(rows // strips, pages, cols // pages).transpose(1, 0, 2)]
    unnamed x198 -> x51, local copies, waits for them, and re-layouts: 117 us -> 8.95 us
    concatenate x8 -> x3, local copies, waits for them, and re-layouts: 100 us -> 0.3 us  [the longest x1 0.14 us: pair_slots(): jnp.concatenate([theirs, mine])]
    transpose x8 -> x0, local copies, waits for them, and re-layouts: 72.3 us -> none  [the longest x2 23.2 us: pack_grads(): block.transpose(0, 2, 1, 3).reshape(strip_count, page_count, -1)]
  transfers between devices with their start and end apart: 11 -> 47, of which waited for: 4 -> 23; matrix products, arithmetic and copies ran while one was open for 30% -> 5% of each run, Pallas kernels for 0% -> 22%
where the time goes in v1:
time: 1400 us; the launch traced here: 1390 us
  waiting for transfers between devices  923 us (66%)
  Pallas kernels  302 us (22%)
  starting transfers between devices  60.9 us (4%)
  local copies, waits for them, and re-layouts  46.3 us (3%)
  other arithmetic  32.4 us (2%)
  between operations  16.2 us (1%)
    reduce_scatter x9, waiting for transfers between devices, scattered(): part = lax.psum_scatter(grad, 'strip', scatter_dimension=0, tiled=True)  566 us
    reduce_scatter x9, waiting for transfers between devices, scattered(): lax.psum_scatter(part, 'page', scatter_dimension=0, tiled=False).astype(F32)  195 us
    ppermute x23, waiting for transfers between devices, from_ahead(): lax.ppermute(array, 'strip', [(i, (i - distance) % count) for i in range(...  99.3 us
    pallas_call x1, Pallas kernels, patch_ffn(): pl.pallas_call(patch_ffn_kernel, grid=(hidden // chunk,), in_specs=[whole...  69.2 us
    unnamed x20, waiting for transfers between devices  62.6 us
    pallas_call x1, Pallas kernels, query_backward(): pl.pallas_call(functools.partial(query_back_kernel, blocks=blocks), grid=...  58.2 us
    ppermute x23, starting transfers between devices, from_ahead(): lax.ppermute(array, 'strip', [(i, (i - distance) % count) for i in range(...  51.9 us
    pallas_call x1, Pallas kernels, window_backward(): pl.pallas_call(window_back_kernel, grid=(total // tokens,), in_specs=[row...  39.6 us
  transfers between devices with their start and end apart: 47, of which 23 were waited for; matrix products, arithmetic and copies ran while one was open for 5% of the time, Pallas kernels for 22%

profile of v1, /device:TPU:0, one launch (start us, length us, event | category | flops | bytes accessed | tf_op | source)
XLA Modules:
  0.0 1390.6 jit_solution(17452271210368983670)
XLA Ops:
  9.3 3.0 collective-permute-start.8
  13.0 3.5 collective-permute-start.7
  17.7 1.7 dynamic-slice_bitcast_fusion.1
  19.4 2.0 collective-permute-start.15
  21.4 3.6 constant_dynamic-slice_fusion.5
  27.8 2.8 fusion.7
  31.4 4.3 query_in.1
  37.6 3.9 collective-permute-start.5
  43.2 12.8 collective-permute-done.4
  57.1 8.5 collective-permute-done.5
  65.7 14.6 %collective-permute-done.6 = bf16[256,768]{1,0:T(8,128)(2,1)S(1)} collective-permute-done((bf16[256,768]{1,0:T(8,128)(2,1)}, bf16[256,768]{1,0:T(8,128)(2,1)S(1)}, u32[]{:S(2)}, u32[]{:S(2)}) %collective-permute-start.6) | collective-permute-done | bytes 393248 | tf_op jit(solution)/shard_map/ppermute | solution.py:788
  81.6 15.7 %patch_in.1 = (bf16[1152,768]{1,0:T(8,128)(2,1)}, bf16[1152,768]{1,0:T(8,128)(2,1)}, bf16[1152,2304]{1,0:T(8,128)(2,1)}, bf16[1152,1536]{1,0:T(8,128)(2,1)}) custom-call(s32[576,1]{1,0:T(8,128)} %get-tuple-element.142.src_ref, bf16[576,768]{1,0:T(8,128)(2,1)} %bitcast.124, bf16[576,768]{1,0:T(8,128)(2,1)} %collective-permute-done.other_ref, ...), custom_call_target="tpu_custom_call" | custom-call | flops 6794772480 | bytes 20000000 | tf_op jit(solution)/shard_map/patch_in/pallas_call | solution.py:124
  97.3 14.7 %window_forward.1 = (bf16[1152,768]{1,0:T(8,128)(2,1)}, bf16[1152,128]{1,0:T(8,128)(2,1)}) custom-call(bf16[1152,2304]{1,0:T(8,128)(2,1)} %get-tuple-element.59.qkv_ref), custom_call_target="tpu_custom_call" | custom-call | flops 2038431744 | bytes 8000000 | tf_op jit(solution)/shard_map/window_forward/pallas_call | solution.py:175
  112.0 69.2 %patch_ffn.1 = (bf16[576,768]{1,0:T(8,128)(2,1)}, bf16[576,768]{1,0:T(8,128)(2,1)}, f32[1152,768]{1,0:T(8,128)}, bf16[1152,768]{1,0:T(8,128)(2,1)}, bf16[768,768...) custom-call(s32[576,1]{1,0:T(8,128)} %get-tuple-element.142.src_ref, ...), custom_call_target="tpu_custom_call" | custom-call | flops 32614907904 | bytes 40000000 | tf_op jit(solution)/shard_map/patch_ffn/pallas_call | solution.py:314
  182.2 34.9 %query_forward.1 = (bf16[1024,768]{1,0:T(8,128)(2,1)}, bf16[1024,128]{1,0:T(8,128)(2,1)}) custom-call(bf16[1024,768]{1,0:T(8,128)(2,1)} %copy-done.10, bf16[1152,1536]{1,0:T(8,128)(2,1)} %get-tuple-element.65.k_ref.v_ref, bf16[1152,1536]{1,0:T(8,128)(2,1)} %get-tuple-element.65.k_ref.v_ref, bf16[256,1536]{1,0:T(8,128)(2,1)} %get-tuple-element.66.sk_ref.sv_ref, ...), custom_call_target="tpu_custom_call" | custom-call | flops 14495514624 | bytes 10000000 | tf_op jit(solution)/shard_map/query_forward/pallas_call | solution.py:527
  217.1 2.3 fusion.40
  219.4 21.5 %collective-permute-start.10 = (bf16[256,768]{1,0:T(8,128)(2,1)S(1)}, bf16[256,768]{1,0:T(8,128)(2,1)S(1)}, u32[]{:S(2)}, u32[]{:S(2)}) collective-permute-start(bf16[256,768]{1,0:T(8,128)(2,1)S(1)} %get-tuple-element.117), channel_id=1, source_target_pairs={{0,2},{1,3},{2,4},{3,5},{4,6},{5,7},{6,0},{7,1},{8,10},{9,11},{10,... | collective-permute-start | bytes 1179656 | tf_op jit(solution)/shard_map/ppermute | solution.py:788
  244.3 26.4 %collective-permute-done.14.refs_7_ = bf16[256,128]{1,0:T(8,128)(2,1)S(1)} collective-permute-done((bf16[256,128]{1,0:T(8,128)(2,1)S(1)}, bf16[256,128]{1,0:T(8,128)(2,1)S(1)}, u32[]{:S(2)}, u32[]{:S(2)}) %collective-permute-start.14) | collective-permute-done | bytes 65568 | tf_op jit(solution)/shard_map/ppermute | solution.py:788
  270.7 2.0 collective-permute-start.12
  272.7 1.9 maximum_select_fusion.1.refs_9_.cot_ref
  276.3 15.9 %query_ffn.1 = (bf16[256,768]{1,0:T(8,128)(2,1)}, f32[256,768]{1,0:T(8,128)}, bf16[256,768]{1,0:T(8,128)(2,1)}, bf16[256,128]{1,0:T(8,128)(2,1)}, bf16[256,768]{...) custom-call(bf16[256,768]{1,0:T(8,128)(2,1)} %copy-done.16, ...), custom_call_target="tpu_custom_call" | custom-call | flops 4831838208 | bytes 20000000 | tf_op jit(solution)/shard_map/query_ffn/pallas_call | solution.py:700
  293.2 3.4 collective-permute-start.18
  298.6 39.6 %window_backward.1.gp_ref = bf16[1152,2304]{1,0:T(8,128)(2,1)} custom-call(bf16[1152,2304]{1,0:T(8,128)(2,1)} %get-tuple-element.59.qkv_ref, bf16[1152,768]{1,0:T(8,128)(2,1)} %get-tuple-element.70.go_ref, bf16[1152,128]{1,0:T(8,128)(2,1)} %get-tuple-element.71.stat_ref), custom_call_target="tpu_custom_call" | custom-call | flops 5096079360 | bytes 13000000 | tf_op jit(solution)/shard_map/window_backward/pallas_call | solution.py:228
  338.2 2.9 collective-permute-start.21
  341.1 8.7 query_weights.1
  352.1 58.2 %query_backward.1 = (bf16[1024,768]{1,0:T(8,128)(2,1)}, bf16[1152,768]{1,0:T(8,128)(2,1)}, bf16[1152,768]{1,0:T(8,128)(2,1)}, bf16[256,768]{1,0:T(8,128)(2,1)}, bf16[256,768]{1,0:T(8,128)(2,1)}) custom-call(bf16[1024,768]{1,0:T(8,128)(2,1)} %copy-done.10, bf16[1024,768]{1,0:T(8,128)(2,1)} %pad_maximum_fusion.2.go_ref, ...), custom_call_target="tpu_custom_call" | custom-call | flops 36238786560 | bytes 15000000 | tf_op jit(solution)/shard_map/query_backward/pallas_call | solution.py:610
  410.3 32.9 %patch_back.1 = (f32[576,768]{1,0:T(8,128)}, bf16[576,768]{1,0:T(8,128)(2,1)}, bf16[768,2304]{1,0:T(8,128)(2,1)}, bf16[768,1536]{1,0:T(8,128)(2,1)}, f32[8,768]{1,0:T(8,128)}) custom-call(s32[576,1]{1,0:T(8,128)} %get-tuple-element.143.inv_ref, bf16[1152,2304]{1,0:T(8,128)(2,1)} %window_backward.1.gp_ref, bf16[1152,768]{1,0:T(8,128)(2,1)} %get-tuple-element.74.gk_ref, ...), custom_call_target="tpu_custom_call" | custom-call | flops 13589544960 | bytes 40000000 | tf_op jit(solution)/shard_map/patch_back/pallas_call | solution.py:412
  446.6 3.4 collective-permute-start.25
  450.6 36.2 %collective-permute-done.26.refs_3_ = bf16[256,768]{1,0:T(8,128)(2,1)S(1)} collective-permute-done((bf16[256,768]{1,0:T(8,128)(2,1)S(1)}, bf16[256,768]{1,0:T(8,128)(2,1)S(1)}, u32[]{:S(2)}, u32[]{:S(2)}) %collective-permute-start.26) | collective-permute-done | bytes 393248 | tf_op jit(solution)/shard_map/ppermute | solution.py:788
  487.9 7.6 query_out.1
  500.4 10.1 all-reduce.1
  517.5 11.3 reduce-scatter.42.cloned.1.call-done
  528.8 1.7 copy.90
  530.5 80.2 %reduce-scatter.22.cloned.1.call-done = bf16[96,2304]{1,0:T(8,128)(2,1)} async-done(((bf16[768,2304]{1,0:T(8,128)(2,1)}), bf16[96,2304]{1,0:T(8,128)(2,1)}) %reduce-scatter.22.cloned.1.call-update) | async-done | bytes 442384 | tf_op jit(solution)/shard_map/reduce_scatter | solution.py:798
  610.8 1.6 reshape.473
  613.3 79.5 %reduce-scatter.38.cloned.1.call-done = bf16[96,2304]{1,0:T(8,128)(2,1)} async-done(((bf16[768,2304]{1,0:T(8,128)(2,1)}), bf16[96,2304]{1,0:T(8,128)(2,1)}) %reduce-scatter.38.cloned.1.call-update) | async-done | bytes 442384 | tf_op jit(solution)/shard_map/reduce_scatter | solution.py:798
  692.8 1.6 reshape.477
  695.3 95.9 %reduce-scatter.34.cloned.1.call-done = bf16[384,768]{1,0:T(8,128)(2,1)} async-done(((bf16[3072,768]{1,0:T(8,128)(2,1)}), bf16[384,768]{1,0:T(8,128)(2,1)}) %reduce-scatter.34.cloned.1.call-update) | async-done | bytes 589840 | tf_op jit(solution)/shard_map/reduce_scatter | solution.py:798
  791.1 2.1 copy.68
  794.9 1.7 collective-permute-start.16
  796.5 105.2 %reduce-scatter.30.cloned.1.call-done = bf16[96,3072]{1,0:T(8,128)(2,1)} async-done(((bf16[768,3072]{1,0:T(8,128)(2,1)}), bf16[96,3072]{1,0:T(8,128)(2,1)}) %reduce-scatter.30.cloned.1.call-update) | async-done | bytes 589840 | tf_op jit(solution)/shard_map/reduce_scatter | solution.py:798
  901.7 2.0 copy.87
  906.8 1.6 collective-permute-start.27
  911.1 59.4 %reduce-scatter.58.cloned.1.call-done = f32[96,1]{1,0:T(8,128)} async-done(((f32[768,1]{1,0:T(8,128)}), f32[96,1]{1,0:T(8,128)}) %reduce-scatter.58.cloned.1.call-update) | async-done | bytes 400
  971.9 96.6 %reduce-scatter.54.cloned.1.call-done = bf16[384,768]{1,0:T(8,128)(2,1)} async-done(((bf16[3072,768]{1,0:T(8,128)(2,1)}), bf16[384,768]{1,0:T(8,128)(2,1)}) %reduce-scatter.54.cloned.1.call-update) | async-done | bytes 589840 | tf_op jit(solution)/shard_map/reduce_scatter | solution.py:798
  1068.5 2.2 copy.73
  1073.1 2.0 pad_maximum_fusion
  1075.1 15.8 %reduce-scatter.28.cloned.1.call-done = bf16[1,96,192]{2,1,0:T(8,128)(2,1)} async-done(((bf16[4,96,192]{2,1,0:T(8,128)(2,1)}), bf16[1,96,192]{2,1,0:T(8,128)(2,1)}) %reduce-scatter.28.cloned.1.call-update) | async-done | bytes 36880 | tf_op jit(solution)/shard_map/reduce_scatter | solution.py:800
  1092.3 21.3 %reduce-scatter.48.cloned.1.call-done = bf16[1,96,192]{2,1,0:T(8,128)(2,1)} async-done(((bf16[4,96,192]{2,1,0:T(8,128)(2,1)}), bf16[1,96,192]{2,1,0:T(8,128)(2,1)}) %reduce-scatter.48.cloned.1.call-update) | async-done | bytes 36880 | tf_op jit(solution)/shard_map/reduce_scatter | solution.py:800
  1115.1 97.4 %reduce-scatter.50.cloned.1.call-done = bf16[96,3072]{1,0:T(8,128)(2,1)} async-done(((bf16[768,3072]{1,0:T(8,128)(2,1)}), bf16[96,3072]{1,0:T(8,128)(2,1)}) %reduce-scatter.50.cloned.1.call-update) | async-done | bytes 589840 | tf_op jit(solution)/shard_map/reduce_scatter | solution.py:798
  1212.4 1.9 copy.86
  1214.4 21.2 %reduce-scatter.44.cloned.1.call-done = bf16[1,96,384]{2,1,0:T(8,128)(2,1)} async-done(((bf16[4,96,384]{2,1,0:T(8,128)(2,1)}), bf16[1,96,384]{2,1,0:T(8,128)(2,1)}) %reduce-scatter.44.cloned.1.call-update) | async-done | bytes 73744 | tf_op jit(solution)/shard_map/reduce_scatter | solution.py:800
  1237.1 22.4 %reduce-scatter.24.cloned.1.call-done = bf16[1,96,576]{2,1,0:T(8,128)(2,1)} async-done(((bf16[4,96,576]{2,1,0:T(8,128)(2,1)}), bf16[1,96,576]{2,1,0:T(8,128)(2,1)}) %reduce-scatter.24.cloned.1.call-update) | async-done | bytes 110608 | tf_op jit(solution)/shard_map/reduce_scatter | solution.py:800
  1259.5 1.6 bitcast_convert_fusion.5
  1261.1 22.4 %reduce-scatter.40.cloned.1.call-done = bf16[1,96,576]{2,1,0:T(8,128)(2,1)} async-done(((bf16[4,96,576]{2,1,0:T(8,128)(2,1)}), bf16[1,96,576]{2,1,0:T(8,128)(2,1)}) %reduce-scatter.40.cloned.1.call-update) | async-done | bytes 110608 | tf_op jit(solution)/shard_map/reduce_scatter | solution.py:800
  1283.5 1.6 bitcast_convert_fusion.4
  1285.1 23.0 %reduce-scatter.36.cloned.1.call-done = bf16[1,384,192]{1,2,0:T(8,128)(2,1)} async-done(((bf16[4,384,192]{1,2,0:T(8,128)(2,1)}), bf16[1,384,192]{1,2,0:T(8,128)(2,1)}) %reduce-scatter.36.cloned.1.call-update) | async-done | bytes 147472 | tf_op jit(solution)/shard_map/reduce_scatter | solution.py:800
  1308.1 1.6 bitcast_convert_fusion.2
  1309.7 22.9 %reduce-scatter.32.cloned.1.call-done = bf16[1,96,768]{2,1,0:T(8,128)(2,1)} async-done(((bf16[4,96,768]{2,1,0:T(8,128)(2,1)}), bf16[1,96,768]{2,1,0:T(8,128)(2,1)}) %reduce-scatter.32.cloned.1.call-update) | async-done | bytes 147472 | tf_op jit(solution)/shard_map/reduce_scatter | solution.py:800
  1332.7 1.6 bitcast_convert_fusion.3
  1334.3 23.0 %reduce-scatter.56.cloned.1.call-done = bf16[1,384,192]{1,2,0:T(8,128)(2,1)} async-done(((bf16[4,384,192]{1,2,0:T(8,128)(2,1)}), bf16[1,384,192]{1,2,0:T(8,128)(2,1)}) %reduce-scatter.56.cloned.1.call-update) | async-done | bytes 147472 | tf_op jit(solution)/shard_map/reduce_scatter | solution.py:800
  1357.3 1.6 bitcast_convert_fusion
  1358.9 23.1 %reduce-scatter.52.cloned.1.call-done = bf16[1,96,768]{2,1,0:T(8,128)(2,1)} async-done(((bf16[4,96,768]{2,1,0:T(8,128)(2,1)}), bf16[1,96,768]{2,1,0:T(8,128)(2,1)}) %reduce-scatter.52.cloned.1.call-update) | async-done | bytes 147472 | tf_op jit(solution)/shard_map/reduce_scatter | solution.py:800
  1382.0 1.6 bitcast_convert_fusion.1
  (181 shorter events, 57.4 us)
Async XLA Ops:
  7.2 505.8 %reduce-scatter.26.cloned.1.call-start = ((), (), s32[]{:S(2)}) async-start(), calls=%async_computation.21 | async-start | bytes 1327104 | tf_op jit(solution)/shard_map/reduce_scatter | solution.py:798
  9.3 32.2 %collective-permute-start.8 = (s32[128]{0:T(128)S(1)}, s32[128]{0:T(128)S(1)}, u32[]{:S(2)}, u32[]{:S(2)}) collective-permute-start(s32[128]{0:T(128)S(1)} %get-tuple-element.136), channel_id=1, source_target_pairs={{0,1},{1,0},{2,3},{3,2},{4,5},{5,4},{6,7},{7,6},{8,9},{9,8},{10,11... | collective-permute-start | bytes 1544 | tf_op jit(solution)/shard_map/ppermute | solution.py:792
  13.0 24.2 %collective-permute-start.7 = (s32[6]{0:T(128)S(1)}, s32[6]{0:T(128)S(1)}, u32[]{:S(2)}, u32[]{:S(2)}) collective-permute-start(s32[6]{0:T(128)S(1)} %get-tuple-element.139), channel_id=1, source_target_pairs={{0,7},{1,0},{2,1},{3,2},{4,3},{5,4},{6,5},{7,6},{8,15},{9,8},{10,9... | collective-permute-start | bytes 80 | tf_op jit(solution)/shard_map/ppermute | solution.py:788
  17.6 13.0 collective-permute-start.3
  19.4 7.1 copy-start.20
  19.4 7.7 copy-start.13
  19.4 7.7 copy-start.12
  19.4 224.3 %collective-permute-start.15 = (bf16[128,768]{1,0:T(8,128)(2,1)}, bf16[128,768]{1,0:T(8,128)(2,1)}, u32[]{:S(2)}, u32[]{:S(2)}) collective-permute-start(bf16[128,768]{1,0:T(8,128)(2,1)} %get-tuple-element.124), channel_id=1, source_target_pairs={{0,1},{1,0},{2,3},{3,2},{4,5},{5,4},{6,7},{7,6},{8,9},{9,8},{10,11... | collective-permute-start | bytes 589832 | tf_op jit(solution)/shard_map/ppermute | solution.py:792
  25.1 55.3 %collective-permute-start = (bf16[576,768]{1,0:T(8,128)(2,1)S(1)}, bf16[576,768]{1,0:T(8,128)(2,1)}, u32[]{:S(2)}, u32[]{:S(2)}) collective-permute-start(bf16[576,768]{1,0:T(8,128)(2,1)S(1)} %bitcast.125), channel_id=1, source_target_pairs={{0,7},{1,0},{2,1},{3,2},{4,3},{5,4},{6,5},{7,6},{8,15},{9,8},{10,9... | collective-permute-start | bytes 2654216 | tf_op jit(solution)/shard_map/ppermute | solution.py:788
  35.8 20.3 %collective-permute-start.4 = (bf16[256,768]{1,0:T(8,128)(2,1)}, bf16[256,768]{1,0:T(8,128)(2,1)S(1)}, u32[]{:S(2)}, u32[]{:S(2)}) collective-permute-start(bf16[256,768]{1,0:T(8,128)(2,1)} %get-tuple-element.64), channel_id=1, source_target_pairs={{0,2},{1,3},{2,4},{3,5},{4,6},{5,7},{6,0},{7,1},{8,10},{9,11},{10,... | collective-permute-start | bytes 1179656 | tf_op jit(solution)/shard_map/ppermute | solution.py:788
  37.6 28.1 %collective-permute-start.5 = (bf16[256,768]{1,0:T(8,128)(2,1)}, bf16[256,768]{1,0:T(8,128)(2,1)S(1)}, u32[]{:S(2)}, u32[]{:S(2)}) collective-permute-start(bf16[256,768]{1,0:T(8,128)(2,1)} %get-tuple-element.64), channel_id=1, source_target_pairs={{0,6},{1,7},{2,0},{3,1},{4,2},{5,3},{6,4},{7,5},{8,14},{9,15},{10,... | collective-permute-start | bytes 1179656 | tf_op jit(solution)/shard_map/ppermute | solution.py:788
  41.5 38.9 %collective-permute-start.6 = (bf16[256,768]{1,0:T(8,128)(2,1)}, bf16[256,768]{1,0:T(8,128)(2,1)S(1)}, u32[]{:S(2)}, u32[]{:S(2)}) collective-permute-start(bf16[256,768]{1,0:T(8,128)(2,1)} %get-tuple-element.64), channel_id=1, source_target_pairs={{0,4},{1,5},{2,6},{3,7},{4,0},{5,1},{6,2},{7,3},{8,12},{9,13},{10,... | collective-permute-start | bytes 1179656 | tf_op jit(solution)/shard_map/ppermute | solution.py:788
  56.1 55.9 %collective-permute-start.1 = (bf16[576,768]{1,0:T(8,128)(2,1)S(1)}, bf16[576,768]{1,0:T(8,128)(2,1)}, u32[]{:S(2)}, u32[]{:S(2)}) collective-permute-start(bf16[576,768]{1,0:T(8,128)(2,1)S(1)} %bitcast.123), channel_id=1, source_target_pairs={{0,7},{1,0},{2,1},{3,2},{4,3},{5,4},{6,5},{7,6},{8,15},{9,8},{10,9... | collective-permute-start | bytes 2654216 | tf_op jit(solution)/shard_map/ppermute | solution.py:788
  80.4 1.2 copy-start.10
  181.2 333.7 %reduce-scatter.46.cloned.1.call-start = ((), (), s32[]{:S(2)}) async-start(), calls=%async_computation.31 | async-start | bytes 1327104 | tf_op jit(solution)/shard_map/reduce_scatter | solution.py:798
  217.1 23.8 %copy-start.9 = (bf16[1024,128]{1,0:T(8,128)(2,1)S(1)}, bf16[1024,128]{1,0:T(8,128)(2,1)}, u32[]{:S(2)}) copy-start(bf16[1024,128]{1,0:T(8,128)(2,1)} %get-tuple-element.68) | copy-start | bytes 786436
  219.4 55.9 %collective-permute-start.11 = (bf16[256,768]{1,0:T(8,128)(2,1)S(1)}, bf16[256,768]{1,0:T(8,128)(2,1)S(1)}, u32[]{:S(2)}, u32[]{:S(2)}) collective-permute-start(bf16[256,768]{1,0:T(8,128)(2,1)S(1)} %get-tuple-element.116), channel_id=1, source_target_pairs={{0,4},{1,5},{2,6},{3,7},{4,0},{5,1},{6,2},{7,3},{8,12},{9,13},{10,... | collective-permute-start | bytes 1179656 | tf_op jit(solution)/shard_map/ppermute | solution.py:788
  219.4 55.9 %collective-permute-start.10 = (bf16[256,768]{1,0:T(8,128)(2,1)S(1)}, bf16[256,768]{1,0:T(8,128)(2,1)S(1)}, u32[]{:S(2)}, u32[]{:S(2)}) collective-permute-start(bf16[256,768]{1,0:T(8,128)(2,1)S(1)} %get-tuple-element.117), channel_id=1, source_target_pairs={{0,2},{1,3},{2,4},{3,5},{4,6},{5,7},{6,0},{7,1},{8,10},{9,11},{10,... | collective-permute-start | bytes 1179656 | tf_op jit(solution)/shard_map/ppermute | solution.py:788
  240.9 34.4 %collective-permute-start.9 = (bf16[256,768]{1,0:T(8,128)(2,1)S(1)}, bf16[256,768]{1,0:T(8,128)(2,1)S(1)}, u32[]{:S(2)}, u32[]{:S(2)}) collective-permute-start(bf16[256,768]{1,0:T(8,128)(2,1)S(1)} %get-tuple-element.119), channel_id=1, source_target_pairs={{0,6},{1,7},{2,0},{3,1},{4,2},{5,3},{6,4},{7,5},{8,14},{9,15},{10,... | collective-permute-start | bytes 1179656 | tf_op jit(solution)/shard_map/ppermute | solution.py:788
  241.6 29.1 %collective-permute-start.14 = (bf16[256,128]{1,0:T(8,128)(2,1)S(1)}, bf16[256,128]{1,0:T(8,128)(2,1)S(1)}, u32[]{:S(2)}, u32[]{:S(2)}) collective-permute-start(bf16[256,128]{1,0:T(8,128)(2,1)S(1)} %get-tuple-element.128), channel_id=1, source_target_pairs={{0,4},{1,5},{2,6},{3,7},{4,0},{5,1},{6,2},{7,3},{8,12},{9,13},{10,... | collective-permute-start | bytes 196616 | tf_op jit(solution)/shard_map/ppermute | solution.py:788
  243.7 30.9 %collective-permute-start.13 = (bf16[256,128]{1,0:T(8,128)(2,1)S(1)}, bf16[256,128]{1,0:T(8,128)(2,1)S(1)}, u32[]{:S(2)}, u32[]{:S(2)}) collective-permute-start(bf16[256,128]{1,0:T(8,128)(2,1)S(1)} %get-tuple-element.129), channel_id=1, source_target_pairs={{0,2},{1,3},{2,4},{3,5},{4,6},{5,7},{6,0},{7,1},{8,10},{9,11},{10,... | collective-permute-start | bytes 196616 | tf_op jit(solution)/shard_map/ppermute | solution.py:788
  270.7 4.6 copy-start.17
  270.7 4.5 collective-permute-start.12
  275.3 0.9 copy-start.15
  275.3 1.0 copy-start.16
  292.2 58.5 %collective-permute-start.19 = (bf16[256,768]{1,0:T(8,128)(2,1)}, bf16[256,768]{1,0:T(8,128)(2,1)S(1)}, u32[]{:S(2)}, u32[]{:S(2)}) collective-permute-start(bf16[256,768]{1,0:T(8,128)(2,1)} %get-tuple-element.72), channel_id=1, source_target_pairs={{0,4},{1,5},{2,6},{3,7},{4,0},{5,1},{6,2},{7,3},{8,12},{9,13},{10,... | collective-permute-start | bytes 1179656 | tf_op jit(solution)/shard_map/ppermute | solution.py:788
  293.2 57.4 %collective-permute-start.18 = (bf16[256,768]{1,0:T(8,128)(2,1)}, bf16[256,768]{1,0:T(8,128)(2,1)S(1)}, u32[]{:S(2)}, u32[]{:S(2)}) collective-permute-start(bf16[256,768]{1,0:T(8,128)(2,1)} %get-tuple-element.72), channel_id=1, source_target_pairs={{0,6},{1,7},{2,0},{3,1},{4,2},{5,3},{6,4},{7,5},{8,14},{9,15},{10,... | collective-permute-start | bytes 1179656 | tf_op jit(solution)/shard_map/ppermute | solution.py:788
  296.6 54.1 %collective-permute-start.17 = (bf16[256,768]{1,0:T(8,128)(2,1)}, bf16[256,768]{1,0:T(8,128)(2,1)S(1)}, u32[]{:S(2)}, u32[]{:S(2)}) collective-permute-start(bf16[256,768]{1,0:T(8,128)(2,1)} %get-tuple-element.72), channel_id=1, source_target_pairs={{0,2},{1,3},{2,4},{3,5},{4,6},{5,7},{6,0},{7,1},{8,10},{9,11},{10,... | collective-permute-start | bytes 1179656 | tf_op jit(solution)/shard_map/ppermute | solution.py:788
  297.1 44.0 %collective-permute-start.22 = (bf16[256,128]{1,0:T(8,128)(2,1)}, bf16[256,128]{1,0:T(8,128)(2,1)S(1)}, u32[]{:S(2)}, u32[]{:S(2)}) collective-permute-start(bf16[256,128]{1,0:T(8,128)(2,1)} %get-tuple-element.73), channel_id=1, source_target_pairs={{0,4},{1,5},{2,6},{3,7},{4,0},{5,1},{6,2},{7,3},{8,12},{9,13},{10,... | collective-permute-start | bytes 196616 | tf_op jit(solution)/shard_map/ppermute | solution.py:788
  298.6 39.6 %copy-start.11 = (bf16[256,128]{1,0:T(8,128)(2,1)S(1)}, bf16[256,128]{1,0:T(8,128)(2,1)}, u32[]{:S(2)}) copy-start(bf16[256,128]{1,0:T(8,128)(2,1)} %get-tuple-element.73) | copy-start | bytes 196612
  338.2 11.7 collective-permute-start.21
  341.1 8.8 collective-permute-start.20
  349.8 1.0 copy-start.8
  349.9 178.9 %reduce-scatter.42.cloned.1.call-start = ((), (), s32[]{:S(2)}) async-start(), calls=%async_computation.29 | async-start | bytes 2654208 | tf_op jit(solution)/shard_map/reduce_scatter | solution.py:798
  443.3 167.5 %reduce-scatter.22.cloned.1.call-start = ((), (), s32[]{:S(2)}) async-start(), calls=%async_computation.19 | async-start | bytes 3981312 | tf_op jit(solution)/shard_map/reduce_scatter | solution.py:798
  443.3 1.4 copy-start.2
  443.9 248.9 %reduce-scatter.38.cloned.1.call-start = ((), (), s32[]{:S(2)}) async-start(), calls=%async_computation.27 | async-start | bytes 3981312 | tf_op jit(solution)/shard_map/reduce_scatter | solution.py:798
  445.6 41.2 %collective-permute-start.26 = (bf16[256,768]{1,0:T(8,128)(2,1)S(1)}, bf16[256,768]{1,0:T(8,128)(2,1)S(1)}, u32[]{:S(2)}, u32[]{:S(2)}) collective-permute-start(bf16[256,768]{1,0:T(8,128)(2,1)S(1)} %get-tuple-element.112), channel_id=1, source_target_pairs={{0,4},{1,5},{2,6},{3,7},{4,0},{5,1},{6,2},{7,3},{8,12},{9,13},{10,... | collective-permute-start | bytes 1179656 | tf_op jit(solution)/shard_map/ppermute | solution.py:788
  446.6 40.3 %collective-permute-start.25 = (bf16[256,768]{1,0:T(8,128)(2,1)S(1)}, bf16[256,768]{1,0:T(8,128)(2,1)S(1)}, u32[]{:S(2)}, u32[]{:S(2)}) collective-permute-start(bf16[256,768]{1,0:T(8,128)(2,1)S(1)} %get-tuple-element.113), channel_id=1, source_target_pairs={{0,2},{1,3},{2,4},{3,5},{4,6},{5,7},{6,0},{7,1},{8,10},{9,11},{10,... | collective-permute-start | bytes 1179656 | tf_op jit(solution)/shard_map/ppermute | solution.py:788
  449.9 36.9 %collective-permute-start.24 = (bf16[256,768]{1,0:T(8,128)(2,1)S(1)}, bf16[256,768]{1,0:T(8,128)(2,1)S(1)}, u32[]{:S(2)}, u32[]{:S(2)}) collective-permute-start(bf16[256,768]{1,0:T(8,128)(2,1)S(1)} %get-tuple-element.115), channel_id=1, source_target_pairs={{0,6},{1,7},{2,0},{3,1},{4,2},{5,3},{6,4},{7,5},{8,14},{9,15},{10,... | collective-permute-start | bytes 1179656 | tf_op jit(solution)/shard_map/ppermute | solution.py:788
  486.8 0.9 copy-start.6
  486.8 1.0 copy-start.7
  495.5 295.6 %reduce-scatter.34.cloned.1.call-start = ((), (), s32[]{:S(2)}) async-start(), calls=%async_computation.25 | async-start | bytes 5308416 | tf_op jit(solution)/shard_map/reduce_scatter | solution.py:798
  496.1 405.6 %reduce-scatter.30.cloned.1.call-start = ((), (), s32[]{:S(2)}) async-start(), calls=%async_computation.23 | async-start | bytes 5308416 | tf_op jit(solution)/shard_map/reduce_scatter | solution.py:798
  496.8 473.7 %reduce-scatter.58.cloned.1.call-start = ((), (), s32[]{:S(2)}) async-start(), calls=%async_computation.37 | async-start | bytes 442368
  512.2 556.3 %reduce-scatter.54.cloned.1.call-start = ((), (), s32[]{:S(2)}) async-start(), calls=%async_computation.35 | async-start | bytes 5308416 | tf_op jit(solution)/shard_map/reduce_scatter | solution.py:798
  513.0 577.9 %reduce-scatter.28.cloned.1.call-start = ((), (), s32[]{:S(2)}) async-start(), calls=%async_computation.22 | async-start | bytes 245760 | tf_op jit(solution)/shard_map/reduce_scatter | solution.py:800
  514.9 598.7 %reduce-scatter.48.cloned.1.call-start = ((), (), s32[]{:S(2)}) async-start(), calls=%async_computation.32 | async-start | bytes 245760 | tf_op jit(solution)/shard_map/reduce_scatter | solution.py:800
  516.8 695.6 %reduce-scatter.50.cloned.1.call-start = ((), (), s32[]{:S(2)}) async-start(), calls=%async_computation.33 | async-start | bytes 5308416 | tf_op jit(solution)/shard_map/reduce_scatter | solution.py:798
  517.4 718.1 %reduce-scatter.44.cloned.1.call-start = ((), (), s32[]{:S(2)}) async-start(), calls=%async_computation.30 | async-start | bytes 368640 | tf_op jit(solution)/shard_map/reduce_scatter | solution.py:800
  530.5 729.0 %reduce-scatter.24.cloned.1.call-start = ((), (), s32[]{:S(2)}) async-start(), calls=%async_computation.20 | async-start | bytes 614400 | tf_op jit(solution)/shard_map/reduce_scatter | solution.py:800
  613.2 670.2 %reduce-scatter.40.cloned.1.call-start = ((), (), s32[]{:S(2)}) async-start(), calls=%async_computation.28 | async-start | bytes 614400 | tf_op jit(solution)/shard_map/reduce_scatter | solution.py:800
  694.3 100.5 %copy-start.3 = (bf16[256,768]{1,0:T(8,128)(2,1)S(1)}, bf16[256,768]{1,0:T(8,128)(2,1)}, u32[]{:S(2)}) copy-start(bf16[256,768]{1,0:T(8,128)(2,1)} %get-tuple-element.69) | copy-start | bytes 1179652
  695.2 612.9 %reduce-scatter.36.cloned.1.call-start = ((), (), s32[]{:S(2)}) async-start(), calls=%async_computation.26 | async-start | bytes 737280 | tf_op jit(solution)/shard_map/reduce_scatter | solution.py:800
  793.2 539.4 %reduce-scatter.32.cloned.1.call-start = ((), (), s32[]{:S(2)}) async-start(), calls=%async_computation.24 | async-start | bytes 737280 | tf_op jit(solution)/shard_map/reduce_scatter | solution.py:800
  793.3 115.1 %collective-permute-start.2 = (bf16[576,768]{1,0:T(8,128)(2,1)}, bf16[576,768]{1,0:T(8,128)(2,1)}, u32[]{:S(2)}, u32[]{:S(2)}) collective-permute-start(bf16[576,768]{1,0:T(8,128)(2,1)} %get-tuple-element.63), channel_id=1, source_target_pairs={{0,1},{1,2},{2,3},{3,4},{4,5},{5,6},{6,7},{7,0},{8,9},{9,10},{10,1... | collective-permute-start | bytes 2654216 | tf_op jit(solution)/shard_map/ppermute | solution.py:788
  794.9 108.9 %collective-permute-start.16 = (bf16[128,768]{1,0:T(8,128)(2,1)S(1)}, bf16[128,768]{1,0:T(8,128)(2,1)S(1)}, u32[]{:S(2)}, u32[]{:S(2)}) collective-permute-start(bf16[128,768]{1,0:T(8,128)(2,1)S(1)} %broadcast_select_fusion.2), channel_id=1, source_target_pairs={{0,1},{1,0},{2,3},{3,2},{4,5},{5,4},{6,7},{7,6},{8,9},{9,8},{10,11... | collective-permute-start | bytes 589832 | tf_op jit(solution)/shard_map/ppermute | solution.py:792
  901.7 4.5 copy-start.1
  903.7 4.7 copy-start.4
  903.7 453.5 %reduce-scatter.56.cloned.1.call-start = ((), (), s32[]{:S(2)}) async-start(), calls=%async_computation.36 | async-start | bytes 737280 | tf_op jit(solution)/shard_map/reduce_scatter | solution.py:800
  904.6 168.2 %collective-permute-start.23 = (bf16[576,768]{1,0:T(8,128)(2,1)}, bf16[576,768]{1,0:T(8,128)(2,1)S(1)}, u32[]{:S(2)}, u32[]{:S(2)}) collective-permute-start(bf16[576,768]{1,0:T(8,128)(2,1)} %get-tuple-element.79), channel_id=1, source_target_pairs={{0,1},{1,2},{2,3},{3,4},{4,5},{5,6},{6,7},{7,0},{8,9},{9,10},{10,1... | collective-permute-start | bytes 2654216 | tf_op jit(solution)/shard_map/ppermute | solution.py:788
  906.8 163.9 %collective-permute-start.27 = (bf16[128,768]{1,0:T(8,128)(2,1)}, bf16[128,768]{1,0:T(8,128)(2,1)}, u32[]{:S(2)}, u32[]{:S(2)}) collective-permute-start(bf16[128,768]{1,0:T(8,128)(2,1)} %select_convert_fusion), channel_id=1, source_target_pairs={{0,1},{1,0},{2,3},{3,2},{4,5},{5,4},{6,7},{7,6},{8,9},{9,8},{10,11... | collective-permute-start | bytes 589832 | tf_op jit(solution)/shard_map/ppermute | solution.py:792
  1070.7 2.1 copy-start
  1070.7 311.3 %reduce-scatter.52.cloned.1.call-start = ((), (), s32[]{:S(2)}) async-start(), calls=%async_computation.34 | async-start | bytes 737280 | tf_op jit(solution)/shard_map/reduce_scatter | solution.py:800
  (5 other events, 3.6 us)
Sparse Core Ops, SparseCore 0:
  181.4 101.0 reduce-scatter.25
  350.0 64.6 reduce-scatter.45
  443.4 85.3 reduce-scatter.41
  532.8 77.9 reduce-scatter.21
  614.3 78.4 reduce-scatter.37
  696.3 94.8 reduce-scatter.33
  794.7 106.8 reduce-scatter.29
  904.9 65.5 reduce-scatter.57
  974.2 94.2 reduce-scatter.53
  1071.4 19.4 reduce-scatter.27
  1093.9 19.7 reduce-scatter.47
  1117.1 95.2 reduce-scatter.49
  1215.5 20.0 reduce-scatter.43
  1238.1 21.3 reduce-scatter.23
  1262.0 21.3 reduce-scatter.39
  1286.0 22.0 reduce-scatter.35
  1310.6 22.0 reduce-scatter.31
  1335.2 22.0 reduce-scatter.55
  1359.9 22.0 reduce-scatter.51

commit v2 on v1

--- a/solution.py
+++ b/solution.py
@@ -97,6 +97,68 @@
 
 def sds(shape, kind):
     return jax.ShapeDtypeStruct(shape, kind)
+
+
+def tile_index(strip, half, order):
+    y = strip % 2
+    lead = (y, half) if order == 0 else (half, y)
+    return lead + ((strip // 2 % 2) * 2 + strip // 4,)
+
+
+def tile_shape(rows, cols):
+    return (2, 2, 2, 4, cols // 256 * (rows // 16), LANES)
+
+
+def store_all(ref, value, order):
+    rows, cols = value.shape
+    size, tiles = rows // 16, cols // 256
+    for strip in range(8):
+        for core in range(2):
+            at = (2 * strip + core) * size
+            for half in range(2):
+                lead = tile_index(strip, half, order)
+                for t in range(tiles):
+                    lanes = (half * tiles + t) * LANES
+                    ref[(core, *lead, slice(t * size, (t + 1) * size), slice(None))] = value[at : at + size, lanes : lanes + LANES]
+
+
+def store_columns(ref, value, order):
+    size = value.shape[0] // 16
+    for strip in range(8):
+        for core in range(2):
+            at = (2 * strip + core) * size
+            lead = list(tile_index(strip, 0, order))
+            for t in range(value.shape[1] // LANES):
+                ref[(core, *lead, slice(t * size, (t + 1) * size), slice(None))] = value[at : at + size, t * LANES : (t + 1) * LANES]
+
+
+def store_strip(ref, value, order):
+    size, tiles = value.shape[0] // 2, value.shape[1] // 256
+    for core in range(2):
+        for half in range(2):
+            lead = (0, half) if order == 0 else (half, 0)
+            for t in range(tiles):
+                lanes = (half * tiles + t) * LANES
+                ref[(core, *lead, 0, slice(t * size, (t + 1) * size), slice(None))] = value[
+                    core * size : (core + 1) * size, lanes : lanes + LANES
+                ]
+
+
+def columns_spec(rows, chunk, per_half, order, at):
+    block = (2, 2, 1, 4) if order == 0 else (2, 1, 2, 4)
+    lead = lambda half: (0, 0, half, 0) if order == 0 else (0, half, 0, 0)
+    return pl.BlockSpec(
+        (*block, chunk // LANES * (rows // 16), LANES), lambda j: (*lead(at(j) // per_half), at(j) % per_half, 0)
+    )
+
+
+def strip_spec(rows, cols, order):
+    block = (2, 1, 2, 1) if order == 0 else (2, 2, 1, 1)
+    lead = lambda y: (0, y, 0) if order == 0 else (0, 0, y)
+    return pl.BlockSpec(
+        (*block, cols // 256 * (rows // 16), LANES),
+        lambda j: (*lead(j % 2), (j // 2 % 2) * 2 + j // 4, 0, 0),
+    )
 
 
 def patch_in_kernel(src_ref, own_ref, other_ref, gain_ref, wq_ref, wx_ref, x_ref, n_ref, qkv_ref, cross_ref):
@@ -249,6 +311,7 @@
     src_ref, inv_ref, att_ref, x_ref, own_ref, other_ref, gain_ref, wo_ref, up_ref, down_ref,
     out_own_ref, out_other_ref, after_grad_ref, att_grad_ref, wo_grad_ref, up_grad_ref, down_grad_ref, gain_grad_ref,
     after, normed, cot, total, back, acts, dacts,
+    *, tiled,
 ):
     step = pl.program_id(0)
     tokens, width = att_ref.shape
@@ -283,8 +346,14 @@
         dact = (slope * dot(cot[rows, :], down_ref[...], 1, 1)).astype(BF)
         dacts[rows, :] = dact
         back[rows, :] += dot(dact, up_ref[...], 1, 1)
-    up_grad_ref[...] = dot(normed[...], dacts[...], 0, 0).astype(BF)
-    down_grad_ref[...] = dot(acts[...], cot[...], 0, 0).astype(BF)
+    up_grad = dot(normed[...], dacts[...], 0, 0).astype(BF)
+    down_grad = dot(acts[...], cot[...], 0, 0).astype(BF)
+    if tiled:
+        store_columns(up_grad_ref, up_grad, 0)
+        store_strip(down_grad_ref, down_grad, 1)
+    else:
+        up_grad_ref[...] = up_grad
+        down_grad_ref[...] = down_grad
 
     @pl.when(step == pl.num_programs(0) - 1)
     def _():
@@ -300,19 +369,38 @@
             normed[rows, :] = branch
             att_grad_ref[rows, :] = dot(branch, wo_ref[...], 1, 1).astype(BF)
         gain_grad_ref[...] = jnp.broadcast_to(gain_sum, gain_grad_ref.shape)
-        wo_grad_ref[...] = dot(att_ref[...], normed[...], 0, 0).astype(BF)
+        wo_grad = dot(att_ref[...], normed[...], 0, 0).astype(BF)
+        if tiled:
+            store_all(wo_grad_ref, wo_grad, 0)
+        else:
+            wo_grad_ref[...] = wo_grad
         halves = split_halves(after[...] + total[...], part)
         onehot = (iota((half, half), 1) == inv_ref[...]).astype(F32).astype(BF)
         out_own_ref[...] = dot(onehot, halves[0].astype(BF)).astype(BF)
         out_other_ref[...] = dot(onehot, halves[1].astype(BF)).astype(BF)
 
 
-def patch_ffn(src, inv, att, x, own, other, gains, wo, up, down, chunk=384):
+def grad_forms(width, hidden, chunk, tiled, wo_order, up_order, down_order):
+    if not tiled:
+        return (
+            [whole((width, width)), pl.BlockSpec((width, chunk), lambda j: (0, j)), pl.BlockSpec((chunk, width), lambda j: (j, 0))],
+            [sds((width, width), BF), sds((width, hidden), BF), sds((hidden, width), BF)],
+        )
+    shapes = [tile_shape(width, width), tile_shape(width, hidden), tile_shape(hidden, width)]
+    per_half = hidden // 2 // chunk
+    return (
+        [whole(shapes[0]), columns_spec(width, chunk, per_half, up_order, lambda j: j), strip_spec(hidden, width, down_order)],
+        [sds(shape, BF) for shape in shapes],
+    )
+
+
+def patch_ffn(src, inv, att, x, own, other, gains, wo, up, down, tiled, chunk=384):
     tokens, width = att.shape
     half = tokens // 2
     hidden = up.shape[1]
-    return pl.pallas_call(
-        patch_ffn_kernel,
+    grad_specs, grad_shapes = grad_forms(width, hidden, chunk, tiled, 0, 0, 1)
+    return pl.pallas_call(
+        functools.partial(patch_ffn_kernel, tiled=tiled),
         grid=(hidden // chunk,),
         in_specs=[whole(a.shape) for a in (src, inv, att, x, own, other, gains, wo)]
         + [pl.BlockSpec((width, chunk), lambda j: (0, j)), pl.BlockSpec((chunk, width), lambda j: (j, 0))],
@@ -321,9 +409,7 @@
             whole((half, width)),
             whole((tokens, width)),
             whole((tokens, width)),
-            whole((width, width)),
-            pl.BlockSpec((width, chunk), lambda j: (0, j)),
-            pl.BlockSpec((chunk, width), lambda j: (j, 0)),
+            *grad_specs,
             whole((8, width)),
         ],
         out_shape=[
@@ -331,9 +417,7 @@
             sds((half, width), BF),
             sds((tokens, width), F32),
             sds((tokens, width), BF),
-            sds((width, width), BF),
-            sds((width, hidden), BF),
-            sds((hidden, width), BF),
+            *grad_shapes,
             sds((8, width), F32),
         ],
         scratch_shapes=[
@@ -351,36 +435,74 @@
     )(src, inv, att, x, own, other, gains, wo, up, down)
 
 
-def patch_back_kernel(
-    inv_ref, gp_ref, gk_ref, gv_ref, n_ref, x_ref, after_ref, gain_ref, wq_ref, wx_ref,
-    own_ref, other_ref, wq_grad_ref, wx_grad_ref, gain_grad_ref, back,
-    *, q_steps, k_steps,
+def qkv_back_kernel(gp_ref, n_ref, w_ref, back_ref, w_grad_ref, *, tiled):
+    @pl.when(pl.program_id(0) == 0)
+    def _():
+        back_ref[...] = jnp.zeros_like(back_ref)
+
+    back_ref[...] += dot(gp_ref[...], w_ref[...], 1, 1)
+    w_grad = dot(n_ref[...], gp_ref[...], 0, 0).astype(BF)
+    if tiled:
+        store_columns(w_grad_ref, w_grad, 0)
+    else:
+        w_grad_ref[...] = w_grad
+
+
+def qkv_back(gp, normed, w, tiled, chunk=384):
+    tokens, width = normed.shape
+    cols = w.shape[1]
+    natural = pl.BlockSpec((width, chunk), lambda j: (0, j))
+    grad_spec = columns_spec(width, chunk, cols // 2 // chunk, 0, lambda j: j) if tiled else natural
+    return pl.pallas_call(
+        functools.partial(qkv_back_kernel, tiled=tiled),
+        grid=(cols // chunk,),
+        in_specs=[pl.BlockSpec((tokens, chunk), lambda j: (0, j)), whole(normed.shape), natural],
+        out_specs=[whole((tokens, width)), grad_spec],
+        out_shape=[sds((tokens, width), F32), sds(tile_shape(width, cols) if tiled else w.shape, BF)],
+        compiler_params=params(),
+        cost_estimate=cost(4 * tokens * width * cols, 2e7),
+        name="qkv_back",
+    )(gp, normed, w)
+
+
+def cross_back_kernel(
+    inv_ref, gk_ref, gv_ref, n_ref, x_ref, after_ref, part_ref, gain_ref, wx_ref, g2_ref, g4_ref,
+    own_ref, other_ref, gain_grad_ref, *rest,
+    tiled,
 ):
     step = pl.program_id(0)
     half, width = own_ref.shape
     tokens = 2 * half
     part = 72
     block = 4 * part
+    back = rest[-1]
 
     @pl.when(step == 0)
     def _():
-        back[...] = jnp.zeros_like(back)
-
-    def one(grad_ref, weight_ref, out_ref):
-        back[...] += dot(grad_ref[...], weight_ref[...], 1, 1)
-        out_ref[...] = dot(n_ref[...], grad_ref[...], 0, 0).astype(BF)
-
-    @pl.when(step < q_steps)
+        back[...] = part_ref[...]
+
+    def one(grad_ref):
+        back[...] += dot(grad_ref[...], wx_ref[...], 1, 1)
+        w_grad = dot(n_ref[...], grad_ref[...], 0, 0).astype(BF)
+        if not tiled:
+            rest[0][...] = w_grad
+            return
+
+        @pl.when(step % 2 == 0)
+        def _():
+            store_columns(rest[0], w_grad, 0)
+
+        @pl.when(step % 2 == 1)
+        def _():
+            store_columns(rest[1], w_grad, 1)
+
+    @pl.when(step < 2)
     def _():
-        one(gp_ref, wq_ref, wq_grad_ref)
-
-    @pl.when((step >= q_steps) & (step < q_steps + k_steps))
+        one(gk_ref)
+
+    @pl.when(step >= 2)
     def _():
-        one(gk_ref, wx_ref, wx_grad_ref)
-
-    @pl.when(step >= q_steps + k_steps)
-    def _():
-        one(gv_ref, wx_ref, wx_grad_ref)
+        one(gv_ref)
 
     @pl.when(step == pl.num_programs(0) - 1)
     def _():
@@ -391,7 +513,8 @@
             grad, gain_part = norm_back(unit, spread, gain_ref[0:1, :], back[rows, :])
             gain_sum = gain_sum + gain_part
             back[rows, :] = after_ref[rows, :] + grad
-        gain_grad_ref[...] = jnp.broadcast_to(gain_sum, gain_grad_ref.shape)
+        row = iota((8, width), 0)
+        gain_grad_ref[...] = jnp.where(row == 0, gain_sum, jnp.where(row == 1, g2_ref[...], jnp.where(row == 3, g4_ref[...], 0.0)))
         halves = split_halves(back[...], part)
         onehot = (iota((half, half), 1) == inv_ref[...]).astype(F32).astype(BF)
         high = halves[0].astype(BF)
@@ -400,49 +523,37 @@
         other_ref[...] = dot(onehot, halves[1].astype(BF)).astype(BF)
 
 
-def patch_back(inv, gp, gk, gv, normed, x, after, gains, wq, wx, chunk=384):
+def cross_back(inv, gk, gv, normed, x, after, part, gains, wx, g2, g4, tiled):
     tokens, width = x.shape
     half = tokens // 2
-    q_steps, k_steps = wq.shape[1] // chunk, width // chunk
-    steps = q_steps + 2 * k_steps
-    at_q = lambda j: jnp.minimum(j, q_steps - 1)
-    at_x = lambda j: jnp.maximum(j - q_steps, 0)
-    at_k = lambda j: jnp.clip(j - q_steps, 0, k_steps - 1)
-    at_v = lambda j: jnp.clip(j - q_steps - k_steps, 0, k_steps - 1)
-    return pl.pallas_call(
-        functools.partial(patch_back_kernel, q_steps=q_steps, k_steps=k_steps),
-        grid=(steps,),
+    chunk = width // 2
+    cols = wx.shape[1]
+    if tiled:
+        shape = tile_shape(width, cols // 2)
+        grad_specs = [columns_spec(width, chunk, 1, order, lambda j: j // 2) for order in (0, 1)]
+        grad_shapes = [sds(shape, BF)] * 2
+    else:
+        grad_specs = [pl.BlockSpec((width, chunk), lambda j: (0, j))]
+        grad_shapes = [sds(wx.shape, BF)]
+    return pl.pallas_call(
+        functools.partial(cross_back_kernel, tiled=tiled),
+        grid=(4,),
         in_specs=[
             whole(inv.shape),
-            pl.BlockSpec((tokens, chunk), lambda j: (0, at_q(j))),
-            pl.BlockSpec((tokens, chunk), lambda j: (0, at_k(j))),
-            pl.BlockSpec((tokens, chunk), lambda j: (0, at_v(j))),
-            whole(normed.shape),
-            whole(x.shape),
-            whole(after.shape),
-            whole(gains.shape),
-            pl.BlockSpec((width, chunk), lambda j: (0, at_q(j))),
-            pl.BlockSpec((width, chunk), lambda j: (0, at_x(j))),
-        ],
-        out_specs=[
-            whole((half, width)),
-            whole((half, width)),
-            pl.BlockSpec((width, chunk), lambda j: (0, at_q(j))),
-            pl.BlockSpec((width, chunk), lambda j: (0, at_x(j))),
-            whole((8, width)),
-        ],
-        out_shape=[
-            sds((half, width), F32),
-            sds((half, width), BF),
-            sds(wq.shape, BF),
-            sds(wx.shape, BF),
-            sds((8, width), F32),
-        ],
+            pl.BlockSpec((tokens, chunk), lambda j: (0, jnp.minimum(j, 1))),
+            pl.BlockSpec((tokens, chunk), lambda j: (0, jnp.maximum(j - 2, 0))),
+            *[whole(a.shape) for a in (normed, x, after, part, gains)],
+            pl.BlockSpec((width, chunk), lambda j: (0, j)),
+            whole(g2.shape),
+            whole(g4.shape),
+        ],
+        out_specs=[whole((half, width)), whole((half, width)), whole((8, width)), *grad_specs],
+        out_shape=[sds((half, width), F32), sds((half, width), BF), sds((8, width), F32), *grad_shapes],
         scratch_shapes=[pltpu.VMEM((tokens, width), F32)],
         compiler_params=params(),
-        cost_estimate=cost(4 * tokens * width * (wq.shape[1] + wx.shape[1]), 4e7),
-        name="patch_back",
-    )(inv, gp, gk, gv, normed, x, after, gains, wq, wx)
+        cost_estimate=cost(4 * tokens * width * cols, 2e7),
+        name="cross_back",
+    )(inv, gk, gv, normed, x, after, part, gains, wx, g2, g4)
 
 
 def query_in_kernel(x_ref, gain_ref, w_ref, n_ref, q_ref, kv_ref):
@@ -478,15 +589,25 @@
     return blocks
 
 
-def query_forward_kernel(q_ref, k_ref, v_ref, sk_ref, sv_ref, kb_ref, qs_ref, ks_ref, out_ref, stat_ref, held, *, blocks):
+def query_forward_kernel(q_ref, k_ref, v_ref, sk_ref, sv_ref, kb_ref, qs_ref, ks_ref, out_ref, held, *, blocks):
     pair = pl.program_id(0)
-    lane = iota((1, LANES), 1)
-    left = lane < 64
 
     @pl.when(pair == 0)
     def _():
         held[...] = jnp.zeros_like(held)
 
+    @pl.when(pair < HEADS // 2)
+    def _():
+        query_forward_pair(pair, q_ref, k_ref, v_ref, sk_ref, sv_ref, kb_ref, qs_ref, ks_ref, out_ref, held, blocks)
+
+    @pl.when(pair == HEADS // 2)
+    def _():
+        out_ref[...] = held[...].astype(BF)
+
+
+def query_forward_pair(pair, q_ref, k_ref, v_ref, sk_ref, sv_ref, kb_ref, qs_ref, ks_ref, out_ref, held, blocks):
+    lane = iota((1, LANES), 1)
+    left = lane < 64
     keys = []
     for side in range(2):
         keys.append(jnp.where(lane == 64 * (1 - side), kb_ref[...], k_ref[...]))
@@ -514,25 +635,21 @@
         out_ref[at : at + size, :] = jnp.where(left, mixed[0], mixed[1]).astype(BF)
         held[at : at + size, :] += columns
 
-    @pl.when(pair == pl.num_programs(0) - 1)
-    def _():
-        stat_ref[...] = held[...].astype(BF)
-
 
 def query_forward(q, cross, slot_kv, key_bias, q_seg, k_seg, blocks):
     total, width = q.shape
     patches, slots = cross.shape[0], slot_kv.shape[0]
     pairs = HEADS // 2
-    col = lambda rows, first: pl.BlockSpec((rows, LANES), lambda p: (0, first + p))
+    col = lambda rows, first: pl.BlockSpec((rows, LANES), lambda p: (0, first + jnp.minimum(p, pairs - 1)))
     return pl.pallas_call(
         functools.partial(query_forward_kernel, blocks=blocks),
-        grid=(pairs,),
+        grid=(pairs + 1,),
         in_specs=[
             col(total, 0), col(patches, 0), col(patches, pairs), col(slots, 0), col(slots, pairs),
             whole(key_bias.shape), whole(q_seg.shape), whole(k_seg.shape),
         ],
-        out_specs=[col(total, 0), whole((total, LANES))],
-        out_shape=[sds((total, width), BF), sds((total, LANES), BF)],
+        out_specs=pl.BlockSpec((total, LANES), lambda p: (0, p)),
+        out_shape=sds((total, width + LANES), BF),
         scratch_shapes=[pltpu.VMEM((total, LANES), F32)],
         compiler_params=params(),
         cost_estimate=cost(16 * total * patches * width, 1e7, total * patches * HEADS),
@@ -602,7 +719,7 @@
     dv_ref[...] = sum_v[...].astype(BF)
 
 
-def query_backward(q, go, stats, cross, slot_kv, key_bias, q_seg, k_seg, blocks):
+def query_backward(q, go, cross, slot_kv, key_bias, q_seg, k_seg, blocks):
     total, width = q.shape
     patches, slots = cross.shape[0], slot_kv.shape[0]
     pairs = HEADS // 2
@@ -611,7 +728,7 @@
         functools.partial(query_back_kernel, blocks=blocks),
         grid=(pairs,),
         in_specs=[
-            col(total, 0), col(total, 0), whole(stats.shape), col(patches, 0), col(patches, pairs),
+            col(total, 0), col(total, 0), pl.BlockSpec((total, LANES), lambda p: (0, pairs)), col(patches, 0), col(patches, pairs),
             col(slots, 0), col(slots, pairs), whole(key_bias.shape), whole(q_seg.shape), whole(k_seg.shape),
         ],
         out_specs=[col(total, 0), col(patches, 0), col(patches, 0), col(slots, 0), col(slots, 0)],
@@ -626,29 +743,29 @@
         compiler_params=params(),
         cost_estimate=cost(40 * total * patches * width, 1.5e7, total * patches * HEADS),
         name="query_backward",
-    )(q, go, stats, cross, cross, slot_kv, slot_kv, key_bias, q_seg, k_seg)
+    )(q, go, go, cross, cross, slot_kv, slot_kv, key_bias, q_seg, k_seg)
 
 
 def query_ffn_kernel(*refs, parts):
-    outs, stats = refs[:parts], refs[parts : 2 * parts]
-    x_ref, cot_ref, gain_ref, wo_ref, up_ref, down_ref = refs[2 * parts : 2 * parts + 6]
+    outs = refs[:parts]
+    x_ref, cot_ref, gain_ref, wo_ref, up_ref, down_ref = refs[parts : parts + 6]
     (
-        out_ref, grad_ref, send_ref, stat_ref, att_ref, normed_ref, act_ref, dact_ref, branch_ref, gain_grad_ref,
+        out_ref, grad_ref, send_ref, att_ref, normed_ref, act_ref, dact_ref, branch_ref, gain_grad_ref,
         mixed, after, total, back, joint,
-    ) = refs[2 * parts + 6 :]
+    ) = refs[parts + 6 :]
     step = pl.program_id(0)
     width = x_ref.shape[1]
 
     @pl.when(step == 0)
     def _():
-        each = [join_lanes(s[...].astype(F32), 0) for s in stats]
+        each = [join_lanes(o[:, width:].astype(F32), 0) for o in outs]
         peak = functools.reduce(jnp.maximum, each)
         weights = [jnp.exp(e - peak) for e in each]
         weight_sum = functools.reduce(jnp.add, weights)
         joint[...] = peak + jnp.log(weight_sum)
         value = None
         for o, w in zip(outs, weights):
-            term = o[...].astype(F32) * spread_heads(w / weight_sum, width)
+            term = o[:, :width].astype(F32) * spread_heads(w / weight_sum, width)
             value = term if value is None else value + term
         mixed[...] = value
         att_ref[...] = value.astype(BF)
@@ -678,7 +795,7 @@
         branch = grad.astype(BF)
         branch_ref[...] = branch
         sent = dot(branch, wo_ref[...], 1, 1).astype(BF)
-        send_ref[...] = sent
+        send_ref[:, :width] = sent
         pick = (iota((width, LANES), 0) // (width // HEADS) == iota((width, LANES), 1)).astype(F32).astype(BF)
         high, middle, low = three_parts(sent.astype(F32) * mixed[...])
         inner = dot(high.astype(BF), pick) + dot(middle.astype(BF), pick) + dot(low.astype(BF), pick)
@@ -689,10 +806,10 @@
             for number, piece in enumerate(three_parts(kept)):
                 amount = first + 16 * number
                 packed = packed + (piece if amount == 0 else pltpu.roll(piece, amount, 1))
-        stat_ref[...] = packed.astype(BF)
-
-
-def query_ffn(outs, stats, x, cot, gains, wo, up, down, chunk=768):
+        send_ref[:, width:] = packed.astype(BF)
+
+
+def query_ffn(outs, x, cot, gains, wo, up, down, chunk=768):
     slots, width = x.shape
     hidden = up.shape[1]
     parts = len(outs)
@@ -700,13 +817,12 @@
     return pl.pallas_call(
         functools.partial(query_ffn_kernel, parts=parts),
         grid=(hidden // chunk,),
-        in_specs=[whole(a.shape) for a in (*outs, *stats, x, cot, gains, wo)]
+        in_specs=[whole(a.shape) for a in (*outs, x, cot, gains, wo)]
         + [pl.BlockSpec((width, chunk), lambda j: (0, j)), pl.BlockSpec((chunk, width), lambda j: (j, 0))],
         out_specs=[
             whole((slots, width)),
             whole((slots, width)),
-            whole((slots, width)),
-            whole((slots, LANES)),
+            whole((slots, width + LANES)),
             whole((slots, width)),
             whole((slots, width)),
             pl.BlockSpec((slots, chunk), lambda j: (0, j)),
@@ -715,48 +831,55 @@
             whole((8, width)),
         ],
         out_shape=[
-            rows(BF), rows(F32), rows(BF), sds((slots, LANES), BF), rows(BF), rows(BF),
+            rows(BF), rows(F32), sds((slots, width + LANES), BF), rows(BF), rows(BF),
             sds((slots, hidden), BF), sds((slots, hidden), BF), rows(BF), sds((8, width), F32),
         ],
         scratch_shapes=[pltpu.VMEM((slots, width), F32)] * 4 + [pltpu.VMEM((slots, LANES), F32)],
         compiler_params=params(),
         cost_estimate=cost(8 * slots * width * hidden, 2e7, slots * hidden),
         name="query_ffn",
-    )(*outs, *stats, x, cot, gains, wo, up, down)
-
-
-def query_weights_kernel(normed_ref, cot_ref, att_ref, branch_ref, act_ref, dact_ref, up_ref, down_ref, wo_ref):
-    up_ref[...] = dot(normed_ref[...], dact_ref[...], 0, 0).astype(BF)
-    down_ref[...] = dot(act_ref[...], cot_ref[...], 0, 0).astype(BF)
+    )(*outs, x, cot, gains, wo, up, down)
+
+
+def query_weights_kernel(normed_ref, cot_ref, att_ref, branch_ref, act_ref, dact_ref, wo_ref, up_ref, down_ref, *, tiled):
+    up_grad = dot(normed_ref[...], dact_ref[...], 0, 0).astype(BF)
+    down_grad = dot(act_ref[...], cot_ref[...], 0, 0).astype(BF)
+    if tiled:
+        store_columns(up_ref, up_grad, 0)
+        store_strip(down_ref, down_grad, 1)
+    else:
+        up_ref[...] = up_grad
+        down_ref[...] = down_grad
 
     @pl.when(pl.program_id(0) == 0)
     def _():
-        wo_ref[...] = dot(att_ref[...], branch_ref[...], 0, 0).astype(BF)
-
-
-def query_weights(normed, cot, att, branch, act, dact, chunk=768):
+        wo_grad = dot(att_ref[...], branch_ref[...], 0, 0).astype(BF)
+        if tiled:
+            store_all(wo_ref, wo_grad, 1)
+        else:
+            wo_ref[...] = wo_grad
+
+
+def query_weights(normed, cot, att, branch, act, dact, tiled, chunk=384):
     slots, width = normed.shape
     hidden = act.shape[1]
-    return pl.pallas_call(
-        query_weights_kernel,
+    grad_specs, grad_shapes = grad_forms(width, hidden, chunk, tiled, 1, 0, 1)
+    return pl.pallas_call(
+        functools.partial(query_weights_kernel, tiled=tiled),
         grid=(hidden // chunk,),
         in_specs=[whole((slots, width))] * 4 + [pl.BlockSpec((slots, chunk), lambda j: (0, j))] * 2,
-        out_specs=[
-            pl.BlockSpec((width, chunk), lambda j: (0, j)),
-            pl.BlockSpec((chunk, width), lambda j: (j, 0)),
-            whole((width, width)),
-        ],
-        out_shape=[sds((width, hidden), BF), sds((hidden, width), BF), sds((width, width), BF)],
+        out_specs=grad_specs,
+        out_shape=grad_shapes,
         compiler_params=params(),
         cost_estimate=cost(4 * slots * width * hidden, 1.6e7),
         name="query_weights",
     )(normed, cot, att, branch, act, dact)
 
 
-def query_out_kernel(*refs, parts):
+def query_out_kernel(*refs, parts, tiled):
     dqs = refs[:parts]
-    dk_ref, dv_ref, n_ref, x_ref, grad_ref, gain_ref, w_ref = refs[parts : parts + 7]
-    out_ref, w_grad_ref, gain_grad_ref = refs[parts + 7 :]
+    dk_ref, dv_ref, n_ref, x_ref, grad_ref, gain_ref, w_ref, rows_ref = refs[parts : parts + 8]
+    out_ref, w_grad_ref, gain_grad_ref = refs[parts + 8 : parts + 11]
     width = x_ref.shape[1]
     value = dqs[0][...].astype(F32)
     for d in dqs[1:]:
@@ -766,22 +889,309 @@
         cols = slice(number * width, (number + 1) * width)
         term = dot(piece, w_ref[:, cols], 1, 1)
         back = term if back is None else back + term
-        w_grad_ref[:, cols] = dot(n_ref[...], piece, 0, 0).astype(BF)
+        (refs[-1] if tiled else w_grad_ref)[:, cols] = dot(n_ref[...], piece, 0, 0).astype(BF)
+    if tiled:
+        store_all(w_grad_ref, refs[-1][...], 1)
     unit, spread = norm_stats(x_ref[...].astype(F32))
     grad, gain_part = norm_back(unit, spread, gain_ref[2:3, :], back)
-    gain_grad_ref[...] = jnp.broadcast_to(gain_part, gain_grad_ref.shape)
     out_ref[...] = grad_ref[...] + grad
-
-
-def query_out(dqs, dk, dv, normed, x, grad, gains, w):
+    gain_rows = rows_ref[...] + jnp.where(iota((8, width), 0) == 2, gain_part, 0.0)
+    if not tiled:
+        gain_grad_ref[...] = gain_rows
+        return
+    turned = gain_rows.T
+    size = width // 16
+    lane = iota((1, LANES), 1)
+    for half in range(2):
+        tile = jnp.where(lane == 0, turned[:, 2 * half : 2 * half + 1], 0.0)
+        tile = jnp.where(lane == 1, turned[:, 2 * half + 1 : 2 * half + 2], tile).astype(BF)
+        for strip in range(8):
+            for core in range(2):
+                at = (2 * strip + core) * size
+                gain_grad_ref[(core, *tile_index(strip, half, 0), slice(None), slice(None))] = tile[at : at + size]
+
+
+def query_out(dqs, dk, dv, normed, x, grad, gains, w, gain_rows, tiled):
     slots, width = x.shape
     return pl.pallas_call(
-        functools.partial(query_out_kernel, parts=len(dqs)),
-        out_shape=[sds((slots, width), F32), sds(w.shape, BF), sds((8, width), F32)],
+        functools.partial(query_out_kernel, parts=len(dqs), tiled=tiled),
+        out_shape=[
+            sds((slots, width), F32),
+            sds(tile_shape(width, w.shape[1]) if tiled else w.shape, BF),
+            sds(tile_shape(width, 256), BF) if tiled else sds((8, width), F32),
+        ],
+        scratch_shapes=[pltpu.VMEM(w.shape, BF)] if tiled else [],
         compiler_params=params(),
         cost_estimate=cost(4 * slots * width * w.shape[1], 1e7),
         name="query_out",
-    )(*dqs, dk, dv, normed, x, grad, gains, w)
+    )(*dqs, dk, dv, normed, x, grad, gains, w, gain_rows)
+
+
+PAIR = pl.DeviceIdType.MESH
+
+
+def coordinates():
+    page, strip = lax.axis_index("page"), lax.axis_index("strip")
+    core, x = lax.rem(page, 2), page // 2
+    y, z_low, z_high = lax.rem(strip, 2), lax.rem(strip // 2, 2), strip // 4
+    flip = lambda index, bit, weight: index + weight - 2 * weight * bit
+    core_mate = (flip(page, core, 1), strip)
+    mates = {
+        "x": (x, (flip(page, x, 2), strip)),
+        "y": (y, (page, flip(strip, y, 1))),
+        "low": (z_low, (page, flip(strip, z_low, 2))),
+        "high": (z_high, (page, flip(strip, z_high, 4))),
+    }
+    return core, core_mate, [[mates[k] for k in ("y", "x", "low", "high")], [mates[k] for k in ("x", "y", "low", "high")]]
+
+
+def meet(mates):
+    barrier = pltpu.get_barrier_semaphore()
+    for mate in mates:
+        pl.semaphore_signal(barrier, inc=1, device_id=mate, device_id_type=PAIR)
+    pl.semaphore_wait(barrier, len(mates))
+
+
+def send(source, target, sems, number, mate):
+    copy = pltpu.make_async_remote_copy(
+        src_ref=source,
+        dst_ref=target,
+        send_sem=sems.at[0, number],
+        recv_sem=sems.at[1, number],
+        device_id=mate,
+        device_id_type=PAIR,
+    )
+    copy.start()
+    return copy
+
+
+def add_into(target, first, source, start, length):
+    def step(i, carry):
+        target[first + i] = (target[first + i].astype(F32) + source[start + i].astype(F32)).astype(BF)
+        return carry
+
+    lax.fori_loop(0, length, step, 0)
+
+
+def spans(arrays):
+    at, found = 0, []
+    for array in arrays:
+        found.append((at, array.shape[2]))
+        at += array.shape[2]
+    return found
+
+
+def core_sum_kernel(*refs, counts, sizes):
+    total = sum(counts)
+    grads = [refs[: counts[0]], refs[counts[0] : total]]
+    outs = refs[total : total + 4]
+    held, remote, near = refs[total + 4 : total + 6], refs[total + 6], refs[total + 7]
+    core, core_mate, orders = coordinates()
+    meet([core_mate])
+    jobs, number = [], 0
+    for order in range(2):
+        bit = orders[order][0][0]
+        for grad, (at, rows) in zip(grads[order], sizes[order]):
+            target = held[order].at[:, pl.ds(at, rows), :]
+            far = send(grad.at[1 - core], target, remote, number, core_mate)
+            mine = []
+            for which, out in enumerate((outs[2 * order], outs[2 * order + 1])):
+                first = 8 * (bit if which else 1 - bit)
+                copy = pltpu.make_async_copy(
+                    grad.at[core, pl.ds(first, 8)], out.at[:, pl.ds(at, rows), :], near.at[2 * number + which]
+                )
+                copy.start()
+                mine.append((copy, out, first))
+            jobs.append((far, mine, order, at, rows))
+            number += 1
+    for far, mine, order, at, rows in jobs:
+        far.wait()
+        for copy, out, first in mine:
+            copy.wait()
+
+            def step(i, carry, out=out, first=first, order=order, at=at, rows=rows):
+                span = pl.ds(at, rows)
+                out[i, span, :] = (out[i, span, :].astype(F32) + held[order][first + i, span, :].astype(F32)).astype(BF)
+                return carry
+
+            lax.fori_loop(0, 8, step, 0)
+
+
+def core_sum(grads, collective):
+    grads = [[g.reshape(2, 16, *g.shape[-2:]) for g in group] for group in grads]
+    sizes = [spans(group) for group in grads]
+    rows = [sum(r for _, r in group) for group in sizes]
+    counts = [len(group) for group in grads]
+    total = sum(counts)
+    return pl.pallas_call(
+        functools.partial(core_sum_kernel, counts=counts, sizes=sizes),
+        in_specs=[pl.BlockSpec(memory_space=pl.ANY)] * total,
+        out_specs=[pl.BlockSpec(memory_space=pltpu.VMEM)] * 4,
+        out_shape=[sds((8, rows[order], LANES), BF) for order in (0, 0, 1, 1)],
+        scratch_shapes=[
+            pltpu.VMEM((16, rows[0], LANES), BF),
+            pltpu.VMEM((16, rows[1], LANES), BF),
+            pltpu.SemaphoreType.DMA((2, total)),
+            pltpu.SemaphoreType.DMA((2 * total,)),
+        ],
+        compiler_params=pltpu.CompilerParams(collective_id=collective, has_side_effects=True, vmem_limit_bytes=VMEM_BYTES),
+        name="core_sum",
+    )(*grads[0], *grads[1])
+
+
+def halved_sum(pairs):
+    page, strip = lax.axis_index("page"), lax.axis_index("strip")
+    bits = {"x": page // 2, "y": strip % 2, "low": strip // 2 % 2, "high": strip // 4}
+    weights = {"x": ("page", 2), "y": ("strip", 1), "low": ("strip", 2), "high": ("strip", 4)}
+    results = []
+    for (out, keep), order in zip(pairs, (("y", "x", "low", "high"), ("x", "y", "low", "high"))):
+        for number, name in enumerate(order):
+            axis, weight = weights[name]
+            got = lax.ppermute(out, axis, [(i, i ^ weight) for i in range(lax.axis_size(axis))])
+            if number == 3:
+                results.append((keep + got)[0])
+                break
+            size = keep.shape[0] // 2
+            bit = bits[order[number + 1]]
+            cut = lambda array, which: lax.dynamic_slice_in_dim(array, which * size, size)
+            out, keep = cut(keep, 1 - bit) + cut(got, 1 - bit), cut(keep, bit) + cut(got, bit)
+    return results
+
+
+def late_sum_kernel(*refs, counts, sizes, early_rows):
+    total = sum(counts)
+    grads = [refs[: counts[0]], refs[counts[0] : total]]
+    early = refs[total : total + 2]
+    own, got = refs[total + 2 : total + 4], refs[total + 4 : total + 6]
+    sums, first_held = refs[total + 6 : total + 8], refs[total + 8 : total + 10]
+    held = [refs[total + 10 : total + 14], refs[total + 14 : total + 18]]
+    done, remote, near = refs[total + 18 : total + 20], refs[total + 20], refs[total + 21]
+    core, core_mate, orders = coordinates()
+    meet([core_mate] + [mate for _, mate in orders[0]])
+    jobs, number = [], 0
+    for order in range(2):
+        for grad, (at, rows) in zip(grads[order], sizes[order]):
+            span = pl.ds(at, rows)
+            far = send(grad.at[1 - core], first_held[order].at[:, span, :], remote, number, core_mate)
+            copy = pltpu.make_async_copy(grad.at[core], sums[order].at[:, span, :], near.at[number])
+            copy.start()
+            jobs.append((far, copy))
+            number += 1
+    loads = []
+    for order in range(2):
+        copy = pltpu.make_async_copy(early[order], own[order].at[pl.ds(0, early_rows), :], near.at[total + order])
+        copy.start()
+        loads.append(copy)
+    for far, copy in jobs:
+        far.wait()
+        copy.wait()
+    bases = [0, 0]
+    flights = []
+    for order in range(2):
+        bit, mate = orders[order][0]
+        out = 8 * (1 - bit)
+        add_into(sums[order], out, first_held[order], out, 8)
+        flights.append(send(sums[order].at[pl.ds(out, 8)], held[order][0], remote, number, mate))
+        number += 1
+    for order in range(2):
+        bases[order] = 8 * orders[order][0][0]
+        add_into(sums[order], bases[order], first_held[order], bases[order], 8)
+    for stage in range(1, 5):
+        size = 8 >> stage
+        for order in range(2):
+            flights[order].wait()
+            base = bases[order]
+            if stage == 4:
+                value = sums[order][base].astype(F32) + held[order][3][0].astype(F32)
+                own[order][early_rows:, :] = value.astype(BF)
+                continue
+            bit, mate = orders[order][stage]
+            out, keep = size * (1 - bit), size * bit
+            add_into(sums[order], base + out, held[order][stage - 1], out, size)
+            flights[order] = send(sums[order].at[pl.ds(base + out, size)], held[order][stage], remote, number, mate)
+            number += 1
+            add_into(sums[order], base + keep, held[order][stage - 1], keep, size)
+            bases[order] = base + keep
+    for copy in loads:
+        copy.wait()
+    flights = []
+    for order in range(2):
+        flights.append(send(own[order], done[order], remote, number, core_mate))
+        number += 1
+    for order in range(2):
+        flights[order].wait()
+        got[order][...] = done[order][...]
+
+
+def late_sum(grads, early, collective):
+    grads = [[g.reshape(2, 16, *g.shape[-2:]) for g in group] for group in grads]
+    sizes = [spans(group) for group in grads]
+    rows = [sum(r for _, r in group) for group in sizes]
+    counts = [len(group) for group in grads]
+    total = sum(counts)
+    early_rows = early[0].shape[0]
+    share = [sds((early_rows + r, LANES), BF) for r in rows]
+    vmem = lambda *shape: pltpu.VMEM(shape, BF)
+    return pl.pallas_call(
+        functools.partial(late_sum_kernel, counts=counts, sizes=sizes, early_rows=early_rows),
+        in_specs=[pl.BlockSpec(memory_space=pl.ANY)] * (total + 2),
+        out_specs=[pl.BlockSpec(memory_space=pltpu.VMEM)] * 4,
+        out_shape=share + share,
+        scratch_shapes=[
+            *[vmem(16, r, LANES) for r in rows],
+            *[vmem(16, r, LANES) for r in rows],
+            *[vmem(8 >> k, rows[0], LANES) for k in range(4)],
+            *[vmem(8 >> k, rows[1], LANES) for k in range(4)],
+            *[vmem(early_rows + r, LANES) for r in rows],
+            pltpu.SemaphoreType.DMA((2, total + 10)),
+            pltpu.SemaphoreType.DMA((total + 2,)),
+        ],
+        compiler_params=pltpu.CompilerParams(collective_id=collective, has_side_effects=True, vmem_limit_bytes=VMEM_BYTES),
+        name="late_sum",
+    )(*grads[0], *grads[1], *early)
+
+
+def finish_kernel(core_ref, own0, own1, got0, got1, gain_ref, *outs, plan):
+    first = core_ref[0] == 0
+    owns, gots = (own0, own1), (got0, got1)
+    lane = iota((1, LANES), 1)
+    left = lane < 64
+
+    def tile(order, at, size, part):
+        mine = owns[order][at : at + size, :].astype(F32)
+        theirs = gots[order][at : at + size, :].astype(F32)
+        return jnp.where(first == (part == 0), mine, theirs)
+
+    for out, (size, tiles) in zip(outs, plan):
+        count = len(tiles)
+        for part in range(2):
+            rows = slice(part * size, (part + 1) * size)
+            values = [tile(order, at, size, part) for order, at in tiles]
+            if count % 2 == 0:
+                for t in range(count // 2):
+                    out[rows, t * LANES : (t + 1) * LANES] = jnp.where(first, values[t], values[t + count // 2])
+                continue
+            turned = [pltpu.roll(v, 64, 1) for v in values[count // 2 :]]
+            for t in range(count // 2):
+                shifted = jnp.where(left, turned[t], turned[t + 1])
+                out[rows, t * LANES : (t + 1) * LANES] = jnp.where(first, values[t], shifted)
+            out[rows, count // 2 * LANES :] = jnp.where(first, values[count // 2], turned[-1])[:, :64]
+    order, at, size = 0, own0.shape[0] - gain_ref.shape[0] // 2, gain_ref.shape[0] // 2
+    for part in range(2):
+        value = tile(order, at, size, part)
+        gain_ref[part * size : (part + 1) * size, :] = jnp.where(first, value, pltpu.roll(value, LANES - 1, 1))[:, :1]
+
+
+def finish(core, shares, shapes, plan, gain_rows):
+    vmem = pl.BlockSpec(memory_space=pltpu.VMEM)
+    return pl.pallas_call(
+        functools.partial(finish_kernel, plan=plan),
+        in_specs=[pl.BlockSpec(memory_space=pltpu.SMEM)] + [vmem] * 4,
+        out_specs=[vmem] * (1 + len(shapes)),
+        out_shape=[sds((gain_rows, 1), F32)] + [sds(shape, F32) for shape in shapes],
+        compiler_params=params(),
+        name="finish",
+    )(core, *shares)
 
 
 def from_ahead(array, count, distance):
@@ -869,29 +1279,41 @@
             pieces.append(piece if k == 0 else from_ahead(piece, count, -2 * k))
         return pieces
 
+    tiled = count == 8
+    after = lambda array, *others: lax.optimization_barrier((array, *others))[0]
+
     normed_three, q_own, slot_kv = query_in_call(query_rows, gains, w_qqkv)
     q_all = gather(q_own)
-    x, normed_one, qkv, cross = patch_in(src, patch_own, patch_other, gains, w_vqkv, w_xkv)
+    x, normed_one, qkv, cross = patch_in(src, after(patch_own, q_own), patch_other, gains, w_vqkv, w_xkv)
     att, win_stats = window_forward(qkv, window)
-    q_out, q_stats = query_forward(q_all, cross, slot_kv, key_bias, near_ids[:, None], own_ids[None, :], blocks)
-    out_parts, stat_parts = give_back(q_out), give_back(q_stats)
+    q_out = query_forward(after(q_all, att), cross, slot_kv, key_bias, near_ids[:, None], own_ids[None, :], blocks)
+    out_parts = give_back(q_out)
     (vis_own, vis_other, grad_after, grad_att, g_vout, g_up, g_down, gain_two) = patch_ffn(
-        src, inv, att, x, cot_own, cot_other, gains, w_vout, w_up, w_down
+        src, inv, after(att, q_out), x, cot_own, cot_other, gains, w_vout, w_up, w_down, tiled
     )
-    (q_res, grad_q, send_q, send_stats, att_q, normed_four, act_q, dact_q, branch_q, gain_four) = query_ffn(
-        out_parts, stat_parts, query_rows, query_cots, gains, w_qout, w_qup, w_qdown
+    out_parts[0] = after(out_parts[0], grad_att)
+    (q_res, grad_q, send_q, att_q, normed_four, act_q, dact_q, branch_q, gain_four) = query_ffn(
+        out_parts, query_rows, query_cots, gains, w_qout, w_qup, w_qdown
     )
-    go_all, stats_all = gather(send_q), gather(send_stats)
-    g_qup, g_qdown, g_qout = query_weights(normed_four, query_cots, att_q, branch_q, act_q, dact_q)
+    go_all = gather(send_q)
+    g_qout, g_qup, g_qdown = query_weights(normed_four, query_cots, att_q, branch_q, act_q, dact_q, tiled)
+    if tiled:
+        out_0, keep_0, out_1, keep_1 = core_sum([[g_up, g_qup, g_vout], [g_down, g_qdown, g_qout]], 0)
+        early = halved_sum([(out_0, keep_0), (out_1, keep_1)])
+        grad_att = after(grad_att, out_0)
     g_proj = window_backward(qkv, grad_att, win_stats, window)
+    back_part, g_vqkv = qkv_back(g_proj, normed_one, w_vqkv, tiled)
     dq, dk, dv, dsk, dsv = query_backward(
-        q_all, go_all, stats_all, cross, slot_kv, key_bias, near_ids[None, :], own_ids[:, None], blocks
+        q_all, after(go_all, back_part), cross, slot_kv, key_bias, near_ids[None, :], own_ids[:, None], blocks
     )
     dq_parts = give_back(dq)
-    vin_own, vin_other, g_vqkv, g_xkv, gain_one = patch_back(
-        inv, g_proj, dk, dv, normed_one, x, grad_after, gains, w_vqkv, w_xkv
+    vin_own, vin_other, gain_rows, *g_xkv = cross_back(
+        inv, dk, dv, normed_one, x, grad_after, back_part, gains, w_xkv, gain_two, gain_four, tiled
     )
-    qin_grad, g_qqkv, gain_three = query_out(dq_parts, dsk, dsv, normed_three, query_rows, grad_q, gains, w_qqkv)
+    dq_parts[0] = after(dq_parts[0], vin_own)
+    qin_grad, g_qqkv, gain_grads = query_out(
+        dq_parts, dsk, dsv, normed_three, query_rows, grad_q, gains, w_qqkv, gain_rows, tiled
+    )
 
     shape = (pages, strip_rows, columns, width)
     visual_out = put(vis_own, from_ahead(vis_other, count, -1)).reshape(shape)
@@ -906,14 +1328,31 @@
     query_out_rows = return_slots(q_res, BF)
     query_in_grad = return_slots(qin_grad, F32)
 
-    gain_rows = jnp.stack([gain_one[0], gain_two[0], gain_three[0], gain_four[0]])
-    gain_rows = lax.psum_scatter(gain_rows, "page", scatter_dimension=0, tiled=True)
-    gain_part = lax.psum_scatter(gain_rows, "strip", scatter_dimension=1, tiled=True).reshape(-1, 1)
-    return (
-        visual_out, query_out_rows, visual_in_grad, query_in_grad, gain_part,
-        scattered(g_vqkv), scattered(g_vout), scattered(g_up), scattered(g_down), scattered(g_qqkv),
-        scattered(g_xkv), scattered(g_qout), scattered(g_qup), scattered(g_qdown),
-    )
+    weights = (w_vqkv, w_vout, w_up, w_down, w_qqkv, w_xkv, w_qout, w_qup, w_qdown)
+    if tiled:
+        sets = [[g_up, g_qup, g_vout, g_vqkv, g_xkv[0], gain_grads], [g_down, g_qdown, g_qout, g_qqkv, g_xkv[1]]]
+        shares = late_sum([sets[0][3:], sets[1][3:]], early, 1)
+        starts = [[sum(g.shape[-2] for g in group[:k]) for k in range(len(group))] for group in sets]
+        where = {w: (0, starts[0][k]) for k, w in enumerate((2, 7, 1, 0, 5))}
+        where.update({w: (1, starts[1][k]) for k, w in enumerate((3, 8, 6, 4))})
+        plan, shapes = [], []
+        for number, weight in enumerate(weights):
+            rows, cols = weight.shape
+            size, tiles = rows // 16, cols // 256
+            order, at = where[number]
+            spots = [(order, at + t * size) for t in range(tiles)]
+            if number == 5:
+                spots = spots[:3] + [(1, starts[1][4] + t * size) for t in range(3)]
+            plan.append((size, spots))
+            shapes.append((rows // 8, cols // lax.axis_size("page")))
+        core = (lax.axis_index("page") % 2).astype(jnp.int32).reshape(1)
+        gain_part, *parts = finish(core, shares, shapes, plan, width // 8)
+    else:
+        grads = (g_vqkv, g_vout, g_up, g_down, g_qqkv, g_xkv[0], g_qout, g_qup, g_qdown)
+        parts = [scattered(g) for g in grads]
+        gain_part = lax.psum_scatter(gain_grads[:4], "page", scatter_dimension=0, tiled=True)
+        gain_part = lax.psum_scatter(gain_part, "strip", scatter_dimension=1, tiled=True).reshape(-1, 1)
+    return (visual_out, query_out_rows, visual_in_grad, query_in_grad, gain_part, *parts)
 
 
 def solution(mesh):

time: 1400 us -> 658 us (0.47)
  waiting for transfers between devices: 923 us -> 118 us
  Pallas kernels: 302 us -> 414 us
  local copies, waits for them, and re-layouts: 46.3 us -> 21.4 us
    reduce_scatter x18 -> x0, waiting for transfers between devices: 761 us -> none  [the longest x9 566 us: scattered(): part = lax.psum_scatter(grad, 'strip', scatter_dimension=0, tiled=True)]
    pallas_call x4 -> x8, Pallas kernels: 118 us -> 231 us  [the longest x1 81.3 us: late_sum(): pl.pallas_call(functools.partial(late_sum_kernel, counts=counts, sizes=si...]
    unnamed x20 -> x0, waiting for transfers between devices: 62.6 us -> none
    ppermute x23 -> x17, waiting for transfers between devices: 99.3 us -> 37.1 us  [from_ahead(): lax.ppermute(array, 'strip', [(i, (i - distance) % count) for i in range(...]
    ppermute x0 -> x8, waiting for transfers between devices: none -> 43.5 us  [halved_sum(): lax.ppermute(out, axis, [(i, i ^ weight) for i in range(lax.axis_size(axi...]
    ppermute x5, waiting for transfers between devices: 0.01 us -> 37.2 us  [from_partner(): return lax.ppermute(array, 'strip', [(i, i ^ 1) for i in range(count)])]
    ppermute x23 -> x17, starting transfers between devices: 51.9 us -> 31.4 us  [from_ahead(): lax.ppermute(array, 'strip', [(i, (i - distance) % count) for i in range(...]
    ppermute x5, starting transfers between devices: 8.28 us -> 25.2 us  [from_partner(): return lax.ppermute(array, 'strip', [(i, i ^ 1) for i in range(count)])]
  transfers between devices with their start and end apart: 47 -> 30, of which waited for: 23 -> 11; matrix products, arithmetic and copies ran while one was open for 5% -> 6% of each run, Pallas kernels for 22% -> 43%
where the time goes in v2:
time: 658 us; the launch traced here: 653 us
  Pallas kernels  414 us (63%)
  waiting for transfers between devices  118 us (18%)
  starting transfers between devices  72.6 us (11%)
  other arithmetic  24.9 us (4%)
  local copies, waits for them, and re-layouts  21.4 us (3%)
    pallas_call x1, Pallas kernels, late_sum(): pl.pallas_call(functools.partial(late_sum_kernel, counts=counts, sizes=si...  81.3 us
    pallas_call x1, Pallas kernels, patch_ffn(): pl.pallas_call(functools.partial(patch_ffn_kernel, tiled=tiled), grid=(hi...  69.5 us
    pallas_call x1, Pallas kernels, query_backward(): pl.pallas_call(functools.partial(query_back_kernel, blocks=blocks), grid=...  58.5 us
    ppermute x8, waiting for transfers between devices, halved_sum(): lax.ppermute(out, axis, [(i, i ^ weight) for i in range(lax.axis_size(axi...  43.5 us
    pallas_call x1, Pallas kernels, window_backward(): pl.pallas_call(window_back_kernel, grid=(total // tokens,), in_specs=[row...  39.4 us
    ppermute x5, waiting for transfers between devices, from_partner(): return lax.ppermute(array, 'strip', [(i, i ^ 1) for i in range(count)])  37.2 us
    ppermute x17, waiting for transfers between devices, from_ahead(): lax.ppermute(array, 'strip', [(i, (i - distance) % count) for i in range(...  37.1 us
    pallas_call x1, Pallas kernels, query_forward(): pl.pallas_call(functools.partial(query_forward_kernel, blocks=blocks), gr...  35 us
  transfers between devices with their start and end apart: 30, of which 11 were waited for; matrix products, arithmetic and copies ran while one was open for 6% of the time, Pallas kernels for 43%

profile of v2, /device:TPU:0, one launch (start us, length us, event | category | flops | bytes accessed | tf_op | source)
XLA Modules:
  0.0 653.4 jit_solution(361218328729941054)
XLA Ops:
  2.0 1.1 dynamic-slice_bitcast_fusion.3
  3.1 3.0 collective-permute-start
  6.1 3.4 constant_dynamic-slice_fusion
  9.6 3.5 collective-permute-start.1
  13.1 1.6 collective-permute-start.5
  15.3 1.4 collective-permute-start.7
  17.3 1.9 fusion.7.src_ref
  19.2 1.9 fusion.15.inv_ref
  23.3 10.0 %collective-permute-done.5 = s32[6]{0:T(128)S(1)} collective-permute-done((s32[6]{0:T(128)S(1)}, s32[6]{0:T(128)S(1)}, u32[]{:S(2)}, u32[]{:S(2)}) %collective-permute-start.5) | collective-permute-done | bytes 56 | tf_op jit(solution)/shard_map/ppermute | solution.py:1198
  34.5 4.3 query_in.1
  38.8 2.0 collective-permute-start.2
  41.9 4.2 collective-permute-start.3
  46.7 7.3 %collective-permute-done.12 = bf16[128,768]{1,0:T(8,128)(2,1)} collective-permute-done((bf16[128,768]{1,0:T(8,128)(2,1)S(1)}, bf16[128,768]{1,0:T(8,128)(2,1)}, u32[]{:S(2)}, u32[]{:S(2)}) %collective-permute-start.12) | collective-permute-done | bytes 196640 | tf_op jit(solution)/shard_map/ppermute | solution.py:1202
  54.0 2.6 collective-permute-start.4
  56.6 1.9 maximum_select_fusion.1.refs_5_.cot_ref
  58.4 3.1 collective-permute-done.2
  61.7 7.6 %collective-permute-done.3 = bf16[256,768]{1,0:T(8,128)(2,1)S(1)} collective-permute-done((bf16[256,768]{1,0:T(8,128)(2,1)}, bf16[256,768]{1,0:T(8,128)(2,1)S(1)}, u32[]{:S(2)}, u32[]{:S(2)}) %collective-permute-start.3) | collective-permute-done | bytes 393248 | tf_op jit(solution)/shard_map/ppermute | solution.py:1198
  69.3 15.1 %collective-permute-done.4 = bf16[256,768]{1,0:T(8,128)(2,1)S(1)} collective-permute-done((bf16[256,768]{1,0:T(8,128)(2,1)}, bf16[256,768]{1,0:T(8,128)(2,1)S(1)}, u32[]{:S(2)}, u32[]{:S(2)}) %collective-permute-start.4) | collective-permute-done | bytes 393248 | tf_op jit(solution)/shard_map/ppermute | solution.py:1198
  84.4 1.2 copy-done.10
  85.6 15.8 %patch_in.1 = (bf16[1152,768]{1,0:T(8,128)(2,1)}, bf16[1152,768]{1,0:T(8,128)(2,1)}, bf16[1152,2304]{1,0:T(8,128)(2,1)}, bf16[1152,1536]{1,0:T(8,128)(2,1)}) custom-call(s32[576,1]{1,0:T(8,128)} %fusion.7.src_ref, bf16[576,768]{1,0:T(8,128)(2,1)} %bitcast.72, bf16[576,768]{1,0:T(8,128)(2,1)} %collective-permute-done.1.other_ref, ...), custom_call_target="tpu_custom_call" | custom-call | flops 6794772480 | bytes 20000000 | tf_op jit(solution)/shard_map/patch_in/pallas_call | solution.py:186
  101.3 14.7 %window_forward.1 = (bf16[1152,768]{1,0:T(8,128)(2,1)}, bf16[1152,128]{1,0:T(8,128)(2,1)}) custom-call(bf16[1152,2304]{1,0:T(8,128)(2,1)} %get-tuple-element.85.qkv_ref), custom_call_target="tpu_custom_call" | custom-call | flops 2038431744 | bytes 8000000 | tf_op jit(solution)/shard_map/window_forward/pallas_call | solution.py:237
  116.0 0.9 broadcast_in_dim.36.kb_ref
  116.9 35.0 %query_forward.1 = bf16[1024,896]{1,0:T(8,128)(2,1)} custom-call(bf16[1024,768]{1,0:T(8,128)(2,1)} %copy-done.10, bf16[1152,1536]{1,0:T(8,128)(2,1)} %get-tuple-element.88.k_ref.v_ref, bf16[1152,1536]{1,0:T(8,128)(2,1)} %get-tuple-element.88.k_ref.v_ref, bf16[256,1536]{1,0:T(8,128)(2,1)} %get-tuple-element.89.sk_ref.sv_ref, ...), custom_call_target="tpu_custom_call" | custom-call | flops 14495514624 | bytes 10000000 | tf_op jit(solution)/shard_map/query_forward/pallas_call | solution.py:644
  152.0 2.4 fusion.39
  154.4 4.3 collective-permute-start.9
  159.3 69.5 %patch_ffn.1 = (bf16[576,768]{1,0:T(8,128)(2,1)}, bf16[576,768]{1,0:T(8,128)(2,1)}, f32[1152,768]{1,0:T(8,128)}, bf16[1152,768]{1,0:T(8,128)(2,1)}, bf16[2,2,2,4...) custom-call(s32[576,1]{1,0:T(8,128)} %fusion.7.src_ref, ...), custom_call_target="tpu_custom_call" | custom-call | flops 32614907904 | bytes 40000000 | tf_op jit(solution)/shard_map/patch_ffn/pallas_call | solution.py:402
  229.9 15.9 %query_ffn.1 = (bf16[256,768]{1,0:T(8,128)(2,1)}, f32[256,768]{1,0:T(8,128)}, bf16[256,896]{1,0:T(8,128)(2,1)}, bf16[256,768]{1,0:T(8,128)(2,1)}, bf16[256,768]{...) custom-call(bf16[256,896]{1,0:T(8,128)(2,1)} %copy-done.16, ...), custom_call_target="tpu_custom_call" | custom-call | flops 4831838208 | bytes 20000000 | tf_op jit(solution)/shard_map/query_ffn/pallas_call | solution.py:817
  245.8 11.0 %query_weights.1 = (bf16[2,2,2,4,144,128]{5,4,3,2,1,0:T(8,128)(2,1)}, bf16[2,2,2,4,576,128]{5,4,3,2,1,0:T(8,128)(2,1)}, bf16[2,2,2,4,576,128]{5,4,3,2,1,0:T(8,128)(2,1)}) custom-call(bf16[256,768]{1,0:T(8,128)(2,1)} %get-tuple-element.99.normed_ref, bf16[256,768]{1,0:T(8,128)(2,1)} %maximum_select_fusion.1.refs_5_.cot_ref, ...), custom_call_target="tpu_custom_call" | custom-call | flops 2415919104 | bytes 16000000 | tf_op jit(solution)/shard_map/query_weights/pallas_call | solution.py:867
  256.8 21.0 %core_sum.1 = (bf16[8,1296,128]{2,1,0:T(8,128)(2,1)}, bf16[8,1296,128]{2,1,0:T(8,128)(2,1)}, bf16[8,1296,128]{2,1,0:T(8,128)(2,1)}, bf16[8,1296,128]{2,1,0:T(8,128)(2,1)}) custom-call(bf16[2,16,576,128]{3,2,1,0:T(8,128)(2,1)} %bitcast.58, bf16[2,16,576,128]{3,2,1,0:T(8,128)(2,1)} %bitcast.60, bf16[2,16,144,128]{3,2,1,0:T(8,128)(2,1)} %bitcast.68, ...), custom_call_target="tpu_custom_call" | custom-call | tf_op jit(solution)/shard_map/core_sum/pallas_call | solution.py:1026
  277.9 3.9 collective-permute-start.14
  281.8 1.5 collective-permute-start.16
  283.3 2.0 collective-permute-start.13
  285.3 39.4 %window_backward.1.gp_ref = bf16[1152,2304]{1,0:T(8,128)(2,1)} custom-call(bf16[1152,2304]{1,0:T(8,128)(2,1)} %get-tuple-element.85.qkv_ref, bf16[1152,768]{1,0:T(8,128)(2,1)} %get-tuple-element.110.go_ref, bf16[1152,128]{1,0:T(8,128)(2,1)} %get-tuple-element.111.stat_ref), custom_call_target="tpu_custom_call" | custom-call | flops 5096079360 | bytes 13000000 | tf_op jit(solution)/shard_map/window_backward/pallas_call | solution.py:290
  324.7 16.1 %qkv_back.1 = (f32[1152,768]{1,0:T(8,128)}, bf16[2,2,2,4,432,128]{5,4,3,2,1,0:T(8,128)(2,1)}) custom-call(bf16[1152,2304]{1,0:T(8,128)(2,1)} %window_backward.1.gp_ref, bf16[1152,768]{1,0:T(8,128)(2,1)} %get-tuple-element.112.n_ref, bf16[768,2304]{1,0:T(8,128)(2,1)} %w_ref.3), custom_call_target="tpu_custom_call" | custom-call | flops 8153726976 | bytes 20000000 | tf_op jit(solution)/shard_map/qkv_back/pallas_call | solution.py:456
  340.8 1.1 collective-permute-done.13
  341.9 1.5 collective-permute-start.26
  344.2 1.4 pad_maximum_fusion.1.go_ref.stat_ref
  345.7 58.5 %query_backward.1 = (bf16[1024,768]{1,0:T(8,128)(2,1)}, bf16[1152,768]{1,0:T(8,128)(2,1)}, bf16[1152,768]{1,0:T(8,128)(2,1)}, bf16[256,768]{1,0:T(8,128)(2,1)}, bf16[256,768]{1,0:T(8,128)(2,1)}) custom-call(bf16[1024,768]{1,0:T(8,128)(2,1)} %copy-done.10, bf16[1024,896]{1,0:T(8,128)(2,1)} %pad_maximum_fusion.1.go_ref.stat_ref, ...), custom_call_target="tpu_custom_call" | custom-call | flops 36238786560 | bytes 15000000 | tf_op jit(solution)/shard_map/query_backward/pallas_call | solution.py:727
  404.1 2.4 fusion.40
  406.5 3.3 collective-permute-start.18
  410.4 1.5 collective-permute-start.20
  411.8 20.7 %cross_back.1 = (f32[576,768]{1,0:T(8,128)}, bf16[576,768]{1,0:T(8,128)(2,1)}, f32[8,768]{1,0:T(8,128)}, bf16[2,2,2,4,144,128]{5,4,3,2,1,0:T(8,128)(2,1)}, bf16[2,2,2,4,144,128]{5,4,3,2,1,0:T(8,128)(2,1)}) custom-call(s32[576,1]{1,0:T(8,128)} %fusion.15.inv_ref, bf16[1152,768]{1,0:T(8,128)(2,1)} %get-tuple-element.115.gk_ref, ...), custom_call_target="tpu_custom_call" | custom-call | flops 5435817984 | bytes 20000000 | tf_op jit(solution)/shard_map/cross_back/pallas_call | solution.py:538
  433.3 3.1 dynamic-slice_add_fusion.1
  436.4 7.5 %collective-permute-start.27 = (bf16[4,1296,128]{2,1,0:T(8,128)(2,1)}, bf16[4,1296,128]{2,1,0:T(8,128)(2,1)}, u32[]{:S(2)}, u32[]{:S(2)}) collective-permute-start(bf16[4,1296,128]{2,1,0:T(8,128)(2,1)} %get-tuple-element.195), channel_id=1, source_target_pairs={{0,1},{1,0},{2,3},{3,2},{4,5},{5,4},{6,7},{7,6},{8,9},{9,8},{10,11... | collective-permute-start | bytes 3981320 | tf_op jit(solution)/shard_map/ppermute | solution.py:1050
  443.9 1.3 collective-permute-done.20.refs_3_
  445.2 7.9 %query_out.1 = (f32[256,768]{1,0:T(8,128)}, bf16[2,2,2,4,432,128]{5,4,3,2,1,0:T(8,128)(2,1)}, bf16[2,2,2,4,48,128]{5,4,3,2,1,0:T(8,128)(2,1)}) custom-call(bf16[256,768]{1,0:T(8,128)(2,1)} %copy-done.7, bf16[256,768]{1,0:T(8,128)(2,1)} %get-tuple-element.216.refs_1_, bf16[256,768]{1,0:T(8,128)(2,1)} %collective-permute-done.19.refs_2_, ...), custom_call_target="tpu_custom_call" | custom-call | flops 1811939328 | bytes 10000000 | tf_op jit(solution)/shard_map/query_out/pallas_call | solution.py:916
  453.2 2.1 dynamic-slice_add_fusion.3
  455.9 19.6 %collective-permute-start.21 = (bf16[128,768]{1,0:T(8,128)(2,1)S(1)}, bf16[128,768]{1,0:T(8,128)(2,1)S(1)}, u32[]{:S(2)}, u32[]{:S(2)}) collective-permute-start(bf16[128,768]{1,0:T(8,128)(2,1)S(1)} %select_convert_fusion), channel_id=1, source_target_pairs={{0,1},{1,0},{2,3},{3,2},{4,5},{5,4},{6,7},{7,6},{8,9},{9,8},{10,11... | collective-permute-start | bytes 589832 | tf_op jit(solution)/shard_map/ppermute | solution.py:1202
  475.5 1.3 broadcast_select_fusion.1
  476.8 1.4 pad_maximum_fusion.2
  478.4 28.8 %collective-permute-done.21 = bf16[128,768]{1,0:T(8,128)(2,1)S(1)} collective-permute-done((bf16[128,768]{1,0:T(8,128)(2,1)S(1)}, bf16[128,768]{1,0:T(8,128)(2,1)S(1)}, u32[]{:S(2)}, u32[]{:S(2)}) %collective-permute-start.21) | collective-permute-done | bytes 196640 | tf_op jit(solution)/shard_map/ppermute | solution.py:1202
  507.3 1.4 dynamic-slice_add_fusion.5
  509.1 0.9 pad_maximum_fusion.3
  510.2 1.8 collective-permute-start.24
  512.3 14.3 %collective-permute-done.28 = bf16[2,1296,128]{2,1,0:T(8,128)(2,1)S(1)} collective-permute-done((bf16[2,1296,128]{2,1,0:T(8,128)(2,1)S(1)}, bf16[2,1296,128]{2,1,0:T(8,128)(2,1)S(1)}, u32[]{:S(2)}, u32[]{:S(2)}) %collective-permute-start.28) | collective-permute-done | bytes 663584 | tf_op jit(solution)/shard_map/ppermute | solution.py:1050
  526.6 4.1 collective-permute-start.29
  530.7 2.0 pad_maximum_fusion
  532.7 14.2 %collective-permute-done.24 = bf16[2,1296,128]{2,1,0:T(8,128)(2,1)S(1)} collective-permute-done((bf16[2,1296,128]{2,1,0:T(8,128)(2,1)S(1)}, bf16[2,1296,128]{2,1,0:T(8,128)(2,1)S(1)}, u32[]{:S(2)}, u32[]{:S(2)}) %collective-permute-start.24) | collective-permute-done | bytes 663584 | tf_op jit(solution)/shard_map/ppermute | solution.py:1050
  547.9 15.0 %collective-permute-done.25 = bf16[1,1296,128]{2,1,0:T(8,128)(2,1)S(1)} collective-permute-done((bf16[1,1296,128]{2,1,0:T(8,128)(2,1)S(1)}, bf16[1,1296,128]{2,1,0:T(8,128)(2,1)S(1)}, u32[]{:S(2)}, u32[]{:S(2)}) %collective-permute-start.25) | collective-permute-done | bytes 331808 | tf_op jit(solution)/shard_map/ppermute | solution.py:1050
  563.7 81.3 %late_sum.1 = (bf16[1920,128]{1,0:T(8,128)(2,1)}, bf16[1872,128]{1,0:T(8,128)(2,1)}, bf16[1920,128]{1,0:T(8,128)(2,1)}, bf16[1872,128]{1,0:T(8,128)(2,1)}) custom-call(bf16[2,16,432,128]{3,2,1,0:T(8,128)(2,1)} %bitcast.62, bf16[2,16,144,128]{3,2,1,0:T(8,128)(2,1)} %bitcast.66, bf16[2,16,48,128]{3,2,1,0:T(8,128)(2,1)} %bitcast.74, ...), custom_call_target="tpu_custom_call" | custom-call | tf_op jit(solution)/shard_map/late_sum/pallas_call | solution.py:1135
  645.0 3.1 finish.1
  648.1 1.9 copy.54
  650.0 1.9 copy.55
  651.8 1.4 copy.53
  (106 shorter events, 13.7 us)
Async XLA Ops:
  3.0 10.1 %copy-start.13 = (s32[2,6]{1,0:T(2,128)S(1)}, s32[2,6]{1,0:T(2,128)}, u32[]{:S(2)}) copy-start(s32[2,6]{1,0:T(2,128)} %param.21) | copy-start | bytes 148
  3.0 11.7 %copy-start.14 = (s32[2,128]{1,0:T(2,128)S(1)}, s32[2,128]{1,0:T(2,128)}, u32[]{:S(2)}) copy-start(s32[2,128]{1,0:T(2,128)} %param.23) | copy-start | bytes 3076
  3.0 13.6 %copy-start.19 = (s32[2]{0:T(128)S(1)}, s32[2]{0:T(128)}, u32[]{:S(2)}) copy-start(s32[2]{0:T(128)} %param.24) | copy-start | bytes 28
  3.1 18.1 %copy-start.12 = (s32[2,1024]{1,0:T(2,128)S(1)}, s32[2,1024]{1,0:T(2,128)}, u32[]{:S(2)}) copy-start(s32[2,1024]{1,0:T(2,128)} %param.22) | copy-start | bytes 24580
  3.1 19.5 %copy-start.8 = (bf16[2,128,768]{2,1,0:T(8,128)(2,1)S(1)}, bf16[2,128,768]{2,1,0:T(8,128)(2,1)}, u32[]{:S(2)}) copy-start(bf16[2,128,768]{2,1,0:T(8,128)(2,1)} %param.37) | copy-start | bytes 1179652
  3.1 19.6 %copy-start.11 = (f32[768,4]{0,1:T(4,128)S(1)}, f32[768,4]{0,1:T(4,128)}, u32[]{:S(2)}) copy-start(f32[768,4]{0,1:T(4,128)} %param.26) | copy-start | bytes 36868
  3.1 30.5 %collective-permute-start = (bf16[128,768]{1,0:T(8,128)(2,1)S(1)}, bf16[128,768]{1,0:T(8,128)(2,1)S(1)}, u32[]{:S(2)}, u32[]{:S(2)}) collective-permute-start(bf16[128,768]{1,0:T(8,128)(2,1)S(1)} %get-tuple-element.224), channel_id=1, source_target_pairs={{0,1},{1,0},{2,3},{3,2},{4,5},{5,4},{6,7},{7,6},{8,9},{9,8},{10,11... | collective-permute-start | bytes 589832 | tf_op jit(solution)/shard_map/ppermute | solution.py:1202
  9.6 76.0 %collective-permute-start.1 = (bf16[576,768]{1,0:T(8,128)(2,1)S(1)}, bf16[576,768]{1,0:T(8,128)(2,1)}, u32[]{:S(2)}, u32[]{:S(2)}) collective-permute-start(bf16[576,768]{1,0:T(8,128)(2,1)S(1)} %bitcast.73), channel_id=1, source_target_pairs={{0,7},{1,0},{2,1},{3,2},{4,3},{5,4},{6,5},{7,6},{8,15},{9,8},{10,9... | collective-permute-start | bytes 2654216 | tf_op jit(solution)/shard_map/ppermute | solution.py:1198
  13.1 20.1 %collective-permute-start.5 = (s32[6]{0:T(128)S(1)}, s32[6]{0:T(128)S(1)}, u32[]{:S(2)}, u32[]{:S(2)}) collective-permute-start(s32[6]{0:T(128)S(1)} %get-tuple-element.233), channel_id=1, source_target_pairs={{0,7},{1,0},{2,1},{3,2},{4,3},{5,4},{6,5},{7,6},{8,15},{9,8},{10,9... | collective-permute-start | bytes 80 | tf_op jit(solution)/shard_map/ppermute | solution.py:1198
  14.7 18.9 %collective-permute-start.6 = (s32[128]{0:T(128)S(1)}, s32[128]{0:T(128)S(1)}, u32[]{:S(2)}, u32[]{:S(2)}) collective-permute-start(s32[128]{0:T(128)S(1)} %get-tuple-element.230), channel_id=1, source_target_pairs={{0,1},{1,0},{2,3},{3,2},{4,5},{5,4},{6,7},{7,6},{8,9},{9,8},{10,11... | collective-permute-start | bytes 1544 | tf_op jit(solution)/shard_map/ppermute | solution.py:1202
  15.3 144.0 %collective-permute-start.7 = (bf16[576,768]{1,0:T(8,128)(2,1)S(1)}, bf16[576,768]{1,0:T(8,128)(2,1)}, u32[]{:S(2)}, u32[]{:S(2)}) collective-permute-start(bf16[576,768]{1,0:T(8,128)(2,1)S(1)} %bitcast.71), channel_id=1, source_target_pairs={{0,7},{1,0},{2,1},{3,2},{4,3},{5,4},{6,5},{7,6},{8,15},{9,8},{10,9... | collective-permute-start | bytes 2654216 | tf_op jit(solution)/shard_map/ppermute | solution.py:1198
  33.2 20.7 %collective-permute-start.12 = (bf16[128,768]{1,0:T(8,128)(2,1)S(1)}, bf16[128,768]{1,0:T(8,128)(2,1)}, u32[]{:S(2)}, u32[]{:S(2)}) collective-permute-start(bf16[128,768]{1,0:T(8,128)(2,1)S(1)} %get-tuple-element.222), channel_id=1, source_target_pairs={{0,1},{1,0},{2,3},{3,2},{4,5},{5,4},{6,7},{7,6},{8,9},{9,8},{10,11... | collective-permute-start | bytes 589832 | tf_op jit(solution)/shard_map/ppermute | solution.py:1202
  38.8 22.8 %copy-start.9 = (bf16[256,768]{1,0:T(8,128)(2,1)S(1)}, bf16[256,768]{1,0:T(8,128)(2,1)}, u32[]{:S(2)}) copy-start(bf16[256,768]{1,0:T(8,128)(2,1)} %get-tuple-element.83) | copy-start | bytes 1179652
  38.8 22.8 %collective-permute-start.2 = (bf16[256,768]{1,0:T(8,128)(2,1)}, bf16[256,768]{1,0:T(8,128)(2,1)S(1)}, u32[]{:S(2)}, u32[]{:S(2)}) collective-permute-start(bf16[256,768]{1,0:T(8,128)(2,1)} %get-tuple-element.83), channel_id=1, source_target_pairs={{0,2},{1,3},{2,4},{3,5},{4,6},{5,7},{6,0},{7,1},{8,10},{9,11},{10,... | collective-permute-start | bytes 1179656 | tf_op jit(solution)/shard_map/ppermute | solution.py:1198
  41.9 27.4 %collective-permute-start.3 = (bf16[256,768]{1,0:T(8,128)(2,1)}, bf16[256,768]{1,0:T(8,128)(2,1)S(1)}, u32[]{:S(2)}, u32[]{:S(2)}) collective-permute-start(bf16[256,768]{1,0:T(8,128)(2,1)} %get-tuple-element.83), channel_id=1, source_target_pairs={{0,6},{1,7},{2,0},{3,1},{4,2},{5,3},{6,4},{7,5},{8,14},{9,15},{10,... | collective-permute-start | bytes 1179656 | tf_op jit(solution)/shard_map/ppermute | solution.py:1198
  54.0 30.4 %collective-permute-start.4 = (bf16[256,768]{1,0:T(8,128)(2,1)}, bf16[256,768]{1,0:T(8,128)(2,1)S(1)}, u32[]{:S(2)}, u32[]{:S(2)}) collective-permute-start(bf16[256,768]{1,0:T(8,128)(2,1)} %get-tuple-element.83), channel_id=1, source_target_pairs={{0,4},{1,5},{2,6},{3,7},{4,0},{5,1},{6,2},{7,3},{8,12},{9,13},{10,... | collective-permute-start | bytes 1179656 | tf_op jit(solution)/shard_map/ppermute | solution.py:1198
  84.4 1.2 copy-start.10
  154.4 74.4 %collective-permute-start.9 = (bf16[256,896]{1,0:T(8,128)(2,1)S(1)}, bf16[256,896]{1,0:T(8,128)(2,1)S(1)}, u32[]{:S(2)}, u32[]{:S(2)}) collective-permute-start(bf16[256,896]{1,0:T(8,128)(2,1)S(1)} %get-tuple-element.207), channel_id=1, source_target_pairs={{0,6},{1,7},{2,0},{3,1},{4,2},{5,3},{6,4},{7,5},{8,14},{9,15},{10,... | collective-permute-start | bytes 1376264 | tf_op jit(solution)/shard_map/ppermute | solution.py:1198
  158.7 70.1 %collective-permute-start.10 = (bf16[256,896]{1,0:T(8,128)(2,1)S(1)}, bf16[256,896]{1,0:T(8,128)(2,1)S(1)}, u32[]{:S(2)}, u32[]{:S(2)}) collective-permute-start(bf16[256,896]{1,0:T(8,128)(2,1)S(1)} %get-tuple-element.205), channel_id=1, source_target_pairs={{0,2},{1,3},{2,4},{3,5},{4,6},{5,7},{6,0},{7,1},{8,10},{9,11},{10,... | collective-permute-start | bytes 1376264 | tf_op jit(solution)/shard_map/ppermute | solution.py:1198
  158.7 70.2 %collective-permute-start.11 = (bf16[256,896]{1,0:T(8,128)(2,1)S(1)}, bf16[256,896]{1,0:T(8,128)(2,1)S(1)}, u32[]{:S(2)}, u32[]{:S(2)}) collective-permute-start(bf16[256,896]{1,0:T(8,128)(2,1)S(1)} %get-tuple-element.204), channel_id=1, source_target_pairs={{0,4},{1,5},{2,6},{3,7},{4,0},{5,1},{6,2},{7,3},{8,12},{9,13},{10,... | collective-permute-start | bytes 1376264 | tf_op jit(solution)/shard_map/ppermute | solution.py:1198
  228.8 0.8 copy-start.16
  228.8 0.9 copy-start.17
  228.9 1.0 copy-start.18
  256.8 21.1 %copy-start.6 = (bf16[256,896]{1,0:T(8,128)(2,1)S(1)}, bf16[256,896]{1,0:T(8,128)(2,1)}, u32[]{:S(2)}) copy-start(bf16[256,896]{1,0:T(8,128)(2,1)} %get-tuple-element.97) | copy-start | bytes 1376260
  256.8 26.5 %copy-start.4 = (bf16[256,768]{1,0:T(8,128)(2,1)S(1)}, bf16[256,768]{1,0:T(8,128)(2,1)}, u32[]{:S(2)}) copy-start(bf16[256,768]{1,0:T(8,128)(2,1)} %get-tuple-element.96) | copy-start | bytes 1179652
  277.8 175.3 %collective-permute-start.22 = (bf16[8,1296,128]{2,1,0:T(8,128)(2,1)}, bf16[8,1296,128]{2,1,0:T(8,128)(2,1)}, u32[]{:S(2)}, u32[]{:S(2)}) collective-permute-start(bf16[8,1296,128]{2,1,0:T(8,128)(2,1)} %get-tuple-element.109), channel_id=1, source_target_pairs={{0,1},{1,0},{2,3},{3,2},{4,5},{5,4},{6,7},{7,6},{8,9},{9,8},{10,11... | collective-permute-start | bytes 7962632 | tf_op jit(solution)/shard_map/ppermute | solution.py:1050
  277.9 66.3 %collective-permute-start.14 = (bf16[256,896]{1,0:T(8,128)(2,1)S(1)}, bf16[256,896]{1,0:T(8,128)(2,1)S(1)}, u32[]{:S(2)}, u32[]{:S(2)}) collective-permute-start(bf16[256,896]{1,0:T(8,128)(2,1)S(1)} %copy-done.6), channel_id=1, source_target_pairs={{0,2},{1,3},{2,4},{3,5},{4,6},{5,7},{6,0},{7,1},{8,10},{9,11},{10,... | collective-permute-start | bytes 1376264 | tf_op jit(solution)/shard_map/ppermute | solution.py:1198
  281.8 62.5 %collective-permute-start.15 = (bf16[256,896]{1,0:T(8,128)(2,1)S(1)}, bf16[256,896]{1,0:T(8,128)(2,1)S(1)}, u32[]{:S(2)}, u32[]{:S(2)}) collective-permute-start(bf16[256,896]{1,0:T(8,128)(2,1)S(1)} %copy-done.6), channel_id=1, source_target_pairs={{0,6},{1,7},{2,0},{3,1},{4,2},{5,3},{6,4},{7,5},{8,14},{9,15},{10,... | collective-permute-start | bytes 1376264 | tf_op jit(solution)/shard_map/ppermute | solution.py:1198
  281.8 62.5 %collective-permute-start.16 = (bf16[256,896]{1,0:T(8,128)(2,1)S(1)}, bf16[256,896]{1,0:T(8,128)(2,1)S(1)}, u32[]{:S(2)}, u32[]{:S(2)}) collective-permute-start(bf16[256,896]{1,0:T(8,128)(2,1)S(1)} %copy-done.6), channel_id=1, source_target_pairs={{0,4},{1,5},{2,6},{3,7},{4,0},{5,1},{6,2},{7,3},{8,12},{9,13},{10,... | collective-permute-start | bytes 1376264 | tf_op jit(solution)/shard_map/ppermute | solution.py:1198
  283.3 58.6 %collective-permute-start.13 = (bf16[128,768]{1,0:T(8,128)(2,1)S(1)}, bf16[128,768]{1,0:T(8,128)(2,1)S(1)}, u32[]{:S(2)}, u32[]{:S(2)}) collective-permute-start(bf16[128,768]{1,0:T(8,128)(2,1)S(1)} %broadcast_select_fusion.2), channel_id=1, source_target_pairs={{0,1},{1,0},{2,3},{3,2},{4,5},{5,4},{6,7},{7,6},{8,9},{9,8},{10,11... | collective-permute-start | bytes 589832 | tf_op jit(solution)/shard_map/ppermute | solution.py:1202
  341.9 91.0 %collective-permute-start.26 = (bf16[8,1296,128]{2,1,0:T(8,128)(2,1)}, bf16[8,1296,128]{2,1,0:T(8,128)(2,1)}, u32[]{:S(2)}, u32[]{:S(2)}) collective-permute-start(bf16[8,1296,128]{2,1,0:T(8,128)(2,1)} %get-tuple-element.137), channel_id=1, source_target_pairs={{0,16},{8,24},{16,0},{24,8},{1,17},{9,25},{17,1},{25,9},{2,18},{10... | collective-permute-start | bytes 7962632 | tf_op jit(solution)/shard_map/ppermute | solution.py:1050
  406.5 26.0 %collective-permute-start.18 = (bf16[256,768]{1,0:T(8,128)(2,1)S(1)}, bf16[256,768]{1,0:T(8,128)(2,1)S(1)}, u32[]{:S(2)}, u32[]{:S(2)}) collective-permute-start(bf16[256,768]{1,0:T(8,128)(2,1)S(1)} %get-tuple-element.217), channel_id=1, source_target_pairs={{0,6},{1,7},{2,0},{3,1},{4,2},{5,3},{6,4},{7,5},{8,14},{9,15},{10,... | collective-permute-start | bytes 1179656 | tf_op jit(solution)/shard_map/ppermute | solution.py:1198
  409.8 34.1 %collective-permute-start.19 = (bf16[256,768]{1,0:T(8,128)(2,1)}, bf16[256,768]{1,0:T(8,128)(2,1)}, u32[]{:S(2)}, u32[]{:S(2)}) collective-permute-start(bf16[256,768]{1,0:T(8,128)(2,1)} %get-tuple-element.215), channel_id=1, source_target_pairs={{0,2},{1,3},{2,4},{3,5},{4,6},{5,7},{6,0},{7,1},{8,10},{9,11},{10,... | collective-permute-start | bytes 1179656 | tf_op jit(solution)/shard_map/ppermute | solution.py:1198
  410.4 34.9 %collective-permute-start.20 = (bf16[256,768]{1,0:T(8,128)(2,1)}, bf16[256,768]{1,0:T(8,128)(2,1)}, u32[]{:S(2)}, u32[]{:S(2)}) collective-permute-start(bf16[256,768]{1,0:T(8,128)(2,1)} %get-tuple-element.214), channel_id=1, source_target_pairs={{0,4},{1,5},{2,6},{3,7},{4,0},{5,1},{6,2},{7,3},{8,12},{9,13},{10,... | collective-permute-start | bytes 1179656 | tf_op jit(solution)/shard_map/ppermute | solution.py:1198
  411.8 21.4 %copy-start.1 = (bf16[8,1296,128]{2,1,0:T(8,128)(2,1)S(1)}, bf16[8,1296,128]{2,1,0:T(8,128)(2,1)}, u32[]{:S(2)}) copy-start(bf16[8,1296,128]{2,1,0:T(8,128)(2,1)} %get-tuple-element.136) | copy-start | bytes 7962628
  432.5 0.7 copy-start.7
  432.5 43.0 %collective-permute-start.8 = (bf16[576,768]{1,0:T(8,128)(2,1)}, bf16[576,768]{1,0:T(8,128)(2,1)}, u32[]{:S(2)}, u32[]{:S(2)}) collective-permute-start(bf16[576,768]{1,0:T(8,128)(2,1)} %get-tuple-element.93), channel_id=1, source_target_pairs={{0,1},{1,2},{2,3},{3,4},{4,5},{5,6},{6,7},{7,0},{8,9},{9,10},{10,1... | collective-permute-start | bytes 2654216 | tf_op jit(solution)/shard_map/ppermute | solution.py:1198
  436.4 70.9 %collective-permute-start.27 = (bf16[4,1296,128]{2,1,0:T(8,128)(2,1)}, bf16[4,1296,128]{2,1,0:T(8,128)(2,1)}, u32[]{:S(2)}, u32[]{:S(2)}) collective-permute-start(bf16[4,1296,128]{2,1,0:T(8,128)(2,1)} %get-tuple-element.195), channel_id=1, source_target_pairs={{0,1},{1,0},{2,3},{3,2},{4,5},{5,4},{6,7},{7,6},{8,9},{9,8},{10,11... | collective-permute-start | bytes 3981320 | tf_op jit(solution)/shard_map/ppermute | solution.py:1050
  445.2 7.9 %copy-start = (bf16[8,1296,128]{2,1,0:T(8,128)(2,1)S(1)}, bf16[8,1296,128]{2,1,0:T(8,128)(2,1)}, u32[]{:S(2)}) copy-start(bf16[8,1296,128]{2,1,0:T(8,128)(2,1)} %get-tuple-element.135) | copy-start | bytes 7962628
  453.1 2.7 copy-start.3
  453.2 22.4 %copy-start.5 = (bf16[576,768]{1,0:T(8,128)(2,1)S(1)}, bf16[576,768]{1,0:T(8,128)(2,1)}, u32[]{:S(2)}) copy-start(bf16[576,768]{1,0:T(8,128)(2,1)} %get-tuple-element.92) | copy-start | bytes 2654212
  455.3 54.8 %collective-permute-start.23 = (bf16[4,1296,128]{2,1,0:T(8,128)(2,1)S(1)}, bf16[4,1296,128]{2,1,0:T(8,128)(2,1)S(1)}, u32[]{:S(2)}, u32[]{:S(2)}) collective-permute-start(bf16[4,1296,128]{2,1,0:T(8,128)(2,1)S(1)} %get-tuple-element.197), channel_id=1, source_target_pairs={{0,16},{8,24},{16,0},{24,8},{1,17},{9,25},{17,1},{25,9},{2,18},{10... | collective-permute-start | bytes 3981320 | tf_op jit(solution)/shard_map/ppermute | solution.py:1050
  455.9 51.3 %collective-permute-start.21 = (bf16[128,768]{1,0:T(8,128)(2,1)S(1)}, bf16[128,768]{1,0:T(8,128)(2,1)S(1)}, u32[]{:S(2)}, u32[]{:S(2)}) collective-permute-start(bf16[128,768]{1,0:T(8,128)(2,1)S(1)} %select_convert_fusion), channel_id=1, source_target_pairs={{0,1},{1,0},{2,3},{3,2},{4,5},{5,4},{6,7},{7,6},{8,9},{9,8},{10,11... | collective-permute-start | bytes 589832 | tf_op jit(solution)/shard_map/ppermute | solution.py:1202
  476.8 1.4 copy-start.15
  478.2 33.8 %collective-permute-start.17 = (bf16[576,768]{1,0:T(8,128)(2,1)S(1)}, bf16[576,768]{1,0:T(8,128)(2,1)S(1)}, u32[]{:S(2)}, u32[]{:S(2)}) collective-permute-start(bf16[576,768]{1,0:T(8,128)(2,1)S(1)} %copy-done.15), channel_id=1, source_target_pairs={{0,1},{1,2},{2,3},{3,4},{4,5},{5,6},{6,7},{7,0},{8,9},{9,10},{10,1... | collective-permute-start | bytes 2654216 | tf_op jit(solution)/shard_map/ppermute | solution.py:1198
  508.8 17.8 %collective-permute-start.28 = (bf16[2,1296,128]{2,1,0:T(8,128)(2,1)S(1)}, bf16[2,1296,128]{2,1,0:T(8,128)(2,1)S(1)}, u32[]{:S(2)}, u32[]{:S(2)}) collective-permute-start(bf16[2,1296,128]{2,1,0:T(8,128)(2,1)S(1)} %get-tuple-element.199), channel_id=1, source_target_pairs={{0,2},{1,3},{2,0},{3,1},{4,6},{5,7},{6,4},{7,5},{8,10},{9,11},{10,... | collective-permute-start | bytes 1990664 | tf_op jit(solution)/shard_map/ppermute | solution.py:1050
  510.1 2.0 copy-start.2
  510.2 36.7 %collective-permute-start.24 = (bf16[2,1296,128]{2,1,0:T(8,128)(2,1)S(1)}, bf16[2,1296,128]{2,1,0:T(8,128)(2,1)S(1)}, u32[]{:S(2)}, u32[]{:S(2)}) collective-permute-start(bf16[2,1296,128]{2,1,0:T(8,128)(2,1)S(1)} %get-tuple-element.201), channel_id=1, source_target_pairs={{0,2},{1,3},{2,0},{3,1},{4,6},{5,7},{6,4},{7,5},{8,10},{9,11},{10,... | collective-permute-start | bytes 1990664 | tf_op jit(solution)/shard_map/ppermute | solution.py:1050
  526.6 20.5 %collective-permute-start.29 = (bf16[1,1296,128]{2,1,0:T(8,128)(2,1)S(1)}, bf16[1,1296,128]{2,1,0:T(8,128)(2,1)S(1)}, u32[]{:S(2)}, u32[]{:S(2)}) collective-permute-start(bf16[1,1296,128]{2,1,0:T(8,128)(2,1)S(1)} %dynamic-slice_add_fusion.8), channel_id=1, source_target_pairs={{0,4},{1,5},{2,6},{3,7},{4,0},{5,1},{6,2},{7,3},{8,12},{9,13},{10,... | collective-permute-start | bytes 995336 | tf_op jit(solution)/shard_map/ppermute | solution.py:1050
  547.0 15.9 %collective-permute-start.25 = (bf16[1,1296,128]{2,1,0:T(8,128)(2,1)S(1)}, bf16[1,1296,128]{2,1,0:T(8,128)(2,1)S(1)}, u32[]{:S(2)}, u32[]{:S(2)}) collective-permute-start(bf16[1,1296,128]{2,1,0:T(8,128)(2,1)S(1)} %dynamic-slice_add_fusion.9), channel_id=1, source_target_pairs={{0,4},{1,5},{2,6},{3,7},{4,0},{5,1},{6,2},{7,3},{8,12},{9,13},{10,... | collective-permute-start | bytes 995336 | tf_op jit(solution)/shard_map/ppermute | solution.py:1050
